TPU v7x, 128 devices: a whole 4x4x4 slice. The times are simulated.
128 devices in a mesh: oct: 8 (over x, core), leaf: 16 (over z, y).
Axes of the slice: x: 4, y: 4, z: 4, core: 2. Of those that a mesh axis runs over, the one named last changes fastest.
Arguments:
- density: float32 [65536, 128], P(('oct', 'leaf')), may hold values from -6 to 6
- positions: float32 [65536, 3, 128], P(('oct', 'leaf')), may hold values from -1 to 1
- counts: int32 [65536], P(('oct', 'leaf')), may hold values from 1 to 128, as said below
- leaf_parent: int32 [65536], P(('oct', 'leaf')), may hold values from 0 to 63
- child_pos: int32 [65536], P(('oct', 'leaf')), may hold values from 0 to 7
- send_slots: int32 [128, 128, 32], P(('oct', 'leaf')), may hold values from -1 to 511, as said below
- far_source: int32 [65536, 27], P(('oct', 'leaf')), may hold values from 0 to 4095, as said below
- far_type: int32 [65536, 27], P(('oct', 'leaf')), may hold values from 0 to 63
- near_offset: int32 [65536, 4], P(('oct', 'leaf')), may hold values from -32 to 32, as said below
- near_dir: int32 [65536, 4], P(('oct', 'leaf')), may hold values from 0 to 26
- coarse_source: int32 [512, 16], P('oct'), may hold values from 0 to 511
- coarse_type: int32 [512, 16], P('oct'), may hold values from 0 to 63
- m2l: bfloat16 [64, 256, 256], replicated, may hold values from -0.375 to 0.375
- m2m: bfloat16 [8, 256, 256], replicated, may hold values from -0.03125 to 0.03125
- l2l: bfloat16 [8, 256, 256], replicated, may hold values from -0.375 to 0.375
Outputs:
- potential: float32 [65536, 128], P(('oct', 'leaf'))
Inputs may be any that keep to these rules, and one draw needn't show every extreme that they name: `counts`: each device's first leaf holds 128 panels; the lightest leaves of a device differ from device to device. `send_slots`: entry [o, d, s] is a leaf of device o, counted within its block, sent to device d in slot s, or -1 for an empty slot. Only partner devices exchange: those of one octant group whose leaf indices differ by at most 2, and those with the same leaf index in the adjacent octant groups or in the octant group halfway round (cyclically); such a pair fills its first 16 to 32 slots, all other pairs none, and every device fills all 32 slots to some one device. `far_source`: each entry o * 32 + s names a filled slot s that device o sends to the device owning the leaf; o is that device or one of its partners. `near_offset`: the neighbour lies in the same octant group; the first entry is the leaf itself (0).
All inputs are finite; a program needn't handle non-finite values.
Results may differ from a plain program's by a relative error of at most 0.012.
Values may be sent and summed in bfloat16 or wider, within the bound.
No kernel may reach another device: no remote copies, remote signals or barrier semaphores. Data moves between devices by JAX's collectives and lax.ppermute only.
A program may use at most 128 MiB of HBM per device.

v0:
```python
import math

import jax
import jax.numpy as jnp
from jax import lax
from jax.sharding import PartitionSpec as P

NB = 4
HW = 32


KAPPA = 0.25
DELTA = 0.05
RADIUS = 2.0


def padded(array, sides, width):
    for axis, dim in sides:
        size, length = (lax.axis_size(axis), array.shape[dim])
        up = [(i, (i + 1) % size) for i in range(size - 1)]
        down = [(j, i) for i, j in up]
        last = lax.slice_in_dim(array, length - width, length, axis=dim)
        first = lax.slice_in_dim(array, 0, width, axis=dim)
        before = lax.ppermute(last, axis, up)
        after = lax.ppermute(first, axis, down)
        array = jnp.concatenate([before, array, after], axis=dim)
    return array


def check_points(number):
    middle = jnp.arange(number, dtype=jnp.float32) + 0.5
    height = 1.0 - 2.0 * middle / number
    radial = jnp.sqrt(jnp.maximum(1.0 - height * height, 0.0))
    azimuth = math.pi * (1.0 + math.sqrt(5.0)) * middle
    return RADIUS * jnp.stack([radial * jnp.cos(azimuth), radial * jnp.sin(azimuth), height])


def damped_green(squared):
    spread = jnp.sqrt(squared + DELTA * DELTA)
    return jnp.exp(-KAPPA * spread) / spread


def leaf_kernels(panel_xyz, checks):
    between = panel_xyz[:, :, :, None] - checks[None, :, None, :]
    return damped_green(jnp.sum(between * between, axis=1)).astype(jnp.bfloat16)


def direction_shift(directions):
    return 2.0 * jnp.stack(
        [directions // 9 - 1, directions // 3 % 3 - 1, directions % 3 - 1], axis=-1
    ).astype(jnp.float32)


def near_field(target_xyz, sources, shifts):
    between = (
        target_xyz[:, None, :, :, None] - sources[:, :, 0:3, None, :] - shifts[:, :, :, None, None]
    )
    kernel = damped_green(jnp.sum(between * between, axis=2)).astype(jnp.bfloat16)
    weights = sources[:, :, 3, :].astype(jnp.bfloat16)
    return jnp.einsum("bnpq,bnq->bp", kernel, weights, preferred_element_type=jnp.float32)


def grouped_sum(entries, kinds, number):
    selector = (kinds[:, :, None] == jnp.arange(number, dtype=jnp.int32)[None, None, :]).astype(
        jnp.bfloat16
    )
    summed = jnp.einsum("bnt,bnk->btk", selector, entries, preferred_element_type=jnp.float32)
    return summed.astype(jnp.bfloat16)


def translate(grouped, table):
    rows = grouped.shape[0]
    return jnp.dot(
        grouped.reshape(rows, -1),
        table.reshape(-1, table.shape[2]),
        preferred_element_type=jnp.float32,
    )


def by_child(values, children):
    chosen = children[:, None] == jnp.arange(8, dtype=jnp.int32)[None, :]
    return jnp.where(chosen[:, :, None], values[:, None, :], jnp.zeros((), values.dtype))


def local(
    density,
    positions,
    counts,
    leaf_parent,
    child_pos,
    send_slots,
    far_source,
    far_type,
    near_offset,
    near_dir,
    coarse_source,
    coarse_type,
    m2l,
    m2m,
    l2l,
):
    leaves, panels = density.shape
    width = m2l.shape[1]
    operators = m2l.shape[0]
    parent_rows = coarse_source.shape[0]
    occupied = jnp.arange(panels, dtype=jnp.int32)[None, :] < counts[:, None]
    masked = jnp.where(occupied, density, jnp.zeros((), density.dtype))
    masked_low = masked.astype(jnp.bfloat16)
    checks = check_points(width)
    stacked = jnp.concatenate([positions, masked[:, None, :]], axis=1)
    window = padded(stacked, (("leaf", 0),), HW)
    blocks = math.gcd(leaves, 64)

    def moment_block(pieces):
        panel_xyz, weights = pieces
        kernel = leaf_kernels(panel_xyz, checks)
        return jnp.einsum(
            "bpk,bp->bk", kernel, weights, preferred_element_type=jnp.float32
        ) / math.sqrt(panels)

    moments = lax.map(
        moment_block,
        (positions.reshape(-1, blocks, 3, panels), masked_low.reshape(-1, blocks, panels)),
    )
    moments = moments.reshape(leaves, width).astype(jnp.bfloat16)
    slot_table = send_slots[0]
    outgoing = jnp.where(
        (slot_table >= 0)[:, :, None],
        moments[jnp.maximum(slot_table, 0)],
        jnp.zeros((), jnp.bfloat16),
    )
    incoming = lax.all_to_all(outgoing, ("oct", "leaf"), split_axis=0, concat_axis=0, tiled=True)
    received = incoming.reshape(-1, width)
    far_local = translate(grouped_sum(received[far_source], far_type, operators), m2l)
    translated = translate(by_child(moments, child_pos), m2m).astype(jnp.bfloat16)
    selector = (leaf_parent[None, :] == jnp.arange(parent_rows, dtype=jnp.int32)[:, None]).astype(
        jnp.bfloat16
    )
    partial_sums = jnp.dot(selector, translated, preferred_element_type=jnp.float32)
    summed = lax.psum(partial_sums.astype(jnp.bfloat16), "leaf")
    every_parent = lax.all_gather(summed, "oct", axis=0, tiled=True)
    parent_local = translate(
        grouped_sum(every_parent[coarse_source], coarse_type, operators), m2l
    ).astype(jnp.bfloat16)
    expansions = (
        far_local + translate(by_child(parent_local[leaf_parent], child_pos), l2l)
    ).astype(jnp.bfloat16)
    small = math.gcd(leaves, 64)
    near_weight = 1.0 / math.sqrt(NB * panels)

    def potential_block(pieces):
        first, panel_xyz, local_rows, offsets, directions = pieces
        targets = HW + first + jnp.arange(small, dtype=jnp.int32)[:, None] + offsets
        sources = window[targets]
        near = near_field(panel_xyz, sources, direction_shift(directions))
        kernel = leaf_kernels(panel_xyz, checks)
        far = jnp.einsum(
            "bpk,bk->bp", kernel, local_rows, preferred_element_type=jnp.float32
        ) / math.sqrt(width)
        return near_weight * near + far

    starts = jnp.arange(leaves // small, dtype=jnp.int32) * small
    fields = lax.map(
        potential_block,
        (
            starts,
            positions.reshape(-1, small, 3, panels),
            expansions.reshape(-1, small, width),
            near_offset.reshape(-1, small, near_offset.shape[1]),
            near_dir.reshape(-1, small, near_dir.shape[1]),
        ),
    )
    fields = fields.reshape(leaves, panels)
    return jnp.where(occupied, 0.5 * density + fields, jnp.zeros((), density.dtype))


def solution(mesh):
    placed = (
        P(("oct", "leaf"), None),
        P(("oct", "leaf"), None, None),
        P(("oct", "leaf")),
        P(("oct", "leaf")),
        P(("oct", "leaf")),
        P(("oct", "leaf"), None, None),
        P(("oct", "leaf"), None),
        P(("oct", "leaf"), None),
        P(("oct", "leaf"), None),
        P(("oct", "leaf"), None),
        P("oct", None),
        P("oct", None),
        P(),
        P(),
        P(),
    )
    return jax.shard_map(
        local, mesh=mesh, in_specs=placed, out_specs=P(("oct", "leaf"), None), check_vma=False
    )
```

profile of v0, /device:TPU:1, one launch (start us, length us, event | category | flops | bytes accessed | tf_op | source)
XLA Modules:
  0.0 704.2 jit_solution(8011697287019484235)
XLA Ops:
  5.1 66.8 %while.23 = (s32[]{:T(128)}, bf16[8,64,256]{2,1,0:T(8,128)(2,1)S(1)}, f32[8,64,3,128]{3,2,1,0:T(4,128)S(1)}, f32[3,256]{1,0:T(4,128)S(1)}, bf16[8,64,128]{2,1,0:T(8,128)(2,1)S(1)}, /*index=5*/s32[]{:T(128)}) while((s32[]{:T(128)}, bf16[8,64,256]{2,1,0:T(8,128)(2,1)S(1)}, f32[8,64,3,128]{3,2,1,0:T(4,128)S(1)}, f32[3,256]{1,0:T(4,128)S(1)}, ...), condition=%wide.region_2.3_spmd, body=%wide.region_0.2_spmd.sunk | while | flops 29376512 | bytes 17321040 | solution.py:121
  5.1 4.4 multiply_reduce_fusion.6
  13.5 4.4 multiply_reduce_fusion.6
  21.8 4.4 multiply_reduce_fusion.6
  30.2 4.4 multiply_reduce_fusion.6
  38.5 4.4 multiply_reduce_fusion.6
  46.9 4.4 multiply_reduce_fusion.6
  55.2 4.4 multiply_reduce_fusion.6
  63.6 4.4 multiply_reduce_fusion.6
  72.2 17.0 %gather_fusion.1 = bf16[4096,256]{1,0:T(8,128)(2,1)} fusion(bf16[512,256]{1,0:T(8,128)(2,1)S(1)} %bitcast.146, s32[4096]{0:T(1024)S(1)} %broadcast_clamp_fusion), kind=kCustom, calls=%fused_computation.1 | custom fusion | bytes 4210688 | tf_op jit(solution)/shard_map/gather | solution.py:129
  92.3 11.5 %all-to-all-start = ((bf16[128,32,256]{2,1,0:T(8,128)(2,1)}), bf16[128,32,256]{2,1,0:T(8,128)(2,1)S(1)}, u32[]{:S(2)}, u32[]{:S(2)}) async-start(bf16[128,32,256]{2,1,0:T(8,128)(2,1)} %broadcast_select_fusion), calls=%async_computation | async-start | bytes 4194304 | tf_op jit(solution)/shard_map/all_to_all | solution.py:132
  105.4 3.9 collective-permute-start
  112.8 68.1 %psum.7 = bf16[64,256]{1,0:T(8,128)(2,1)S(1)} all-reduce(bf16[64,256]{1,0:T(8,128)(2,1)S(1)} %fusion.59), channel_id=1, replica_groups=mesh['oct'=8,'leaf'=16] {'leaf'}, use_global_device_ids=true, to_apply=%region_3.4 | all-reduce | flops 16384 | bytes 65536 | tf_op jit(solution)/shard_map/psum | solution.py:140
  186.1 28.6 %all_gather.3 = bf16[512,256]{1,0:T(8,128)(2,1)S(1)} all-gather(bf16[64,256]{1,0:T(8,128)(2,1)S(1)} %psum.7), channel_id=1, replica_groups=mesh['oct'=8,'leaf'=16] {'oct'}, dimensions={0}, use_global_device_ids=true | all-gather | bytes 294912 | tf_op jit(solution)/shard_map/all_gather | solution.py:141
  214.7 5.0 gather_fusion.3
  222.5 6.2 fusion.56
  237.0 38.8 %gather_fusion.2 = bf16[13824,256]{1,0:T(8,128)(2,1)} fusion(bf16[4096,256]{1,0:T(8,128)(2,1)S(1)} %bitcast.145, s32[14336]{0:T(1024)S(1)} %pad_clamp_fusion.1), kind=kCustom, calls=%fused_computation.2 | custom fusion | bytes 14211072 | tf_op jit(solution)/shard_map/gather | solution.py:134
  275.7 11.3 %reshape.405 = bf16[512,27,256]{2,1,0:T(8,128)(2,1)} reshape(bf16[13824,256]{1,0:T(8,128)(2,1)} %gather_fusion.2) | data formatting | bytes 14155776 | tf_op jit(solution)/shard_map/gather | solution.py:134
  287.1 13.6 %convolution_convert_fusion = bf16[512,64,256]{2,1,0:T(8,128)(2,1)} fusion(bf16[512,27,256]{2,1,0:T(8,128)(2,1)} %reshape.405, s32[512,27]{1,0:T(8,128)S(1)} %copy-done.3), kind=kOutput, calls=%fused_computation.57 | convolution fusion | flops 462258176 | bytes 23910400 | tf_op jit(solution)/shard_map/bnt,bnk->btk/dot_general | solution.py:67
  300.8 26.3 %fusion.47 = bf16[512,256]{1,0:T(8,128)(2,1)S(1)} fusion(f32[512,256]{1,0:T(8,128)S(1)} %copy-done.14, bf16[64,256,256]{2,1,0:T(8,128)(2,1)} %param.31, bf16[512,64,256]{2,1,0:T(8,128)(2,1)} %convolution_convert_fusion), kind=kOutput, calls=%fused_computation.75 | convolution fusion | flops 4295229440 | bytes 25952256 | tf_op jit(solution)/shard_map/dot_general | solution.py:73
  327.1 375.6 %while.24 = (s32[]{:T(128)}, f32[8,64,128]{2,1,0:T(8,128)S(1)}, f32[8,64,3,128]{3,2,1,0:T(4,128)}, s32[8]{0:T(128)S(1)}, s32[8,64,4]{1,0,2:T(8,128)}, /*index=5*...) while((s32[]{:T(128)}, f32[8,64,128]{2,1,0:T(8,128)S(1)}, ...), condition=%wide.region_7.8_spmd, body=%wide.region_4.7_spmd.sunk | while | flops 100699968 | bytes 55417496 | solution.py:163
  333.1 21.4 %multiply_reduce_fusion.8 = f32[64,4,128,128]{3,2,1,0:T(8,128)} fusion(f32[64,4,3]{2,1,0:T(4,128)S(1)} %copy.149, f32[64,4,3,128]{3,2,1,0:T(4,128)S(1)} %copy.152, f32[64,3,128]{2,1,0:T(4,128)S(1)} %dynamic-slice_bitcast_fusion.10), kind=kLoop, calls=%fused_computation.15.clone.1 | loop fusion | flops 46137344 | bytes 17271808 | tf_op jit(solution)/shard_map/while/body/eval_jaxpr/reduce_sum | solution.py:58
  354.6 11.2 %fusion.99 = f32[64,1,128,1]{2,1,3,0:T(1,128)S(1)} fusion(f32[64,4,128,128]{3,2,1,0:T(8,128)} %multiply_reduce_fusion.8, bf16[64,4,128,1]{2,0,1,3:T(8,128)(2,1)S(1)} %bitcast.157), kind=kOutput, calls=%fused_computation.19.clone.1 | convolution fusion | flops 25165824 | bytes 16875520 | tf_op jit(solution)/shard_map/while/body/eval_jaxpr/bnpq,bnq->bp/dot_general | solution.py:60
  365.7 4.4 multiply_reduce_fusion.7
  370.2 3.9 fusion.96
  380.1 21.4 %multiply_reduce_fusion.8 = f32[64,4,128,128]{3,2,1,0:T(8,128)} fusion(f32[64,4,3]{2,1,0:T(4,128)S(1)} %copy.149, f32[64,4,3,128]{3,2,1,0:T(4,128)S(1)} %copy.152, f32[64,3,128]{2,1,0:T(4,128)S(1)} %dynamic-slice_bitcast_fusion.10), kind=kLoop, calls=%fused_computation.15.clone.1 | loop fusion | flops 46137344 | bytes 17271808 | tf_op jit(solution)/shard_map/while/body/eval_jaxpr/reduce_sum | solution.py:58
  401.5 11.2 %fusion.99 = f32[64,1,128,1]{2,1,3,0:T(1,128)S(1)} fusion(f32[64,4,128,128]{3,2,1,0:T(8,128)} %multiply_reduce_fusion.8, bf16[64,4,128,1]{2,0,1,3:T(8,128)(2,1)S(1)} %bitcast.157), kind=kOutput, calls=%fused_computation.19.clone.1 | convolution fusion | flops 25165824 | bytes 16875520 | tf_op jit(solution)/shard_map/while/body/eval_jaxpr/bnpq,bnq->bp/dot_general | solution.py:60
  412.7 4.4 multiply_reduce_fusion.7
  417.1 3.9 fusion.96
  427.0 21.4 %multiply_reduce_fusion.8 = f32[64,4,128,128]{3,2,1,0:T(8,128)} fusion(f32[64,4,3]{2,1,0:T(4,128)S(1)} %copy.149, f32[64,4,3,128]{3,2,1,0:T(4,128)S(1)} %copy.152, f32[64,3,128]{2,1,0:T(4,128)S(1)} %dynamic-slice_bitcast_fusion.10), kind=kLoop, calls=%fused_computation.15.clone.1 | loop fusion | flops 46137344 | bytes 17271808 | tf_op jit(solution)/shard_map/while/body/eval_jaxpr/reduce_sum | solution.py:58
  448.4 11.2 %fusion.99 = f32[64,1,128,1]{2,1,3,0:T(1,128)S(1)} fusion(f32[64,4,128,128]{3,2,1,0:T(8,128)} %multiply_reduce_fusion.8, bf16[64,4,128,1]{2,0,1,3:T(8,128)(2,1)S(1)} %bitcast.157), kind=kOutput, calls=%fused_computation.19.clone.1 | convolution fusion | flops 25165824 | bytes 16875520 | tf_op jit(solution)/shard_map/while/body/eval_jaxpr/bnpq,bnq->bp/dot_general | solution.py:60
  459.6 4.4 multiply_reduce_fusion.7
  464.1 3.9 fusion.96
  474.0 21.4 %multiply_reduce_fusion.8 = f32[64,4,128,128]{3,2,1,0:T(8,128)} fusion(f32[64,4,3]{2,1,0:T(4,128)S(1)} %copy.149, f32[64,4,3,128]{3,2,1,0:T(4,128)S(1)} %copy.152, f32[64,3,128]{2,1,0:T(4,128)S(1)} %dynamic-slice_bitcast_fusion.10), kind=kLoop, calls=%fused_computation.15.clone.1 | loop fusion | flops 46137344 | bytes 17271808 | tf_op jit(solution)/shard_map/while/body/eval_jaxpr/reduce_sum | solution.py:58
  495.4 11.2 %fusion.99 = f32[64,1,128,1]{2,1,3,0:T(1,128)S(1)} fusion(f32[64,4,128,128]{3,2,1,0:T(8,128)} %multiply_reduce_fusion.8, bf16[64,4,128,1]{2,0,1,3:T(8,128)(2,1)S(1)} %bitcast.157), kind=kOutput, calls=%fused_computation.19.clone.1 | convolution fusion | flops 25165824 | bytes 16875520 | tf_op jit(solution)/shard_map/while/body/eval_jaxpr/bnpq,bnq->bp/dot_general | solution.py:60
  506.6 4.4 multiply_reduce_fusion.7
  520.9 21.4 %multiply_reduce_fusion.8 = f32[64,4,128,128]{3,2,1,0:T(8,128)} fusion(f32[64,4,3]{2,1,0:T(4,128)S(1)} %copy.149, f32[64,4,3,128]{3,2,1,0:T(4,128)S(1)} %copy.152, f32[64,3,128]{2,1,0:T(4,128)S(1)} %dynamic-slice_bitcast_fusion.10), kind=kLoop, calls=%fused_computation.15.clone.1 | loop fusion | flops 46137344 | bytes 17271808 | tf_op jit(solution)/shard_map/while/body/eval_jaxpr/reduce_sum | solution.py:58
  542.3 11.2 %fusion.99 = f32[64,1,128,1]{2,1,3,0:T(1,128)S(1)} fusion(f32[64,4,128,128]{3,2,1,0:T(8,128)} %multiply_reduce_fusion.8, bf16[64,4,128,1]{2,0,1,3:T(8,128)(2,1)S(1)} %bitcast.157), kind=kOutput, calls=%fused_computation.19.clone.1 | convolution fusion | flops 25165824 | bytes 16875520 | tf_op jit(solution)/shard_map/while/body/eval_jaxpr/bnpq,bnq->bp/dot_general | solution.py:60
  553.5 4.4 multiply_reduce_fusion.7
  567.9 21.4 %multiply_reduce_fusion.8 = f32[64,4,128,128]{3,2,1,0:T(8,128)} fusion(f32[64,4,3]{2,1,0:T(4,128)S(1)} %copy.149, f32[64,4,3,128]{3,2,1,0:T(4,128)S(1)} %copy.152, f32[64,3,128]{2,1,0:T(4,128)S(1)} %dynamic-slice_bitcast_fusion.10), kind=kLoop, calls=%fused_computation.15.clone.1 | loop fusion | flops 46137344 | bytes 17271808 | tf_op jit(solution)/shard_map/while/body/eval_jaxpr/reduce_sum | solution.py:58
  589.3 11.2 %fusion.99 = f32[64,1,128,1]{2,1,3,0:T(1,128)S(1)} fusion(f32[64,4,128,128]{3,2,1,0:T(8,128)} %multiply_reduce_fusion.8, bf16[64,4,128,1]{2,0,1,3:T(8,128)(2,1)S(1)} %bitcast.157), kind=kOutput, calls=%fused_computation.19.clone.1 | convolution fusion | flops 25165824 | bytes 16875520 | tf_op jit(solution)/shard_map/while/body/eval_jaxpr/bnpq,bnq->bp/dot_general | solution.py:60
  600.4 4.4 multiply_reduce_fusion.7
  614.8 21.4 %multiply_reduce_fusion.8 = f32[64,4,128,128]{3,2,1,0:T(8,128)} fusion(f32[64,4,3]{2,1,0:T(4,128)S(1)} %copy.149, f32[64,4,3,128]{3,2,1,0:T(4,128)S(1)} %copy.152, f32[64,3,128]{2,1,0:T(4,128)S(1)} %dynamic-slice_bitcast_fusion.10), kind=kLoop, calls=%fused_computation.15.clone.1 | loop fusion | flops 46137344 | bytes 17271808 | tf_op jit(solution)/shard_map/while/body/eval_jaxpr/reduce_sum | solution.py:58
  636.2 11.2 %fusion.99 = f32[64,1,128,1]{2,1,3,0:T(1,128)S(1)} fusion(f32[64,4,128,128]{3,2,1,0:T(8,128)} %multiply_reduce_fusion.8, bf16[64,4,128,1]{2,0,1,3:T(8,128)(2,1)S(1)} %bitcast.157), kind=kOutput, calls=%fused_computation.19.clone.1 | convolution fusion | flops 25165824 | bytes 16875520 | tf_op jit(solution)/shard_map/while/body/eval_jaxpr/bnpq,bnq->bp/dot_general | solution.py:60
  647.4 4.4 multiply_reduce_fusion.7
  661.8 21.4 %multiply_reduce_fusion.8 = f32[64,4,128,128]{3,2,1,0:T(8,128)} fusion(f32[64,4,3]{2,1,0:T(4,128)S(1)} %copy.149, f32[64,4,3,128]{3,2,1,0:T(4,128)S(1)} %copy.152, f32[64,3,128]{2,1,0:T(4,128)S(1)} %dynamic-slice_bitcast_fusion.10), kind=kLoop, calls=%fused_computation.15.clone.1 | loop fusion | flops 46137344 | bytes 17271808 | tf_op jit(solution)/shard_map/while/body/eval_jaxpr/reduce_sum | solution.py:58
  683.2 11.2 %fusion.99 = f32[64,1,128,1]{2,1,3,0:T(1,128)S(1)} fusion(f32[64,4,128,128]{3,2,1,0:T(8,128)} %multiply_reduce_fusion.8, bf16[64,4,128,1]{2,0,1,3:T(8,128)(2,1)S(1)} %bitcast.157), kind=kOutput, calls=%fused_computation.19.clone.1 | convolution fusion | flops 25165824 | bytes 16875520 | tf_op jit(solution)/shard_map/while/body/eval_jaxpr/bnpq,bnq->bp/dot_general | solution.py:60
  694.3 4.4 multiply_reduce_fusion.7
  (260 shorter events, 124.1 us)
Async XLA Ops:
  0.0 231.4 %copy-start = (bf16[8,256,256]{2,1,0:T(8,128)(2,1)S(1)}, bf16[8,256,256]{2,1,0:T(8,128)(2,1)}, u32[]{:S(2)}) copy-start(bf16[8,256,256]{2,1,0:T(8,128)(2,1)} %param.33) | copy-start | bytes 3145732
  71.9 17.4 %copy-start.2 = (f32[8,64,3,128]{3,2,1,0:T(4,128)}, f32[8,64,3,128]{3,2,1,0:T(4,128)S(1)}, u32[]{:S(2)}) copy-start(f32[8,64,3,128]{3,2,1,0:T(4,128)S(1)} %get-tuple-element.418) | copy-start | bytes 2359300
  71.9 17.4 %copy-start.5 = (f32[3,256]{1,0:T(4,128)}, f32[3,256]{1,0:T(4,128)S(1)}, u32[]{:S(2)}) copy-start(f32[3,256]{1,0:T(4,128)S(1)} %get-tuple-element.421) | copy-start | bytes 9220
  89.3 21.3 %copy-start.12 = (s32[512]{0:T(512)S(1)}, s32[512]{0:T(512)}, u32[]{:S(2)}) copy-start(s32[512]{0:T(512)} %param.23) | copy-start | bytes 6148
  89.3 21.3 %copy-start.13 = (s32[512]{0:T(512)S(1)}, s32[512]{0:T(512)}, u32[]{:S(2)}) copy-start(s32[512]{0:T(512)} %param.22) | copy-start | bytes 6148
  89.3 91.6 %copy-start.11 = (s32[64,16]{0,1:T(8,128)S(1)}, s32[64,16]{0,1:T(8,128)}, u32[]{:S(2)}) copy-start(s32[64,16]{0,1:T(8,128)} %param.29) | copy-start | bytes 12292
  89.3 91.8 %copy-start.9 = (s32[64,16]{0,1:T(8,128)S(1)}, s32[64,16]{0,1:T(8,128)}, u32[]{:S(2)}) copy-start(s32[64,16]{0,1:T(8,128)} %param.30) | copy-start | bytes 12292
  89.3 94.8 %copy-start.10 = (s32[512,4]{0,1:T(4,128)S(1)}, s32[512,4]{0,1:T(4,128)}, u32[]{:S(2)}) copy-start(s32[512,4]{0,1:T(4,128)} %param.27) | copy-start | bytes 24580
  92.3 144.7 %all-to-all-start = ((bf16[128,32,256]{2,1,0:T(8,128)(2,1)}), bf16[128,32,256]{2,1,0:T(8,128)(2,1)S(1)}, u32[]{:S(2)}, u32[]{:S(2)}) async-start(bf16[128,32,256]{2,1,0:T(8,128)(2,1)} %broadcast_select_fusion), calls=%async_computation | async-start | bytes 4194304 | tf_op jit(solution)/shard_map/all_to_all | solution.py:132
  105.4 128.6 %collective-permute-start = (f32[32,4,128]{2,1,0:T(4,128)}, f32[32,4,128]{2,1,0:T(4,128)}, u32[]{:S(2)}, u32[]{:S(2)}) collective-permute-start(f32[32,4,128]{2,1,0:T(4,128)} %get-tuple-element.266), channel_id=1, source_target_pairs={{0,1},{1,2},{2,3},{3,4},{4,5},{5,6},{6,7},{7,8},{8,9},{9,10},{10,1... | collective-permute-start | bytes 196616 | tf_op jit(solution)/shard_map/ppermute | solution.py:24
  109.3 124.7 %collective-permute-start.1 = (f32[32,4,128]{2,1,0:T(4,128)}, f32[32,4,128]{2,1,0:T(4,128)}, u32[]{:S(2)}, u32[]{:S(2)}) collective-permute-start(f32[32,4,128]{2,1,0:T(4,128)} %get-tuple-element.267), channel_id=1, source_target_pairs={{1,0},{2,1},{3,2},{4,3},{5,4},{6,5},{7,6},{8,7},{9,8},{10,9},{11,1... | collective-permute-start | bytes 196616 | tf_op jit(solution)/shard_map/ppermute | solution.py:25
  275.7 11.3 %copy-start.3 = (s32[512,27]{1,0:T(8,128)S(1)}, s32[512,27]{1,0:T(8,128)}, u32[]{:S(2)}) copy-start(s32[512,27]{1,0:T(8,128)} %copy.95) | copy-start | bytes 165892
  287.1 13.7 %copy-start.14 = (f32[512,256]{1,0:T(8,128)S(1)}, f32[512,256]{1,0:T(8,128)}, u32[]{:S(2)}) copy-start(f32[512,256]{1,0:T(8,128)} %fusion.35) | copy-start | bytes 1572868
  300.8 26.3 %copy-start.6 = (f32[3,256]{1,0:T(4,128)S(1)}, f32[3,256]{1,0:T(4,128)}, u32[]{:S(2)}) copy-start(f32[3,256]{1,0:T(4,128)} %copy-done.5) | copy-start | bytes 9220
  300.8 26.3 %copy-start.7 = (f32[8,64,128]{2,1,0:T(8,128)S(1)}, f32[8,64,128]{2,1,0:T(8,128)}, u32[]{:S(2)}) copy-start(f32[8,64,128]{2,1,0:T(8,128)} %custom-call.11) | copy-start | bytes 786436
  327.1 375.6 %copy-start.4 = (f32[512,128]{1,0:T(8,128)S(1)}, f32[512,128]{1,0:T(8,128)}, u32[]{:S(2)}) copy-start(f32[512,128]{1,0:T(8,128)} %param.19) | copy-start | bytes 786436
  327.1 375.6 %copy-start.8 = (s32[512]{0:T(512)S(1)}, s32[512]{0:T(512)}, u32[]{:S(2)}) copy-start(s32[512]{0:T(512)} %param.21) | copy-start | bytes 6148
  702.7 1.3 copy-start.1
where the time goes:
time: 713 us; the launch traced here: 704 us
  other arithmetic  256 us (36%)
  matrix products  204 us (29%)
  local copies, waits for them, and re-layouts  124 us (17%)
  blocking collectives  96.7 us (14%)
  starting transfers between devices  16.7 us (2%)
    reduce_sum x8, other arithmetic, near_field(): jnp.sum(between * between, axis=2)  171 us
    dot_general x8, matrix products, near_field(): jnp.einsum('bnpq,bnq->bp', kernel, weights, preferred_element_type=jnp.fl...  89.3 us
    reduce_sum x16, other arithmetic, leaf_kernels(): return damped_green(jnp.sum(between * between, axis=1)).astype(jnp.bfloat16)  70.7 us
    psum x1, blocking collectives, local(): summed = lax.psum(partial_sums.astype(jnp.bfloat16), 'leaf')  68.1 us
    gather x2, local copies, waits for them, and re-layouts, local(): received[far_source]  50.1 us
    dot_general x3, matrix products, translate(): jnp.dot(grouped.reshape(rows, -1), table.reshape(-1, table.shape[2]), pre...  35.1 us
    dot_general x8, matrix products, potential_block(): jnp.einsum('bpk,bk->bp', kernel, local_rows, preferred_element_type=jnp.f...  31 us
    dot_general x8, matrix products, moment_block(): jnp.einsum('bpk,bp->bk', kernel, weights, preferred_element_type=jnp.floa...  30.8 us
  transfers between devices with their start and end apart: 3, of which 0 were waited for; matrix products, arithmetic and copies ran while one was open for 4% of the time, Pallas kernels for 0%

commit v1 on v0

v1 whole, which is shorter than its diff:
```python
import functools
import math

import jax
import jax.numpy as jnp
import ml_dtypes
import numpy as np
from jax import lax
from jax.experimental import pallas as pl
from jax.experimental.pallas import tpu as pltpu
from jax.sharding import PartitionSpec as P

HW = 32
KAPPA = 0.25
DELTA = 0.05
RADIUS = 2.0
RATE = -KAPPA * math.log2(math.e)
ROWS = 32
BF = jnp.bfloat16
F32 = jnp.float32
VMEM = pl.BlockSpec(memory_space=pltpu.VMEM)
SMEM = pl.BlockSpec(memory_space=pltpu.SMEM)


def np_split(values, number):
    pieces = []
    rest = values.astype(np.float32)
    for _ in range(number):
        piece = rest.astype(ml_dtypes.bfloat16)
        pieces.append(piece)
        rest = rest - piece.astype(np.float32)
    return pieces


def check_rows(number):
    middle = np.arange(number, dtype=np.float32) + np.float32(0.5)
    height = (1.0 - 2.0 * middle / np.float32(number)).astype(np.float32)
    radial = np.sqrt(np.maximum(1.0 - height * height, 0.0)).astype(np.float32)
    azimuth = np.float32(math.pi * (1.0 + math.sqrt(5.0))) * middle
    points = RADIUS * np.stack([radial * np.cos(azimuth), radial * np.sin(azimuth), height])
    high, low = np_split(points, 2)
    high, low = high.astype(np.float32), low.astype(np.float32)
    rounded = high + low
    squares = np_split(np.sum(rounded * rounded, axis=0), 3)
    rows = np.zeros((ROWS, number), np.float32)
    rows[0:3], rows[3:6], rows[6:9], rows[9:12] = -2 * high, -2 * low, -2 * high, -2 * low
    for k in range(3):
        rows[12 + k] = squares[k].astype(np.float32)
    rows[15:18] = 1.0
    return rows.astype(ml_dtypes.bfloat16)


def shift_rows():
    scale = np.zeros((27, ROWS, 128), np.float32)
    add = np.zeros((27, ROWS, 128), np.float32)
    scale[:, 0:18] = 1.0
    scale[:, 31] = 1.0
    for d in range(27):
        shift = 2.0 * np.array([d // 9 - 1, d // 3 % 3 - 1, d % 3 - 1], np.float32)
        for k in range(3):
            scale[d, 18 + k] = -shift[k]
            scale[d, 21 + k] = -shift[k]
            add[d, 24 + k] = -2 * shift[k]
            add[d, 27 + k] = -2 * shift[k]
        add[d, 30] = np.sum(shift * shift)
    return scale.astype(ml_dtypes.bfloat16), add.astype(ml_dtypes.bfloat16)


def split(value):
    high = value.astype(BF).astype(F32)
    return high, value - high


def panel_rows(coords, weights):
    highs, lows, square = [], [], None
    for value in coords:
        high, rest = split(value)
        low = rest.astype(BF).astype(F32)
        highs.append(high)
        lows.append(low)
        rounded = high + low
        square = rounded * rounded if square is None else square + rounded * rounded
    one = jnp.ones_like(square)
    zero = jnp.zeros_like(square)

    def thirds(value):
        first, rest = split(value)
        second, rest = split(rest)
        return [first, second, rest]

    minus_high = [-2.0 * value for value in highs]
    minus_low = [-2.0 * value for value in lows]
    target = highs + highs + lows + lows + [one] * 3 + thirds(square + DELTA * DELTA)
    target += [one] * 6 + highs + lows + [one, zero]
    source = minus_high + minus_low + minus_high + minus_low + thirds(square) + [one] * 3
    source += minus_high + minus_low + [zero] * 7 + [weights]
    return target, source


def place_rows(rows, scratch, write):
    for r, value in enumerate(rows):
        scratch[pl.ds(r, 8, stride=ROWS), :] = value
    for u in range(8):
        write(u, scratch[u * ROWS : (u + 1) * ROWS, :].astype(BF))


def green(squared):
    low = squared.astype(BF)
    inverse = lax.rsqrt(low)
    return jnp.exp2((low * inverse) * BF(RATE)) * inverse


def dot(a, b, over=((1,), (0,))):
    return lax.dot_general(a, b, (over, ((), ())), preferred_element_type=F32)


def moments_kernel(
    slots_ref, pos_ref, dens_ref, counts_ref, code_ref, checks_ref, m2m_ref,
    target_ref, source_ref, weight_ref, send_ref, part_ref, moments_low, moments_high, scratch, spare,
):
    step = pl.program_id(0)
    leaves = pos_ref.shape[1]
    total = moments_low.shape[0]
    checks = checks_ref[...]
    lane = lax.broadcasted_iota(jnp.int32, (8, 128), 1)

    def build(group, carry):
        at = pl.ds(pl.multiple_of(group * 8, 8), 8)
        masked = jnp.where(lane < counts_ref[at, :], dens_ref[at, :], 0.0)
        weight_ref[at, :] = masked
        target, source = panel_rows([pos_ref[d, at, :] for d in range(3)], masked)

        def put_target(u, value):
            target_ref[group * 8 + u] = value

        def put_source(u, value):
            source_ref[group * 8 + u] = value

        place_rows(target, scratch, put_target)
        place_rows(source, spare, put_source)
        return carry

    lax.fori_loop(0, leaves // 8, build, 0)
    unroll = 16

    def expand(group, carry):
        for u in range(unroll):
            leaf = group * unroll + u
            kernel = green(dot(target_ref[leaf], checks, ((0,), (0,))))
            out = dot(source_ref[leaf][16:32], kernel)[15:16]
            low = (out * (1.0 / math.sqrt(128))).astype(BF).astype(F32)
            at = pl.ds(step * leaves + leaf, 1)
            moments_low[at, :], moments_high[at, :] = low[:, :128], low[:, 128:]
        return carry

    lax.fori_loop(0, leaves // unroll, expand, 0)

    @pl.when(step == pl.num_programs(0) - 1)
    def _():
        for partner in range(8):

            def pick(s, carry):
                slot = jnp.maximum(slots_ref[partner, s], 0)
                spare[pl.ds(s, 1), :] = moments_low[pl.ds(slot, 1), :]
                scratch[pl.ds(s, 1), :] = moments_high[pl.ds(slot, 1), :]
                return carry

            lax.fori_loop(0, 32, pick, 0, unroll=8)
            send_ref[partner] = jnp.concatenate(
                [spare[0:32, :], scratch[0:32, :]], axis=1
            ).astype(BF)
        low = jnp.concatenate([moments_low[...], moments_high[...]], axis=1).astype(BF)
        parents = part_ref.shape[0]
        acc = jnp.zeros(part_ref.shape, F32)
        for c in range(8):
            row = lax.broadcasted_iota(jnp.int32, (parents, total), 0) + c * parents
            chosen = jnp.where(row == code_ref[...], 1.0, 0.0).astype(BF)
            high, rest = split(dot(chosen, low))
            acc += dot(high.astype(BF), m2m_ref[c]) + dot(rest.astype(BF), m2m_ref[c])
        part_ref[...] = acc.astype(BF)


def halo_kernel(raw_ref, source_ref, scratch):
    def build(group, carry):
        at = pl.ds(pl.multiple_of(group * 8, 8), 8)
        _, source = panel_rows([raw_ref[d, at, :] for d in range(3)], raw_ref[3, at, :])

        def put_source(u, value):
            source_ref[group * 8 + u] = value

        place_rows(source, scratch, put_source)
        return carry

    lax.fori_loop(0, raw_ref.shape[1] // 8, build, 0)


def near_kernel(
    index_ref, dir_ref, target_ref, before_ref, source_ref, after_ref, scale_ref, add_ref,
    out_ref, window, sems,
):
    step = pl.program_id(0)
    leaves = target_ref.shape[0]
    total = source_ref.shape[0]

    @pl.when(step == 0)
    def _():
        copies = [
            pltpu.make_async_copy(before_ref, window.at[0:HW], sems.at[0]),
            pltpu.make_async_copy(source_ref, window.at[HW : HW + total], sems.at[1]),
            pltpu.make_async_copy(after_ref, window.at[HW + total : 2 * HW + total], sems.at[2]),
        ]
        for copy in copies:
            copy.start()
        for copy in copies:
            copy.wait()

    unroll = 16

    def one(leaf):
        whole = step * leaves + leaf
        rows, weights = [], []
        for j in range(4):
            base = window[index_ref[j, whole]]
            way = dir_ref[j, whole]
            rows.append(base * scale_ref[way] + add_ref[way])
            weights.append(base[16:32])
        kernel = green(dot(target_ref[leaf], jnp.concatenate(rows, 1), ((0,), (0,))))
        return dot(jnp.concatenate(weights, 1), kernel, ((1,), (1,)))[15:16]

    def body(group, carry):
        for u in range(unroll):
            leaf = group * unroll + u
            out_ref[pl.ds(leaf, 1), :] = one(leaf) * (1.0 / math.sqrt(512))
        return carry

    lax.fori_loop(0, leaves // unroll, body, 0)


def translate_kernel(
    far_ref, coarse_from_ref, coarse_to_ref, recv_ref, parents_ref, m2l_ref, l2l_ref,
    out_ref, z_low, z_high, groups_low, groups_high, parents_low, parents_high, acc,
    rows_low, rows_high,
):
    step = pl.program_id(0)
    count = m2l_ref.shape[0]
    received = recv_ref.shape[0]
    cells = acc.shape[0]
    entries, leaves = far_ref.shape
    coarse, _ = coarse_from_ref.shape

    @pl.when(step == 0)
    def _():
        groups_low[...] = jnp.zeros(groups_low.shape, F32)
        groups_high[...] = jnp.zeros(groups_high.shape, F32)
        parents_low[...] = parents_ref[:, :128].astype(F32)
        parents_high[...] = parents_ref[:, 128:].astype(F32)
        acc[...] = jnp.zeros(acc.shape, F32)

        def gather(q, carry):
            for j in range(coarse):
                at = pl.ds(coarse_to_ref[j, q], 1)
                row = pl.ds(coarse_from_ref[j, q], 1)
                groups_low[at, :] = groups_low[at, :] + parents_low[row, :]
                groups_high[at, :] = groups_high[at, :] + parents_high[row, :]
            return carry

        lax.fori_loop(0, cells, gather, 0)

    for t in range(count):
        kind = step * count + t
        at = pl.ds(pl.multiple_of(kind * cells, cells), cells)
        group = jnp.concatenate([groups_low[at, :], groups_high[at, :]], axis=1).astype(BF)
        table = m2l_ref[t]
        out = dot(recv_ref[...], table)
        at = pl.ds(pl.multiple_of(kind * received, received), received)
        z_low[at, :] = out[:, :128]
        z_high[at, :] = out[:, 128:]
        acc[...] += dot(group, table)

    @pl.when(step == pl.num_programs(0) - 1)
    def _():
        local = acc[...].astype(BF)
        first = received * count * pl.num_programs(0)
        for c in range(8):
            out = dot(local, l2l_ref[c])
            at = pl.ds(first + c * cells, cells)
            z_low[at, :] = out[:, :128]
            z_high[at, :] = out[:, 128:]

        def block(group, carry):
            for u in range(8):
                lows, highs = [None] * 4, [None] * 4
                for j in range(entries):
                    at = pl.ds(far_ref[j, group * 8 + u], 1)
                    low, high = z_low[at, :], z_high[at, :]
                    k = j % 4
                    lows[k] = low if lows[k] is None else lows[k] + low
                    highs[k] = high if highs[k] is None else highs[k] + high
                at = pl.ds(group * 8 + u, 1)
                rows_low[at, :] = (lows[0] + lows[1]) + (lows[2] + lows[3])
                rows_high[at, :] = (highs[0] + highs[1]) + (highs[2] + highs[3])
            return carry

        lax.fori_loop(0, leaves // 8, block, 0)
        out_ref[:, :128] = rows_low[...].astype(BF)
        out_ref[:, 128:] = rows_high[...].astype(BF)


def far_kernel(target_ref, checks_ref, exp_ref, near_ref, dens_ref, counts_ref, out_ref):
    leaves = target_ref.shape[0]
    unroll = 16
    lane = lax.broadcasted_iota(jnp.int32, (unroll, 128), 1)
    checks = checks_ref[...]

    def body(group, carry):
        at = pl.ds(pl.multiple_of(group * unroll, unroll), unroll)
        local = exp_ref[at, :]
        outs = []
        for u in range(unroll):
            kernel = green(dot(checks, target_ref[group * unroll + u]))
            outs.append(dot(local, kernel)[u : u + 1])
        far = jnp.concatenate(outs, 0) * (1.0 / math.sqrt(256))
        value = 0.5 * dens_ref[at, :] + near_ref[at, :] + far
        out_ref[at, :] = jnp.where(lane < counts_ref[at, :], value, 0.0)
        return carry

    lax.fori_loop(0, leaves // unroll, body, 0)


def params(mib=56):
    return pltpu.CompilerParams(vmem_limit_bytes=mib * 2**20)


def local(
    density, positions, counts, leaf_parent, child_pos, send_slots, far_source, far_type,
    near_offset, near_dir, coarse_source, coarse_type, m2l, m2m, l2l,
):
    leaves, panels = density.shape
    width = m2l.shape[1]
    kinds = m2l.shape[0]
    cells = coarse_source.shape[0]
    oct_size, leaf_size = lax.axis_size("oct"), lax.axis_size("leaf")
    group, place = lax.axis_index("oct"), lax.axis_index("leaf")
    cap = send_slots.shape[2]
    planes = positions.transpose(1, 0, 2)
    counts_column = counts[:, None]
    spread_counts = jnp.broadcast_to(counts_column, (leaves, panels))
    checks = check_rows(width)
    scale, add = shift_rows()

    lanes = jnp.arange(panels, dtype=jnp.int32)[None, :]

    def edge(begin):
        rows = slice(begin, begin + HW)
        masked = jnp.where(lanes < counts_column[rows], density[rows], 0.0)
        return jnp.concatenate([planes[:, rows], masked[None]], axis=0)

    up = [(i, i + 1) for i in range(leaf_size - 1)]
    down = [(i + 1, i) for i in range(leaf_size - 1)]
    before = lax.ppermute(edge(leaves - HW), "leaf", up)
    after = lax.ppermute(edge(0), "leaf", down)

    moves = [("leaf", k - 2) for k in range(5)]
    moves += [("oct", 1), ("oct", -1), ("oct", oct_size // 2)]
    targets = []
    for axis, by in moves:
        if axis == "leaf":
            targets.append(group * leaf_size + jnp.clip(place - by, 0, leaf_size - 1))
        else:
            targets.append((group - by) % oct_size * leaf_size + place)
    slots = jnp.stack([send_slots[0, target] for target in targets])
    code = (child_pos * cells + leaf_parent)[None, :]

    steps = 8
    block = leaves // steps
    target, source, weights, send, partial = pl.pallas_call(
        moments_kernel,
        grid=(steps,),
        in_specs=[
            SMEM,
            pl.BlockSpec((3, block, panels), lambda i: (0, i, 0)),
            pl.BlockSpec((block, panels), lambda i: (i, 0)),
            pl.BlockSpec((block, panels), lambda i: (i, 0)),
            VMEM, VMEM, VMEM,
        ],
        out_specs=[
            pl.BlockSpec((block, ROWS, panels), lambda i: (i, 0, 0)),
            pl.BlockSpec((block, ROWS, panels), lambda i: (i, 0, 0)),
            pl.BlockSpec((block, panels), lambda i: (i, 0)),
            VMEM, VMEM,
        ],
        out_shape=[
            jax.ShapeDtypeStruct((leaves, ROWS, panels), BF),
            jax.ShapeDtypeStruct((leaves, ROWS, panels), BF),
            jax.ShapeDtypeStruct((leaves, panels), F32),
            jax.ShapeDtypeStruct((8, cap, width), BF),
            jax.ShapeDtypeStruct((cells, width), BF),
        ],
        scratch_shapes=[
            pltpu.VMEM((leaves, 128), F32),
            pltpu.VMEM((leaves, 128), F32),
            pltpu.VMEM((8 * ROWS, panels), F32),
            pltpu.VMEM((8 * ROWS, panels), F32),
        ],
        compiler_params=params(),
        name="moments",
    )(slots, planes, density, spread_counts, code, checks, m2m)

    halo = pl.pallas_call(
        halo_kernel,
        in_specs=[VMEM],
        out_specs=VMEM,
        out_shape=jax.ShapeDtypeStruct((2 * HW, ROWS, panels), BF),
        scratch_shapes=[pltpu.VMEM((8 * ROWS, panels), F32)],
        compiler_params=params(),
        name="halo",
    )(jnp.concatenate([before, after], axis=1))

    pieces = []
    for k, (axis, by) in enumerate(moves):
        if axis == "leaf" and by == 0:
            pieces.append(send[k])
        elif axis == "leaf":
            pairs = [(i, i - by) for i in range(leaf_size) if 0 <= i - by < leaf_size]
            pieces.append(lax.ppermute(send[k], "leaf", pairs))
        else:
            pairs = [(i, (i - by) % oct_size) for i in range(oct_size)]
            pieces.append(lax.ppermute(send[k], "oct", pairs))
    received = jnp.concatenate(pieces, axis=0)

    group_parts = lax.all_gather(partial, "leaf", axis=0)
    group_sum = jnp.sum(group_parts.astype(F32), axis=0).astype(BF)
    every_parent = lax.all_gather(group_sum, "oct", axis=0, tiled=True)

    index = (jnp.arange(leaves, dtype=jnp.int32)[:, None] + near_offset + HW).T
    near = pl.pallas_call(
        near_kernel,
        grid=(steps,),
        in_specs=[
            SMEM, SMEM,
            pl.BlockSpec((block, ROWS, panels), lambda i: (i, 0, 0)),
            pl.BlockSpec(memory_space=pl.ANY),
            pl.BlockSpec(memory_space=pl.ANY),
            pl.BlockSpec(memory_space=pl.ANY),
            VMEM, VMEM,
        ],
        out_specs=pl.BlockSpec((block, panels), lambda i: (i, 0)),
        out_shape=jax.ShapeDtypeStruct((leaves, panels), F32),
        scratch_shapes=[
            pltpu.VMEM((leaves + 2 * HW, ROWS, panels), BF),
            pltpu.SemaphoreType.DMA((3,)),
        ],
        compiler_params=params(),
        name="near",
    )(index, near_dir.T, target, halo[:HW], source, halo[HW:], scale, add)

    owner, slot = far_source // cap, far_source % cap
    owner_group, owner_place = owner // leaf_size, owner % leaf_size
    partner = jnp.where(
        owner_group == group,
        owner_place - place + 2,
        jnp.where(
            owner_group == (group + 1) % oct_size,
            5,
            jnp.where(owner_group == (group + oct_size - 1) % oct_size, 6, 7),
        ),
    )
    far_rows = (far_type * 8 + partner) * cap + slot
    own_row = kinds * 8 * cap + child_pos * cells + leaf_parent
    far_rows = jnp.concatenate([far_rows.T, own_row[None, :]], axis=0)
    coarse_to = (coarse_type * cells + jnp.arange(cells, dtype=jnp.int32)[:, None]).T
    span = 8
    expansions = pl.pallas_call(
        translate_kernel,
        grid=(kinds // span,),
        in_specs=[
            SMEM, SMEM, SMEM, VMEM, VMEM,
            pl.BlockSpec((span, width, width), lambda i: (i, 0, 0)),
            VMEM,
        ],
        out_specs=VMEM,
        out_shape=jax.ShapeDtypeStruct((leaves, width), BF),
        scratch_shapes=[
            pltpu.VMEM((kinds * 8 * cap + 8 * cells, 128), F32),
            pltpu.VMEM((kinds * 8 * cap + 8 * cells, 128), F32),
            pltpu.VMEM((kinds * cells, 128), F32),
            pltpu.VMEM((kinds * cells, 128), F32),
            pltpu.VMEM((oct_size * cells, 128), F32),
            pltpu.VMEM((oct_size * cells, 128), F32),
            pltpu.VMEM((cells, width), F32),
            pltpu.VMEM((leaves, 128), F32),
            pltpu.VMEM((leaves, 128), F32),
        ],
        compiler_params=params(),
        name="translate",
    )(far_rows, coarse_source.T, coarse_to, received, every_parent, m2l, l2l)

    return pl.pallas_call(
        far_kernel,
        grid=(steps,),
        in_specs=[
            pl.BlockSpec((block, ROWS, panels), lambda i: (i, 0, 0)),
            VMEM,
            pl.BlockSpec((block, width), lambda i: (i, 0)),
            pl.BlockSpec((block, panels), lambda i: (i, 0)),
            pl.BlockSpec((block, panels), lambda i: (i, 0)),
            pl.BlockSpec((block, panels), lambda i: (i, 0)),
        ],
        out_specs=pl.BlockSpec((block, panels), lambda i: (i, 0)),
        out_shape=jax.ShapeDtypeStruct((leaves, panels), F32),
        compiler_params=params(),
        name="far",
    )(target, checks.T, expansions, near, density, spread_counts)


def solution(mesh):
    both = ("oct", "leaf")
    placed = (
        P(both, None), P(both, None, None), P(both), P(both), P(both), P(both, None, None),
        P(both, None), P(both, None), P(both, None), P(both, None),
        P("oct", None), P("oct", None), P(), P(), P(),
    )
    return jax.shard_map(
        local, mesh=mesh, in_specs=placed, out_specs=P(both, None), check_vma=False
    )
```

time: 713 us -> 390 us (0.55)
  Pallas kernels: 0 us -> 299 us
  other arithmetic: 256 us -> 6.22 us
  matrix products: 204 us -> 0 us
  local copies, waits for them, and re-layouts: 124 us -> 9.23 us
  blocking collectives: 96.7 us -> 38.9 us
  waiting for transfers between devices: 0.01 us -> 9.08 us
    pallas_call x0 -> x5, Pallas kernels: none -> 299 us  [the longest x1 109 us: local(): pl.pallas_call(moments_kernel, grid=(steps,), in_specs=[SMEM, pl.BlockSpe...]
    reduce_sum x24 -> x1, other arithmetic: 242 us -> 0.08 us  [local(): group_sum = jnp.sum(group_parts.astype(F32), axis=0).astype(BF)]
    dot_general x30 -> x0, matrix products: 204 us -> none  [the longest x8 89.3 us: near_field(): jnp.einsum('bnpq,bnq->bp', kernel, weights, preferred_element_type=jnp.fl...]
    gather x21 -> x0, local copies, waits for them, and re-layouts: 93.2 us -> none  [the longest x2 50.1 us: local(): received[far_source]]
    psum x1 -> x0, blocking collectives: 68.1 us -> none  [local(): summed = lax.psum(partial_sums.astype(jnp.bfloat16), 'leaf')]
    ppermute x2 -> x9, starting transfers between devices: 5.18 us -> 23.8 us  [the longest x4 9.86 us: local(): pieces.append(lax.ppermute(send[k], 'leaf', pairs))]
    all_to_all x1 -> x0, starting transfers between devices: 11.5 us -> none  [local(): lax.all_to_all(outgoing, ('oct', 'leaf'), split_axis=0, concat_axis=0, ti...]
    all_gather x1 -> x2, blocking collectives: 28.6 us -> 38.9 us  [the longest x1 20.4 us: local(): group_parts = lax.all_gather(partial, 'leaf', axis=0)]
  transfers between devices with their start and end apart: 3 -> 9, of which waited for: 0 -> 4; matrix products, arithmetic and copies ran while one was open for 4% -> 3% of each run, Pallas kernels for 0% -> 38%
where the time goes in v1:
time: 390 us; the launch traced here: 387 us
  Pallas kernels  299 us (77%)
  blocking collectives  38.9 us (10%)
  starting transfers between devices  23.8 us (6%)
  local copies, waits for them, and re-layouts  9.23 us (2%)
  waiting for transfers between devices  9.08 us (2%)
  other arithmetic  6.22 us (2%)
    pallas_call x1, Pallas kernels, local(): pl.pallas_call(moments_kernel, grid=(steps,), in_specs=[SMEM, pl.BlockSpe...  109 us
    pallas_call x1, Pallas kernels, local(): pl.pallas_call(far_kernel, grid=(steps,), in_specs=[pl.BlockSpec((block,...  97.7 us
    pallas_call x1, Pallas kernels, local(): pl.pallas_call(near_kernel, grid=(steps,), in_specs=[SMEM, SMEM, pl.Block...  53.6 us
    pallas_call x1, Pallas kernels, local(): pl.pallas_call(translate_kernel, grid=(kinds // span,), in_specs=[SMEM, S...  36.8 us
    all_gather x1, blocking collectives, local(): group_parts = lax.all_gather(partial, 'leaf', axis=0)  20.4 us
    all_gather x1, blocking collectives, local(): every_parent = lax.all_gather(group_sum, 'oct', axis=0, tiled=True)  18.5 us
    ppermute x4, starting transfers between devices, local(): pieces.append(lax.ppermute(send[k], 'leaf', pairs))  9.86 us
    ppermute x4, waiting for transfers between devices, local(): pieces.append(lax.ppermute(send[k], 'leaf', pairs))  8.23 us
  transfers between devices with their start and end apart: 9, of which 4 were waited for; matrix products, arithmetic and copies ran while one was open for 3% of the time, Pallas kernels for 38%

profile of v1, /device:TPU:1, one launch (start us, length us, event | category | flops | bytes accessed | tf_op | source)
XLA Modules:
  0.0 386.8 jit_solution(6017372792377375595)
XLA Ops:
  0.0 0.0 copy-start.1
  0.0 0.0 copy-start.2
  0.0 0.8 fusion.11
  0.8 0.8 fusion.9
  1.7 0.8 select_bitcast_fusion.1
  2.5 1.3 collective-permute-start.8
  3.8 4.7 %collective-permute-start.7 = (f32[4,32,128]{2,1,0:T(8,128)S(1)}, f32[4,32,128]{2,1,0:T(8,128)S(1)}, u32[]{:S(2)}, u32[]{:S(2)}) collective-permute-start(f32[4,32,128]{2,1,0:T(8,128)S(1)} %pad_maximum_fusion.1), channel_id=1, source_target_pairs={{0,1},{1,2},{2,3},{3,4},{4,5},{5,6},{6,7},{7,8},{8,9},{9,10},{10,1... | collective-permute-start | bytes 196616 | tf_op jit(solution)/shard_map/ppermute | solution.py:360
  8.6 1.3 add_add_fusion
  9.8 1.3 dynamic-slice_reduce_fusion
  11.2 0.6 stack.3.slots_ref
  11.8 1.5 broadcast_in_dim.36.counts_ref
  13.3 108.8 %moments.1 = (bf16[512,32,128]{2,1,0:T(8,128)(2,1)}, bf16[512,32,128]{2,1,0:T(8,128)(2,1)}, f32[512,128]{1,0:T(8,128)}, bf16[8,32,256]{2,1,0:T(8,128)(2,1)}, bf16[64,256]{1,0:T(8,128)(2,1)}) custom-call(s32[8,32]{1,0:T(8,128)} %stack.3.slots_ref, f32[3,512,128]{2,1,0:T(8,128)} %bitcast.42, f32[512,128]{1,0:T(8,128)} %dens_ref.3, ...), custom_call_target="tpu_custom_call" | custom-call | tf_op jit(solution)/shard_map/moments/pallas_call | solution.py:376
  122.2 0.8 slice_bitcast_fusion
  123.0 3.0 collective-permute-start.6
  126.0 1.7 collective-permute-start.5
  127.7 4.8 %collective-permute-start = (bf16[32,256]{1,0:T(8,128)(2,1)S(1)}, bf16[32,256]{1,0:T(8,128)(2,1)S(1)}, u32[]{:S(2)}, u32[]{:S(2)}) collective-permute-start(bf16[32,256]{1,0:T(8,128)(2,1)S(1)} %get-tuple-element.33), channel_id=1, source_target_pairs={{0,2},{1,3},{2,4},{3,5},{4,6},{5,7},{6,8},{7,9},{8,10},{9,11},{10,... | collective-permute-start | bytes 49160 | tf_op jit(solution)/shard_map/ppermute | solution.py:425
  132.5 1.3 add_bitcast_fusion.index_ref
  133.8 1.3 add_bitcast_fusion.1.coarse_to_ref
  135.1 20.4 %all-gather = bf16[1024,256]{1,0:T(8,128)(2,1)S(1)} all-gather(bf16[64,256]{1,0:T(8,128)(2,1)} %get-tuple-element.11), channel_id=2, replica_groups=mesh['oct'=8,'leaf'=16] {'leaf'}, dimensions={0}, use_global_device_ids=true | all-gather | bytes 557056 | tf_op jit(solution)/shard_map/all_gather | solution.py:431
  155.5 0.1 reduce_sum.12
  155.6 18.5 %all_gather.11.parents_ref = bf16[512,256]{1,0:T(8,128)(2,1)} all-gather(bf16[64,256]{1,0:T(8,128)(2,1)S(1)} %reduce_sum.12), channel_id=1, replica_groups=mesh['oct'=8,'leaf'=16] {'oct'}, dimensions={0}, use_global_device_ids=true | all-gather | bytes 294912 | tf_op jit(solution)/shard_map/all_gather | solution.py:433
  174.1 0.0 copy-done.1
  174.1 0.0 copy-done.2
  174.1 0.1 fusion.6
  174.2 0.6 pad_add_fusion.far_ref
  174.8 0.0 collective-permute-done
  174.9 2.5 collective-permute-start.1
  177.4 0.8 collective-permute-done.1
  178.2 1.3 collective-permute-start.2
  179.5 0.7 constant_dynamic-update-slice_fusion.5
  180.2 2.7 collective-permute-done.2
  182.9 1.3 collective-permute-start.3
  184.2 4.7 %collective-permute-done.3 = bf16[32,256]{1,0:T(8,128)(2,1)S(1)} collective-permute-done((bf16[32,256]{1,0:T(8,128)(2,1)S(1)}, bf16[32,256]{1,0:T(8,128)(2,1)S(1)}, u32[]{:S(2)}, u32[]{:S(2)}) %collective-permute-start.3) | collective-permute-done | bytes 16416 | tf_op jit(solution)/shard_map/ppermute | solution.py:425
  188.9 3.3 collective-permute-start.4
  192.3 0.8 collective-permute-done.4
  193.1 0.0 collective-permute-done.5
  193.1 0.0 collective-permute-done.6
  193.1 0.0 copy-start
  193.1 0.6 copy-done
  193.8 36.8 %translate.1.exp_ref = bf16[512,256]{1,0:T(8,128)(2,1)} custom-call(s32[28,512]{1,0:T(8,128)} %pad_add_fusion.far_ref, s32[16,64]{1,0:T(8,128)} %bitcast.43, s32[16,64]{1,0:T(8,128)} %add_bitcast_fusion.1.coarse_to_ref, bf16[256,256]{1,0:T(8,128)(2,1)} %copy-done, bf16[512,256]{1,0:T(8,128)(2,1)} %all_gather.11.parents_ref, bf16[64,256,256]{2,1,0:T(8,128)(2,1)} %m2l_ref.1, ...), custom_call_target="tpu_custom_call" | custom-call | tf_op jit(solution)/shard_map/translate/pallas_call | solution.py:473
  230.6 0.0 collective-permute-done.8
  230.6 0.0 collective-permute-done.7
  230.6 0.7 pad_maximum_fusion.raw_ref
  231.3 2.4 halo.1
  233.7 1.9 fusion.10
  235.6 53.6 %near.1.near_ref = f32[512,128]{1,0:T(8,128)} custom-call(s32[4,512]{1,0:T(4,128)} %add_bitcast_fusion.index_ref, s32[4,512]{1,0:T(4,128)} %bitcast.44, bf16[512,32,128]{2,1,0:T(8,128)(2,1)} %get-tuple-element.9.target_ref, bf16[32,32,128]{2,1,0:T(8,128)(2,1)} %get-tuple-element.24.before_ref, bf16[512,32,128]{2,1,0:T(8,128)(2,1)} %get-tuple-element.12.source_ref, ...), custom_call_target="tpu_custom_call" | custom-call | tf_op jit(solution)/shard_map/near/pallas_call | solution.py:436
  289.2 97.7 %far.1 = f32[512,128]{1,0:T(8,128)} custom-call(bf16[512,32,128]{2,1,0:T(8,128)(2,1)} %get-tuple-element.9.target_ref, bf16[256,32]{1,0:T(8,128)(2,1)} %constant.132.clone.checks_ref, bf16[512,256]{1,0:T(8,128)(2,1)} %translate.1.exp_ref, f32[512,128]{1,0:T(8,128)} %near.1.near_ref, f32[512,128]{1,0:T(8,128)} %dens_ref.3, s32[512,128]{1,0:T(8,128)} %broadcast_in_dim.36.counts_ref), custom_call_target="tpu_custom_call" | custom-call | tf_op jit(solution)/shard_map/far/pallas_call | solution.py:498
  (9 shorter events, 0.0 us)
Async XLA Ops:
  0.0 174.1 %copy-start.1 = (s32[512,27]{0,1:T(8,128)S(1)}, s32[512,27]{0,1:T(8,128)}, u32[]{:S(2)}) copy-start(s32[512,27]{0,1:T(8,128)} %param.26) | copy-start | bytes 165892
  0.0 174.1 %copy-start.2 = (s32[512,27]{0,1:T(8,128)S(1)}, s32[512,27]{0,1:T(8,128)}, u32[]{:S(2)}) copy-start(s32[512,27]{0,1:T(8,128)} %param.25) | copy-start | bytes 165892
  2.5 228.1 %collective-permute-start.8 = (f32[4,32,128]{2,1,0:T(8,128)S(1)}, f32[4,32,128]{2,1,0:T(8,128)S(1)}, u32[]{:S(2)}, u32[]{:S(2)}) collective-permute-start(f32[4,32,128]{2,1,0:T(8,128)S(1)} %pad_maximum_fusion.2), channel_id=1, source_target_pairs={{1,0},{2,1},{3,2},{4,3},{5,4},{6,5},{7,6},{8,7},{9,8},{10,9},{11,1... | collective-permute-start | bytes 196616 | tf_op jit(solution)/shard_map/ppermute | solution.py:361
  3.8 226.8 %collective-permute-start.7 = (f32[4,32,128]{2,1,0:T(8,128)S(1)}, f32[4,32,128]{2,1,0:T(8,128)S(1)}, u32[]{:S(2)}, u32[]{:S(2)}) collective-permute-start(f32[4,32,128]{2,1,0:T(8,128)S(1)} %pad_maximum_fusion.1), channel_id=1, source_target_pairs={{0,1},{1,2},{2,3},{3,4},{4,5},{5,6},{6,7},{7,8},{8,9},{9,10},{10,1... | collective-permute-start | bytes 196616 | tf_op jit(solution)/shard_map/ppermute | solution.py:360
  123.0 70.1 %collective-permute-start.6 = (bf16[32,256]{1,0:T(8,128)(2,1)S(1)}, bf16[32,256]{1,0:T(8,128)(2,1)S(1)}, u32[]{:S(2)}, u32[]{:S(2)}) collective-permute-start(bf16[32,256]{1,0:T(8,128)(2,1)S(1)} %get-tuple-element.27), channel_id=1, source_target_pairs={{0,64},{16,80},{32,96},{48,112},{64,0},{80,16},{96,32},{112,48},{1... | collective-permute-start | bytes 49160 | tf_op jit(solution)/shard_map/ppermute | solution.py:428
  126.0 67.1 %collective-permute-start.5 = (bf16[32,256]{1,0:T(8,128)(2,1)S(1)}, bf16[32,256]{1,0:T(8,128)(2,1)S(1)}, u32[]{:S(2)}, u32[]{:S(2)}) collective-permute-start(bf16[32,256]{1,0:T(8,128)(2,1)S(1)} %get-tuple-element.28), channel_id=1, source_target_pairs={{0,16},{16,32},{32,48},{48,64},{64,80},{80,96},{96,112},{112,0},{1... | collective-permute-start | bytes 49160 | tf_op jit(solution)/shard_map/ppermute | solution.py:428
  127.7 47.1 %collective-permute-start = (bf16[32,256]{1,0:T(8,128)(2,1)S(1)}, bf16[32,256]{1,0:T(8,128)(2,1)S(1)}, u32[]{:S(2)}, u32[]{:S(2)}) collective-permute-start(bf16[32,256]{1,0:T(8,128)(2,1)S(1)} %get-tuple-element.33), channel_id=1, source_target_pairs={{0,2},{1,3},{2,4},{3,5},{4,6},{5,7},{6,8},{7,9},{8,10},{9,11},{10,... | collective-permute-start | bytes 49160 | tf_op jit(solution)/shard_map/ppermute | solution.py:425
  174.9 3.4 collective-permute-start.1
  178.2 4.7 %collective-permute-start.2 = (bf16[32,256]{1,0:T(8,128)(2,1)S(1)}, bf16[32,256]{1,0:T(8,128)(2,1)S(1)}, u32[]{:S(2)}, u32[]{:S(2)}) collective-permute-start(bf16[32,256]{1,0:T(8,128)(2,1)S(1)} %get-tuple-element.31), channel_id=1, source_target_pairs={{1,0},{2,1},{3,2},{4,3},{5,4},{6,5},{7,6},{8,7},{9,8},{10,9},{11,1... | collective-permute-start | bytes 49160 | tf_op jit(solution)/shard_map/ppermute | solution.py:425
  182.9 6.0 %collective-permute-start.3 = (bf16[32,256]{1,0:T(8,128)(2,1)S(1)}, bf16[32,256]{1,0:T(8,128)(2,1)S(1)}, u32[]{:S(2)}, u32[]{:S(2)}) collective-permute-start(bf16[32,256]{1,0:T(8,128)(2,1)S(1)} %get-tuple-element.30), channel_id=1, source_target_pairs={{2,0},{3,1},{4,2},{5,3},{6,4},{7,5},{8,6},{9,7},{10,8},{11,9},{12,... | collective-permute-start | bytes 49160 | tf_op jit(solution)/shard_map/ppermute | solution.py:425
  188.9 4.2 %collective-permute-start.4 = (bf16[32,256]{1,0:T(8,128)(2,1)S(1)}, bf16[32,256]{1,0:T(8,128)(2,1)S(1)}, u32[]{:S(2)}, u32[]{:S(2)}) collective-permute-start(bf16[32,256]{1,0:T(8,128)(2,1)S(1)} %get-tuple-element.29), channel_id=1, source_target_pairs={{0,112},{16,0},{32,16},{48,32},{64,48},{80,64},{96,80},{112,96},{1... | collective-permute-start | bytes 49160 | tf_op jit(solution)/shard_map/ppermute | solution.py:428
  193.1 0.7 copy-start

commit v2 on v1

--- a/solution.py
+++ b/solution.py
@@ -116,8 +116,9 @@
 
 def moments_kernel(
     slots_ref, pos_ref, dens_ref, counts_ref, code_ref, checks_ref, m2m_ref,
-    target_ref, source_ref, weight_ref, send_ref, part_ref, moments_low, moments_high, scratch, spare,
+    target_ref, source_ref, tile_ref, part_ref, *rest,
 ):
+    send_refs, (weights, moments_low, moments_high, scratch, spare) = rest[:8], rest[8:]
     step = pl.program_id(0)
     leaves = pos_ref.shape[1]
     total = moments_low.shape[0]
@@ -127,7 +128,7 @@
     def build(group, carry):
         at = pl.ds(pl.multiple_of(group * 8, 8), 8)
         masked = jnp.where(lane < counts_ref[at, :], dens_ref[at, :], 0.0)
-        weight_ref[at, :] = masked
+        weights[at, :] = masked
         target, source = panel_rows([pos_ref[d, at, :] for d in range(3)], masked)
 
         def put_target(u, value):
@@ -141,19 +142,37 @@
         return carry
 
     lax.fori_loop(0, leaves // 8, build, 0)
-    unroll = 16
+    row = lax.broadcasted_iota(jnp.int32, (16, 128), 0)
+
+    def squares(leaf):
+        return dot(checks, jnp.concatenate([target_ref[leaf + u] for u in range(4)], axis=1))
+
+    def finish(first, part, kernel, sums):
+        tile_ref[:, pl.ds(pl.multiple_of((first + part * 4) * 128, 512), 512)] = kernel
+        block = part // 4
+        value = weights[pl.ds(pl.multiple_of(first + block * 16, 16), 16), :]
+        spread = [jnp.where(row == part % 4 * 4 + u, value, 0.0) for u in range(4)]
+        out = dot(jnp.concatenate(spread, axis=1).astype(BF), kernel, ((1,), (1,)))
+        sums[block] = out if part % 4 == 0 else sums[block] + out
+        if part % 4 == 3:
+            low = (sums[block] * (1.0 / math.sqrt(128))).astype(BF).astype(F32)
+            at = pl.ds(pl.multiple_of(step * leaves + first + block * 16, 16), 16)
+            moments_low[at, :], moments_high[at, :] = low[:, :128], low[:, 128:]
 
     def expand(group, carry):
-        for u in range(unroll):
-            leaf = group * unroll + u
-            kernel = green(dot(target_ref[leaf], checks, ((0,), (0,))))
-            out = dot(source_ref[leaf][16:32], kernel)[15:16]
-            low = (out * (1.0 / math.sqrt(128))).astype(BF).astype(F32)
-            at = pl.ds(step * leaves + leaf, 1)
-            moments_low[at, :], moments_high[at, :] = low[:, :128], low[:, 128:]
+        first = group * span
+        ahead, kernels, sums = {}, {}, {}
+        for s in range(span // 4 + 2):
+            if s < span // 4:
+                ahead[s] = squares(first + s * 4)
+            if 0 <= s - 1 < span // 4:
+                kernels[s - 1] = green(ahead.pop(s - 1))
+            if 0 <= s - 2:
+                finish(first, s - 2, kernels.pop(s - 2), sums)
         return carry
 
-    lax.fori_loop(0, leaves // unroll, expand, 0)
+    span = 64
+    lax.fori_loop(0, leaves // span, expand, 0)
 
     @pl.when(step == pl.num_programs(0) - 1)
     def _():
@@ -166,7 +185,7 @@
                 return carry
 
             lax.fori_loop(0, 32, pick, 0, unroll=8)
-            send_ref[partner] = jnp.concatenate(
+            send_refs[partner][...] = jnp.concatenate(
                 [spare[0:32, :], scratch[0:32, :]], axis=1
             ).astype(BF)
         low = jnp.concatenate([moments_low[...], moments_high[...]], axis=1).astype(BF)
@@ -194,43 +213,48 @@
     lax.fori_loop(0, raw_ref.shape[1] // 8, build, 0)
 
 
-def near_kernel(
-    index_ref, dir_ref, target_ref, before_ref, source_ref, after_ref, scale_ref, add_ref,
-    out_ref, window, sems,
-):
-    step = pl.program_id(0)
+def near_kernel(begin, index_ref, dir_ref, target_ref, *refs):
+    *parts, scale_ref, add_ref, out_ref, window, sems = refs
     leaves = target_ref.shape[0]
-    total = source_ref.shape[0]
-
-    @pl.when(step == 0)
-    def _():
-        copies = [
-            pltpu.make_async_copy(before_ref, window.at[0:HW], sems.at[0]),
-            pltpu.make_async_copy(source_ref, window.at[HW : HW + total], sems.at[1]),
-            pltpu.make_async_copy(after_ref, window.at[HW + total : 2 * HW + total], sems.at[2]),
-        ]
-        for copy in copies:
-            copy.start()
-        for copy in copies:
-            copy.wait()
-
-    unroll = 16
-
-    def one(leaf):
-        whole = step * leaves + leaf
+    copies, at = [], 0
+    for k, part in enumerate(parts):
+        size = part.shape[0]
+        if size == HW:
+            source = part
+        else:
+            low = max(begin - HW, 0)
+            size = min(begin + leaves + HW, size) - low
+            source = part.at[low : low + size]
+        copies.append(pltpu.make_async_copy(source, window.at[at : at + size], sems.at[k]))
+        at += size
+    for copy in copies:
+        copy.start()
+    for copy in copies:
+        copy.wait()
+
+    def squares(leaf):
+        whole = begin + leaf
         rows, weights = [], []
         for j in range(4):
             base = window[index_ref[j, whole]]
             way = dir_ref[j, whole]
             rows.append(base * scale_ref[way] + add_ref[way])
             weights.append(base[16:32])
-        kernel = green(dot(target_ref[leaf], jnp.concatenate(rows, 1), ((0,), (0,))))
-        return dot(jnp.concatenate(weights, 1), kernel, ((1,), (1,)))[15:16]
+        value = dot(target_ref[leaf], jnp.concatenate(rows, 1), ((0,), (0,)))
+        return value, jnp.concatenate(weights, 1)
+
+    unroll, depth = 32, 2
 
     def body(group, carry):
-        for u in range(unroll):
-            leaf = group * unroll + u
-            out_ref[pl.ds(leaf, 1), :] = one(leaf) * (1.0 / math.sqrt(512))
+        first = group * unroll
+        ahead = []
+        for u in range(unroll + depth):
+            if u < unroll:
+                ahead.append(squares(first + u))
+            if u >= depth:
+                value, weights = ahead[u - depth]
+                out = dot(weights, green(value), ((1,), (1,)))[15:16]
+                out_ref[pl.ds(first + u - depth, 1), :] = out * (1.0 / math.sqrt(512))
         return carry
 
     lax.fori_loop(0, leaves // unroll, body, 0)
@@ -306,25 +330,26 @@
         out_ref[:, 128:] = rows_high[...].astype(BF)
 
 
-def far_kernel(target_ref, checks_ref, exp_ref, near_ref, dens_ref, counts_ref, out_ref):
-    leaves = target_ref.shape[0]
+def far_kernel(tile_ref, exp_ref, dens_ref, counts_ref, *refs):
+    near_refs, out_ref = refs[:-1], refs[-1]
+    step = pl.program_id(0)
+    leaves = out_ref.shape[0]
     unroll = 16
     lane = lax.broadcasted_iota(jnp.int32, (unroll, 128), 1)
-    checks = checks_ref[...]
-
-    def body(group, carry):
-        at = pl.ds(pl.multiple_of(group * unroll, unroll), unroll)
-        local = exp_ref[at, :]
-        outs = []
+    row = lax.broadcasted_iota(jnp.int32, (unroll, 128), 0)
+    per = pl.num_programs(0) // len(near_refs)
+    for group in range(leaves // unroll):
+        at = pl.ds(group * unroll, unroll)
+        out = dot(exp_ref[at, :], tile_ref[:, group * unroll * 128 : (group + 1) * unroll * 128])
+        far = jnp.zeros((unroll, 128), F32)
         for u in range(unroll):
-            kernel = green(dot(checks, target_ref[group * unroll + u]))
-            outs.append(dot(local, kernel)[u : u + 1])
-        far = jnp.concatenate(outs, 0) * (1.0 / math.sqrt(256))
-        value = 0.5 * dens_ref[at, :] + near_ref[at, :] + far
+            far = jnp.where(row == u, out[:, u * 128 : (u + 1) * 128], far)
+        near = near_refs[0][pl.ds(pl.multiple_of(step % per * leaves + group * unroll, 16), 16), :]
+        for k in range(1, len(near_refs)):
+            other = near_refs[k][pl.ds(pl.multiple_of(step % per * leaves + group * unroll, 16), 16), :]
+            near = jnp.where(step // per == k, other, near)
+        value = 0.5 * dens_ref[at, :] + near + far * (1.0 / math.sqrt(256))
         out_ref[at, :] = jnp.where(lane < counts_ref[at, :], value, 0.0)
-        return carry
-
-    lax.fori_loop(0, leaves // unroll, body, 0)
 
 
 def params(mib=56):
@@ -373,7 +398,8 @@
 
     steps = 8
     block = leaves // steps
-    target, source, weights, send, partial = pl.pallas_call(
+    chunk = leaves // 4
+    target, source, tile, partial, *send = pl.pallas_call(
         moments_kernel,
         grid=(steps,),
         in_specs=[
@@ -386,17 +412,18 @@
         out_specs=[
             pl.BlockSpec((block, ROWS, panels), lambda i: (i, 0, 0)),
             pl.BlockSpec((block, ROWS, panels), lambda i: (i, 0, 0)),
-            pl.BlockSpec((block, panels), lambda i: (i, 0)),
-            VMEM, VMEM,
-        ],
+            pl.BlockSpec((width, block * panels), lambda i: (0, i)),
+        ]
+        + [VMEM] * 9,
         out_shape=[
             jax.ShapeDtypeStruct((leaves, ROWS, panels), BF),
             jax.ShapeDtypeStruct((leaves, ROWS, panels), BF),
-            jax.ShapeDtypeStruct((leaves, panels), F32),
-            jax.ShapeDtypeStruct((8, cap, width), BF),
+            jax.ShapeDtypeStruct((width, leaves * panels), BF),
             jax.ShapeDtypeStruct((cells, width), BF),
-        ],
+        ]
+        + [jax.ShapeDtypeStruct((cap, width), BF)] * 8,
         scratch_shapes=[
+            pltpu.VMEM((block, 128), F32),
             pltpu.VMEM((leaves, 128), F32),
             pltpu.VMEM((leaves, 128), F32),
             pltpu.VMEM((8 * ROWS, panels), F32),
@@ -404,7 +431,7 @@
         ],
         compiler_params=params(),
         name="moments",
-    )(slots, planes, density, spread_counts, code, checks, m2m)
+    )(slots, planes, density, spread_counts, code, checks.T, m2m)
 
     halo = pl.pallas_call(
         halo_kernel,
@@ -428,31 +455,68 @@
             pieces.append(lax.ppermute(send[k], "oct", pairs))
     received = jnp.concatenate(pieces, axis=0)
 
-    group_parts = lax.all_gather(partial, "leaf", axis=0)
-    group_sum = jnp.sum(group_parts.astype(F32), axis=0).astype(BF)
-    every_parent = lax.all_gather(group_sum, "oct", axis=0, tiled=True)
-
-    index = (jnp.arange(leaves, dtype=jnp.int32)[:, None] + near_offset + HW).T
-    near = pl.pallas_call(
-        near_kernel,
-        grid=(steps,),
-        in_specs=[
-            SMEM, SMEM,
-            pl.BlockSpec((block, ROWS, panels), lambda i: (i, 0, 0)),
-            pl.BlockSpec(memory_space=pl.ANY),
-            pl.BlockSpec(memory_space=pl.ANY),
-            pl.BlockSpec(memory_space=pl.ANY),
-            VMEM, VMEM,
-        ],
-        out_specs=pl.BlockSpec((block, panels), lambda i: (i, 0)),
-        out_shape=jax.ShapeDtypeStruct((leaves, panels), F32),
-        scratch_shapes=[
-            pltpu.VMEM((leaves + 2 * HW, ROWS, panels), BF),
-            pltpu.SemaphoreType.DMA((3,)),
-        ],
-        compiler_params=params(),
-        name="near",
-    )(index, near_dir.T, target, halo[:HW], source, halo[HW:], scale, add)
+    index = (jnp.arange(leaves, dtype=jnp.int32)[:, None] % chunk + near_offset + HW).T
+    ways = near_dir.T
+
+    def near_part(begin):
+        if begin == 0:
+            parts = [halo[:HW], source]
+        elif begin + chunk == leaves:
+            parts = [source, halo[HW:]]
+        else:
+            parts = [source]
+        return pl.pallas_call(
+            functools.partial(near_kernel, begin),
+            grid=(1,),
+            in_specs=[
+                SMEM, SMEM,
+                pl.BlockSpec((chunk, ROWS, panels), lambda i: (begin // chunk, 0, 0)),
+            ]
+            + [pl.BlockSpec(memory_space=pl.ANY)] * len(parts)
+            + [VMEM, VMEM],
+            out_specs=VMEM,
+            out_shape=jax.ShapeDtypeStruct((chunk, panels), F32),
+            scratch_shapes=[
+                pltpu.VMEM((chunk + 2 * HW, ROWS, panels), BF),
+                pltpu.SemaphoreType.DMA((2,)),
+            ],
+            compiler_params=params(),
+            cost_estimate=pl.CostEstimate(
+                flops=10**10, bytes_accessed=10**6, transcendentals=chunk * 2 * 65536
+            ),
+            name="near",
+        )(index, ways, target, *parts, scale, add)
+
+    inner = 4
+
+    def exchange(value, number, other):
+        got = [value.astype(F32)]
+        for by in range(1, number):
+            pairs = [(i, other(i, by)) for i in range(leaf_size)]
+            got.append(lax.ppermute(value, "leaf", pairs).astype(F32))
+        return got
+
+    near = []
+    fours = exchange(partial, inner, lambda i, by: i // inner * inner + (i + by) % inner)
+    near.append(near_part(0))
+    near[0], *fours = lax.optimization_barrier((near[0], *fours))
+    total = sum(fours[1:], fours[0]).astype(BF)
+    over = leaf_size // inner
+    sixteen = exchange(total, over, lambda i, by: (i + by * inner) % leaf_size)
+    sixteen[0], source, target = lax.optimization_barrier((sixteen[0], source, target))
+    near.append(near_part(chunk))
+    near[1], *sixteen = lax.optimization_barrier((near[1], *sixteen))
+    total = sum(sixteen[1:], sixteen[0]).astype(BF)
+    others = []
+    for by in range(1, oct_size):
+        pairs = [(i, (i + by) % oct_size) for i in range(oct_size)]
+        others.append(lax.ppermute(total, "oct", pairs))
+    total, source, target = lax.optimization_barrier((total, source, target))
+    for k in range(2, leaves // chunk):
+        near.append(near_part(k * chunk))
+    *near, received, total = lax.optimization_barrier((*near, received, total))
+    others = lax.optimization_barrier((near[-1], *others))[1:]
+    every_parent = jnp.concatenate([total, *others], axis=0)
 
     owner, slot = far_source // cap, far_source % cap
     owner_group, owner_place = owner // leaf_size, owner % leaf_size
@@ -468,6 +532,7 @@
     far_rows = (far_type * 8 + partner) * cap + slot
     own_row = kinds * 8 * cap + child_pos * cells + leaf_parent
     far_rows = jnp.concatenate([far_rows.T, own_row[None, :]], axis=0)
+    coarse_from = (group - coarse_source // cells) % oct_size * cells + coarse_source % cells
     coarse_to = (coarse_type * cells + jnp.arange(cells, dtype=jnp.int32)[:, None]).T
     span = 8
     expansions = pl.pallas_call(
@@ -493,24 +558,23 @@
         ],
         compiler_params=params(),
         name="translate",
-    )(far_rows, coarse_source.T, coarse_to, received, every_parent, m2l, l2l)
+    )(far_rows, coarse_from.T, coarse_to, received, every_parent, m2l, l2l)
 
     return pl.pallas_call(
         far_kernel,
         grid=(steps,),
         in_specs=[
-            pl.BlockSpec((block, ROWS, panels), lambda i: (i, 0, 0)),
-            VMEM,
+            pl.BlockSpec((width, block * panels), lambda i: (0, i)),
             pl.BlockSpec((block, width), lambda i: (i, 0)),
             pl.BlockSpec((block, panels), lambda i: (i, 0)),
             pl.BlockSpec((block, panels), lambda i: (i, 0)),
-            pl.BlockSpec((block, panels), lambda i: (i, 0)),
-        ],
+        ]
+        + [VMEM] * len(near),
         out_specs=pl.BlockSpec((block, panels), lambda i: (i, 0)),
         out_shape=jax.ShapeDtypeStruct((leaves, panels), F32),
         compiler_params=params(),
         name="far",
-    )(target, checks.T, expansions, near, density, spread_counts)
+    )(tile, expansions, density, spread_counts, *near)
 
 
 def solution(mesh):

time: 390 us -> 234 us (0.60)
  Pallas kernels: 299 us -> 145 us
  blocking collectives: 38.9 us -> 0 us
  starting transfers between devices: 23.8 us -> 50.6 us
  waiting for transfers between devices: 9.08 us -> 20.7 us
    pallas_call x2 -> x5, Pallas kernels: 151 us -> 68.1 us  [the longest x4 53.8 us: near_part(): pl.pallas_call(functools.partial(near_kernel, begin), grid=(1,), in_specs...]
    pallas_call x1, Pallas kernels: 109 us -> 37.8 us  [local(): pl.pallas_call(moments_kernel, grid=(steps,), in_specs=[SMEM, pl.BlockSpe...]
    all_gather x2 -> x0, blocking collectives: 38.9 us -> none  [the longest x1 20.4 us: local(): group_parts = lax.all_gather(partial, 'leaf', axis=0)]
    ppermute x0 -> x13, starting transfers between devices: none -> 27.4 us  [the longest x6 15.3 us: exchange(): got.append(lax.ppermute(value, 'leaf', pairs).astype(F32))]
    ppermute x3, waiting for transfers between devices: 0.84 us -> 5.96 us  [local(): pieces.append(lax.ppermute(send[k], 'oct', pairs))]
  transfers between devices with their start and end apart: 9 -> 22, of which waited for: 4 -> 8; matrix products, arithmetic and copies ran while one was open for 3% -> 4% of each run, Pallas kernels for 38% -> 17%
where the time goes in v2:
time: 234 us; the launch traced here: 233 us
  Pallas kernels  145 us (62%)
  starting transfers between devices  50.6 us (22%)
  waiting for transfers between devices  20.7 us (9%)
  local copies, waits for them, and re-layouts  8.44 us (4%)
  other arithmetic  7.9 us (3%)
    pallas_call x4, Pallas kernels, near_part(): pl.pallas_call(functools.partial(near_kernel, begin), grid=(1,), in_specs...  53.8 us
    pallas_call x1, Pallas kernels, local(): pl.pallas_call(moments_kernel, grid=(steps,), in_specs=[SMEM, pl.BlockSpe...  37.8 us
    pallas_call x1, Pallas kernels, local(): pl.pallas_call(translate_kernel, grid=(kinds // span,), in_specs=[SMEM, S...  36.8 us
    ppermute x6, starting transfers between devices, exchange(): got.append(lax.ppermute(value, 'leaf', pairs).astype(F32))  15.3 us
    pallas_call x1, Pallas kernels, local(): pl.pallas_call(far_kernel, grid=(steps,), in_specs=[pl.BlockSpec((width,...  14.3 us
    ppermute x7, starting transfers between devices, local(): others.append(lax.ppermute(total, 'oct', pairs))  12.1 us
    ppermute x4, waiting for transfers between devices, local(): pieces.append(lax.ppermute(send[k], 'leaf', pairs))  10.4 us
    ppermute x4, starting transfers between devices, local(): pieces.append(lax.ppermute(send[k], 'leaf', pairs))  9.77 us
  transfers between devices with their start and end apart: 22, of which 8 were waited for; matrix products, arithmetic and copies ran while one was open for 4% of the time, Pallas kernels for 17%

profile of v2, /device:TPU:1, one launch (start us, length us, event | category | flops | bytes accessed | tf_op | source)
XLA Modules:
  0.0 233.1 jit_solution(9439296152635345617)
XLA Ops:
  0.0 1.3 add_add_fusion
  1.3 1.3 dynamic-slice_reduce_fusion
  3.2 1.5 broadcast_in_dim.36.counts_ref
  4.8 37.8 %moments.1 = (bf16[512,32,128]{2,1,0:T(8,128)(2,1)}, bf16[512,32,128]{2,1,0:T(8,128)(2,1)}, bf16[256,65536]{1,0:T(8,128)(2,1)}, bf16[64,256]{1,0:T(8,128)(2,1)},...) custom-call(s32[8,32]{1,0:T(8,128)} %stack.3.slots_ref, ...), custom_call_target="tpu_custom_call" | custom-call | tf_op jit(solution)/shard_map/moments/pallas_call | solution.py:402
  42.6 3.6 %collective-permute-start.4 = (bf16[64,256]{1,0:T(8,128)(2,1)}, bf16[64,256]{1,0:T(8,128)(2,1)S(1)}, u32[]{:S(2)}, u32[]{:S(2)}) collective-permute-start(bf16[64,256]{1,0:T(8,128)(2,1)} %get-tuple-element.49), channel_id=1, source_target_pairs={{0,3},{1,0},{2,1},{3,2},{4,7},{5,4},{6,5},{7,6},{8,11},{9,8},{10,9... | collective-permute-start | bytes 98312 | tf_op jit(solution)/shard_map/ppermute | solution.py:496
  46.5 0.7 collective-permute-start.2
  47.2 0.8 fusion.21
  48.0 0.8 fusion.19
  48.9 0.8 select_bitcast_fusion.1
  49.7 1.3 collective-permute-start.1
  51.0 5.9 %collective-permute-start.8 = (bf16[32,256]{1,0:T(8,128)(2,1)}, bf16[32,256]{1,0:T(8,128)(2,1)S(1)}, u32[]{:S(2)}, u32[]{:S(2)}) collective-permute-start(bf16[32,256]{1,0:T(8,128)(2,1)} %get-tuple-element.65), channel_id=1, source_target_pairs={{0,2},{1,3},{2,4},{3,5},{4,6},{5,7},{6,8},{7,9},{8,10},{9,11},{10,... | collective-permute-start | bytes 49160 | tf_op jit(solution)/shard_map/ppermute | solution.py:452
  56.9 1.3 add_bitcast_fusion.index_ref
  58.2 1.3 fusion.13
  59.6 1.0 fusion.6
  61.2 0.8 convert_element_type.30
  62.0 1.3 collective-permute-start.9
  63.3 1.1 collective-permute-done.9
  64.4 1.3 collective-permute-start.10
  65.7 0.7 constant_dynamic-update-slice_fusion.5
  66.4 4.0 %collective-permute-done.10 = bf16[32,256]{1,0:T(8,128)(2,1)S(1)} collective-permute-done((bf16[32,256]{1,0:T(8,128)(2,1)}, bf16[32,256]{1,0:T(8,128)(2,1)S(1)}, u32[]{:S(2)}, u32[]{:S(2)}) %collective-permute-start.10) | collective-permute-done | bytes 16416 | tf_op jit(solution)/shard_map/ppermute | solution.py:452
  70.3 1.3 collective-permute-start.11
  71.6 5.4 %collective-permute-done.11 = bf16[32,256]{1,0:T(8,128)(2,1)S(1)} collective-permute-done((bf16[32,256]{1,0:T(8,128)(2,1)}, bf16[32,256]{1,0:T(8,128)(2,1)S(1)}, u32[]{:S(2)}, u32[]{:S(2)}) %collective-permute-start.11) | collective-permute-done | bytes 16416 | tf_op jit(solution)/shard_map/ppermute | solution.py:452
  77.1 5.2 %collective-permute-start.12 = (bf16[32,256]{1,0:T(8,128)(2,1)}, bf16[32,256]{1,0:T(8,128)(2,1)S(1)}, u32[]{:S(2)}, u32[]{:S(2)}) collective-permute-start(bf16[32,256]{1,0:T(8,128)(2,1)} %get-tuple-element.70), channel_id=1, source_target_pairs={{0,112},{16,0},{32,16},{48,32},{64,48},{80,64},{96,80},{112,96},{1... | collective-permute-start | bytes 49160 | tf_op jit(solution)/shard_map/ppermute | solution.py:455
  82.3 2.7 %collective-permute-done.12 = bf16[32,256]{1,0:T(8,128)(2,1)S(1)} collective-permute-done((bf16[32,256]{1,0:T(8,128)(2,1)}, bf16[32,256]{1,0:T(8,128)(2,1)S(1)}, u32[]{:S(2)}, u32[]{:S(2)}) %collective-permute-start.12) | collective-permute-done | bytes 16416 | tf_op jit(solution)/shard_map/ppermute | solution.py:455
  85.1 1.4 collective-permute-done.13
  86.4 2.4 %collective-permute-start.14 = (bf16[32,256]{1,0:T(8,128)(2,1)}, bf16[32,256]{1,0:T(8,128)(2,1)S(1)}, u32[]{:S(2)}, u32[]{:S(2)}) collective-permute-start(bf16[32,256]{1,0:T(8,128)(2,1)} %get-tuple-element.72), channel_id=1, source_target_pairs={{0,64},{16,80},{32,96},{48,112},{64,0},{80,16},{96,32},{112,48},{1... | collective-permute-start | bytes 49160 | tf_op jit(solution)/shard_map/ppermute | solution.py:455
  88.9 1.9 collective-permute-done.14
  90.7 4.4 %collective-permute-start = (f32[4,32,128]{2,1,0:T(8,128)S(1)}, f32[4,32,128]{2,1,0:T(8,128)S(1)}, u32[]{:S(2)}, u32[]{:S(2)}) collective-permute-start(f32[4,32,128]{2,1,0:T(8,128)S(1)} %pad_maximum_fusion.1), channel_id=1, source_target_pairs={{0,1},{1,2},{2,3},{3,4},{4,5},{5,6},{6,7},{7,8},{8,9},{9,10},{10,1... | collective-permute-start | bytes 196616 | tf_op jit(solution)/shard_map/ppermute | solution.py:385
  95.3 1.2 collective-permute-done
  97.2 2.4 %halo.1 = bf16[64,32,128]{2,1,0:T(8,128)(2,1)} custom-call(f32[4,64,128]{2,1,0:T(8,128)} %pad_maximum_fusion.raw_ref), custom_call_target="tpu_custom_call" | custom-call | tf_op jit(solution)/shard_map/halo/pallas_call | solution.py:436
  99.6 1.8 fusion.20
  101.4 13.5 %near.4.refs_0_ = f32[128,128]{1,0:T(8,128)} custom-call(s32[4,512]{1,0:T(4,128)} %add_bitcast_fusion.index_ref, s32[4,512]{1,0:T(4,128)} %bitcast.36, bf16[512,32,128]{2,1,0:T(8,128)(2,1)} %get-tuple-element.63.target_ref, bf16[32,32,128]{2,1,0:T(8,128)(2,1)} %get-tuple-element.100.refs_0_, bf16[512,32,128]{2,1,0:T(8,128)(2,1)} %get-tuple-element.64.refs_1_.refs_0_, ...), custom_call_target="tpu_custom_call" | custom-call | flops 10000000000 | bytes 1000000 | tf_op jit(solution)/shard_map/near/pallas_call | solution.py:468
  114.9 7.9 %collective-permute-start.6 = (bf16[64,256]{1,0:T(8,128)(2,1)S(1)}, bf16[64,256]{1,0:T(8,128)(2,1)S(1)}, u32[]{:S(2)}, u32[]{:S(2)}) collective-permute-start(bf16[64,256]{1,0:T(8,128)(2,1)S(1)} %get-tuple-element.96), channel_id=1, source_target_pairs={{0,8},{1,9},{2,10},{3,11},{4,12},{5,13},{6,14},{7,15},{8,0},{9,1},... | collective-permute-start | bytes 98312 | tf_op jit(solution)/shard_map/ppermute | solution.py:496
  122.8 0.8 collective-permute-start.5
  123.6 1.9 collective-permute-start.7
  125.5 13.5 %near.5.refs_1_ = f32[128,128]{1,0:T(8,128)} custom-call(s32[4,512]{1,0:T(4,128)} %add_bitcast_fusion.index_ref, s32[4,512]{1,0:T(4,128)} %bitcast.37, bf16[512,32,128]{2,1,0:T(8,128)(2,1)} %get-tuple-element.63.target_ref, bf16[512,32,128]{2,1,0:T(8,128)(2,1)} %get-tuple-element.64.refs_1_.refs_0_, bf16[27,32,128]{2,1,0:T(8,128)(2,1)} %constant.167.clone.refs_2_.refs_1_, ...), custom_call_target="tpu_custom_call" | custom-call | flops 10000000000 | bytes 1000000 | tf_op jit(solution)/shard_map/near/pallas_call | solution.py:468
  139.1 5.3 %collective-permute-start.21 = (bf16[64,256]{1,0:T(8,128)(2,1)S(1)}, bf16[64,256]{1,0:T(8,128)(2,1)S(1)}, u32[]{:S(2)}, u32[]{:S(2)}) collective-permute-start(bf16[64,256]{1,0:T(8,128)(2,1)S(1)} %add_convert_fusion), channel_id=1, source_target_pairs={{0,112},{16,0},{32,16},{48,32},{64,48},{80,64},{96,80},{112,96},{1... | collective-permute-start | bytes 98312 | tf_op jit(solution)/shard_map/ppermute | solution.py:513
  144.3 1.3 collective-permute-start.20
  145.6 0.8 collective-permute-start.19
  146.4 1.4 collective-permute-start.18
  147.8 1.9 collective-permute-start.17
  149.7 13.5 %near.6.refs_2_ = f32[128,128]{1,0:T(8,128)} custom-call(s32[4,512]{1,0:T(4,128)} %add_bitcast_fusion.index_ref, s32[4,512]{1,0:T(4,128)} %bitcast.38, bf16[512,32,128]{2,1,0:T(8,128)(2,1)} %get-tuple-element.63.target_ref, bf16[512,32,128]{2,1,0:T(8,128)(2,1)} %get-tuple-element.64.refs_1_.refs_0_, bf16[27,32,128]{2,1,0:T(8,128)(2,1)} %constant.167.clone.refs_2_.refs_1_, ...), custom_call_target="tpu_custom_call" | custom-call | flops 10000000000 | bytes 1000000 | tf_op jit(solution)/shard_map/near/pallas_call | solution.py:468
  163.2 13.4 %near.7.refs_3_ = f32[128,128]{1,0:T(8,128)} custom-call(s32[4,512]{1,0:T(4,128)} %add_bitcast_fusion.index_ref, s32[4,512]{1,0:T(4,128)} %bitcast.39, bf16[512,32,128]{2,1,0:T(8,128)(2,1)} %get-tuple-element.63.target_ref, bf16[512,32,128]{2,1,0:T(8,128)(2,1)} %get-tuple-element.64.refs_1_.refs_0_, bf16[32,32,128]{2,1,0:T(8,128)(2,1)} %get-tuple-element.99.refs_1_, ...), custom_call_target="tpu_custom_call" | custom-call | flops 10000000000 | bytes 1000000 | tf_op jit(solution)/shard_map/near/pallas_call | solution.py:468
  177.3 0.9 collective-permute-start.15
  178.2 3.1 %collective-permute-done.16 = bf16[64,256]{1,0:T(8,128)(2,1)S(1)} collective-permute-done((bf16[64,256]{1,0:T(8,128)(2,1)S(1)}, bf16[64,256]{1,0:T(8,128)(2,1)S(1)}, u32[]{:S(2)}, u32[]{:S(2)}) %collective-permute-start.16) | collective-permute-done | bytes 32800 | tf_op jit(solution)/shard_map/ppermute | solution.py:513
  181.3 0.7 copy-done
  182.0 36.8 %translate.1.exp_ref = bf16[512,256]{1,0:T(8,128)(2,1)} custom-call(s32[28,512]{1,0:T(8,128)} %pad_add_fusion.far_ref, s32[16,64]{1,0:T(8,128)} %get-tuple-element.107.coarse_from_ref, s32[16,64]{1,0:T(8,128)} %get-tuple-element.108.coarse_to_ref, bf16[256,256]{1,0:T(8,128)(2,1)} %copy-done.1, bf16[512,256]{1,0:T(8,128)(2,1)} %copy-done, ...), custom_call_target="tpu_custom_call" | custom-call | tf_op jit(solution)/shard_map/translate/pallas_call | solution.py:538
  218.8 14.3 %far.1 = f32[512,128]{1,0:T(8,128)} custom-call(bf16[256,65536]{1,0:T(8,128)(2,1)} %get-tuple-element.46.tile_ref, bf16[512,256]{1,0:T(8,128)(2,1)} %translate.1.exp_ref, f32[512,128]{1,0:T(8,128)} %dens_ref.3, s32[512,128]{1,0:T(8,128)} %broadcast_in_dim.36.counts_ref, f32[128,128]{1,0:T(8,128)} %near.4.refs_0_, f32[128,128]{1,0:T(8,128)} %near.5.refs_1_, ...), custom_call_target="tpu_custom_call" | custom-call | tf_op jit(solution)/shard_map/far/pallas_call | solution.py:563
  (49 shorter events, 3.2 us)
Async XLA Ops:
  42.6 52.6 %collective-permute-start.4 = (bf16[64,256]{1,0:T(8,128)(2,1)}, bf16[64,256]{1,0:T(8,128)(2,1)S(1)}, u32[]{:S(2)}, u32[]{:S(2)}) collective-permute-start(bf16[64,256]{1,0:T(8,128)(2,1)} %get-tuple-element.49), channel_id=1, source_target_pairs={{0,3},{1,0},{2,1},{3,2},{4,7},{5,4},{6,5},{7,6},{8,11},{9,8},{10,9... | collective-permute-start | bytes 98312 | tf_op jit(solution)/shard_map/ppermute | solution.py:496
  46.2 49.1 %collective-permute-start.3 = (bf16[64,256]{1,0:T(8,128)(2,1)}, bf16[64,256]{1,0:T(8,128)(2,1)S(1)}, u32[]{:S(2)}, u32[]{:S(2)}) collective-permute-start(bf16[64,256]{1,0:T(8,128)(2,1)} %get-tuple-element.49), channel_id=1, source_target_pairs={{0,2},{1,3},{2,0},{3,1},{4,6},{5,7},{6,4},{7,5},{8,10},{9,11},{10,... | collective-permute-start | bytes 98312 | tf_op jit(solution)/shard_map/ppermute | solution.py:496
  46.5 48.7 %collective-permute-start.2 = (bf16[64,256]{1,0:T(8,128)(2,1)}, bf16[64,256]{1,0:T(8,128)(2,1)S(1)}, u32[]{:S(2)}, u32[]{:S(2)}) collective-permute-start(bf16[64,256]{1,0:T(8,128)(2,1)} %get-tuple-element.49), channel_id=1, source_target_pairs={{0,1},{1,2},{2,3},{3,0},{4,5},{5,6},{6,7},{7,4},{8,9},{9,10},{10,1... | collective-permute-start | bytes 98312 | tf_op jit(solution)/shard_map/ppermute | solution.py:496
  49.7 45.6 %collective-permute-start.1 = (f32[4,32,128]{2,1,0:T(8,128)S(1)}, f32[4,32,128]{2,1,0:T(8,128)S(1)}, u32[]{:S(2)}, u32[]{:S(2)}) collective-permute-start(f32[4,32,128]{2,1,0:T(8,128)S(1)} %pad_maximum_fusion.2), channel_id=1, source_target_pairs={{1,0},{2,1},{3,2},{4,3},{5,4},{6,5},{7,6},{8,7},{9,8},{10,9},{11,1... | collective-permute-start | bytes 196616 | tf_op jit(solution)/shard_map/ppermute | solution.py:386
  51.0 11.0 %collective-permute-start.8 = (bf16[32,256]{1,0:T(8,128)(2,1)}, bf16[32,256]{1,0:T(8,128)(2,1)S(1)}, u32[]{:S(2)}, u32[]{:S(2)}) collective-permute-start(bf16[32,256]{1,0:T(8,128)(2,1)} %get-tuple-element.65), channel_id=1, source_target_pairs={{0,2},{1,3},{2,4},{3,5},{4,6},{5,7},{6,8},{7,9},{8,10},{9,11},{10,... | collective-permute-start | bytes 49160 | tf_op jit(solution)/shard_map/ppermute | solution.py:452
  62.0 2.4 %collective-permute-start.9 = (bf16[32,256]{1,0:T(8,128)(2,1)}, bf16[32,256]{1,0:T(8,128)(2,1)S(1)}, u32[]{:S(2)}, u32[]{:S(2)}) collective-permute-start(bf16[32,256]{1,0:T(8,128)(2,1)} %get-tuple-element.66), channel_id=1, source_target_pairs={{0,1},{1,2},{2,3},{3,4},{4,5},{5,6},{6,7},{7,8},{8,9},{9,10},{10,1... | collective-permute-start | bytes 49160 | tf_op jit(solution)/shard_map/ppermute | solution.py:452
  64.4 6.0 %collective-permute-start.10 = (bf16[32,256]{1,0:T(8,128)(2,1)}, bf16[32,256]{1,0:T(8,128)(2,1)S(1)}, u32[]{:S(2)}, u32[]{:S(2)}) collective-permute-start(bf16[32,256]{1,0:T(8,128)(2,1)} %get-tuple-element.68), channel_id=1, source_target_pairs={{1,0},{2,1},{3,2},{4,3},{5,4},{6,5},{7,6},{8,7},{9,8},{10,9},{11,1... | collective-permute-start | bytes 49160 | tf_op jit(solution)/shard_map/ppermute | solution.py:452
  70.3 6.7 %collective-permute-start.11 = (bf16[32,256]{1,0:T(8,128)(2,1)}, bf16[32,256]{1,0:T(8,128)(2,1)S(1)}, u32[]{:S(2)}, u32[]{:S(2)}) collective-permute-start(bf16[32,256]{1,0:T(8,128)(2,1)} %get-tuple-element.69), channel_id=1, source_target_pairs={{2,0},{3,1},{4,2},{5,3},{6,4},{7,5},{8,6},{9,7},{10,8},{11,9},{12,... | collective-permute-start | bytes 49160 | tf_op jit(solution)/shard_map/ppermute | solution.py:452
  77.1 8.0 %collective-permute-start.12 = (bf16[32,256]{1,0:T(8,128)(2,1)}, bf16[32,256]{1,0:T(8,128)(2,1)S(1)}, u32[]{:S(2)}, u32[]{:S(2)}) collective-permute-start(bf16[32,256]{1,0:T(8,128)(2,1)} %get-tuple-element.70), channel_id=1, source_target_pairs={{0,112},{16,0},{32,16},{48,32},{64,48},{80,64},{96,80},{112,96},{1... | collective-permute-start | bytes 49160 | tf_op jit(solution)/shard_map/ppermute | solution.py:455
  85.0 1.4 collective-permute-start.13
  86.4 4.3 %collective-permute-start.14 = (bf16[32,256]{1,0:T(8,128)(2,1)}, bf16[32,256]{1,0:T(8,128)(2,1)S(1)}, u32[]{:S(2)}, u32[]{:S(2)}) collective-permute-start(bf16[32,256]{1,0:T(8,128)(2,1)} %get-tuple-element.72), channel_id=1, source_target_pairs={{0,64},{16,80},{32,96},{48,112},{64,0},{80,16},{96,32},{112,48},{1... | collective-permute-start | bytes 49160 | tf_op jit(solution)/shard_map/ppermute | solution.py:455
  90.7 5.7 %collective-permute-start = (f32[4,32,128]{2,1,0:T(8,128)S(1)}, f32[4,32,128]{2,1,0:T(8,128)S(1)}, u32[]{:S(2)}, u32[]{:S(2)}) collective-permute-start(f32[4,32,128]{2,1,0:T(8,128)S(1)} %pad_maximum_fusion.1), channel_id=1, source_target_pairs={{0,1},{1,2},{2,3},{3,4},{4,5},{5,6},{6,7},{7,8},{8,9},{9,10},{10,1... | collective-permute-start | bytes 196616 | tf_op jit(solution)/shard_map/ppermute | solution.py:385
  95.2 19.7 %copy-start.1 = (bf16[256,256]{1,0:T(8,128)(2,1)}, bf16[256,256]{1,0:T(8,128)(2,1)S(1)}, u32[]{:S(2)}) copy-start(bf16[256,256]{1,0:T(8,128)(2,1)S(1)} %constant_dynamic-update-slice_fusion.recv_ref) | copy-start | bytes 393220
  114.9 24.1 %collective-permute-start.6 = (bf16[64,256]{1,0:T(8,128)(2,1)S(1)}, bf16[64,256]{1,0:T(8,128)(2,1)S(1)}, u32[]{:S(2)}, u32[]{:S(2)}) collective-permute-start(bf16[64,256]{1,0:T(8,128)(2,1)S(1)} %get-tuple-element.96), channel_id=1, source_target_pairs={{0,8},{1,9},{2,10},{3,11},{4,12},{5,13},{6,14},{7,15},{8,0},{9,1},... | collective-permute-start | bytes 98312 | tf_op jit(solution)/shard_map/ppermute | solution.py:496
  122.8 16.2 %collective-permute-start.5 = (bf16[64,256]{1,0:T(8,128)(2,1)S(1)}, bf16[64,256]{1,0:T(8,128)(2,1)S(1)}, u32[]{:S(2)}, u32[]{:S(2)}) collective-permute-start(bf16[64,256]{1,0:T(8,128)(2,1)S(1)} %get-tuple-element.96), channel_id=1, source_target_pairs={{0,4},{1,5},{2,6},{3,7},{4,8},{5,9},{6,10},{7,11},{8,12},{9,13},{1... | collective-permute-start | bytes 98312 | tf_op jit(solution)/shard_map/ppermute | solution.py:496
  123.6 15.4 %collective-permute-start.7 = (bf16[64,256]{1,0:T(8,128)(2,1)S(1)}, bf16[64,256]{1,0:T(8,128)(2,1)S(1)}, u32[]{:S(2)}, u32[]{:S(2)}) collective-permute-start(bf16[64,256]{1,0:T(8,128)(2,1)S(1)} %get-tuple-element.96), channel_id=1, source_target_pairs={{0,12},{1,13},{2,14},{3,15},{4,0},{5,1},{6,2},{7,3},{8,4},{9,5},{1... | collective-permute-start | bytes 98312 | tf_op jit(solution)/shard_map/ppermute | solution.py:496
  139.1 37.5 %collective-permute-start.21 = (bf16[64,256]{1,0:T(8,128)(2,1)S(1)}, bf16[64,256]{1,0:T(8,128)(2,1)S(1)}, u32[]{:S(2)}, u32[]{:S(2)}) collective-permute-start(bf16[64,256]{1,0:T(8,128)(2,1)S(1)} %add_convert_fusion), channel_id=1, source_target_pairs={{0,112},{16,0},{32,16},{48,32},{64,48},{80,64},{96,80},{112,96},{1... | collective-permute-start | bytes 98312 | tf_op jit(solution)/shard_map/ppermute | solution.py:513
  144.3 32.9 %collective-permute-start.20 = (bf16[64,256]{1,0:T(8,128)(2,1)S(1)}, bf16[64,256]{1,0:T(8,128)(2,1)S(1)}, u32[]{:S(2)}, u32[]{:S(2)}) collective-permute-start(bf16[64,256]{1,0:T(8,128)(2,1)S(1)} %add_convert_fusion), channel_id=1, source_target_pairs={{0,96},{16,112},{32,0},{48,16},{64,32},{80,48},{96,64},{112,80},{1... | collective-permute-start | bytes 98312 | tf_op jit(solution)/shard_map/ppermute | solution.py:513
  145.6 32.5 %collective-permute-start.19 = (bf16[64,256]{1,0:T(8,128)(2,1)S(1)}, bf16[64,256]{1,0:T(8,128)(2,1)S(1)}, u32[]{:S(2)}, u32[]{:S(2)}) collective-permute-start(bf16[64,256]{1,0:T(8,128)(2,1)S(1)} %add_convert_fusion), channel_id=1, source_target_pairs={{0,80},{16,96},{32,112},{48,0},{64,16},{80,32},{96,48},{112,64},{1... | collective-permute-start | bytes 98312 | tf_op jit(solution)/shard_map/ppermute | solution.py:513
  146.4 31.7 %collective-permute-start.18 = (bf16[64,256]{1,0:T(8,128)(2,1)S(1)}, bf16[64,256]{1,0:T(8,128)(2,1)S(1)}, u32[]{:S(2)}, u32[]{:S(2)}) collective-permute-start(bf16[64,256]{1,0:T(8,128)(2,1)S(1)} %add_convert_fusion), channel_id=1, source_target_pairs={{0,64},{16,80},{32,96},{48,112},{64,0},{80,16},{96,32},{112,48},{1... | collective-permute-start | bytes 98312 | tf_op jit(solution)/shard_map/ppermute | solution.py:513
  147.8 30.3 %collective-permute-start.17 = (bf16[64,256]{1,0:T(8,128)(2,1)S(1)}, bf16[64,256]{1,0:T(8,128)(2,1)S(1)}, u32[]{:S(2)}, u32[]{:S(2)}) collective-permute-start(bf16[64,256]{1,0:T(8,128)(2,1)S(1)} %add_convert_fusion), channel_id=1, source_target_pairs={{0,48},{16,64},{32,80},{48,96},{64,112},{80,0},{96,16},{112,32},{1... | collective-permute-start | bytes 98312 | tf_op jit(solution)/shard_map/ppermute | solution.py:513
  176.6 4.6 %collective-permute-start.16 = (bf16[64,256]{1,0:T(8,128)(2,1)S(1)}, bf16[64,256]{1,0:T(8,128)(2,1)S(1)}, u32[]{:S(2)}, u32[]{:S(2)}) collective-permute-start(bf16[64,256]{1,0:T(8,128)(2,1)S(1)} %add_convert_fusion), channel_id=1, source_target_pairs={{0,32},{16,48},{32,64},{48,80},{64,96},{80,112},{96,0},{112,16},{1... | collective-permute-start | bytes 98312 | tf_op jit(solution)/shard_map/ppermute | solution.py:513
  177.3 4.0 %collective-permute-start.15 = (bf16[64,256]{1,0:T(8,128)(2,1)S(1)}, bf16[64,256]{1,0:T(8,128)(2,1)S(1)}, u32[]{:S(2)}, u32[]{:S(2)}) collective-permute-start(bf16[64,256]{1,0:T(8,128)(2,1)S(1)} %add_convert_fusion), channel_id=1, source_target_pairs={{0,16},{16,32},{32,48},{48,64},{64,80},{80,96},{96,112},{112,0},{1... | collective-permute-start | bytes 98312 | tf_op jit(solution)/shard_map/ppermute | solution.py:513
  181.3 0.7 copy-start

commit v3 on v2

--- a/solution.py
+++ b/solution.py
@@ -97,6 +97,14 @@
     return target, source
 
 
+def spread(ref, first, number):
+    row = lax.broadcasted_iota(jnp.int32, (number, 128), 0)
+    value = jnp.full((number, 128), ref[first], jnp.int32)
+    for u in range(1, number):
+        value = jnp.where(row == u, ref[first + u], value)
+    return value
+
+
 def place_rows(rows, scratch, write):
     for r, value in enumerate(rows):
         scratch[pl.ds(r, 8, stride=ROWS), :] = value
@@ -115,10 +123,11 @@
 
 
 def moments_kernel(
-    slots_ref, pos_ref, dens_ref, counts_ref, code_ref, checks_ref, m2m_ref,
-    target_ref, source_ref, tile_ref, part_ref, *rest,
+    sizes, slots_ref, counts_ref, pos_ref, dens_ref, code_ref, checks_ref, m2m_ref,
+    target_ref, source_ref, tile_ref, first_ref, last_ref, *rest,
 ):
-    send_refs, (weights, moments_low, moments_high, scratch, spare) = rest[:8], rest[8:]
+    send_refs, part_refs = rest[:8], (rest[8], rest[0], rest[1])
+    weights, moments_low, moments_high, scratch, spare = rest[9:]
     step = pl.program_id(0)
     leaves = pos_ref.shape[1]
     total = moments_low.shape[0]
@@ -127,7 +136,7 @@
 
     def build(group, carry):
         at = pl.ds(pl.multiple_of(group * 8, 8), 8)
-        masked = jnp.where(lane < counts_ref[at, :], dens_ref[at, :], 0.0)
+        masked = jnp.where(lane < spread(counts_ref, step * leaves + group * 8, 8), dens_ref[at, :], 0.0)
         weights[at, :] = masked
         target, source = panel_rows([pos_ref[d, at, :] for d in range(3)], masked)
 
@@ -151,8 +160,8 @@
         tile_ref[:, pl.ds(pl.multiple_of((first + part * 4) * 128, 512), 512)] = kernel
         block = part // 4
         value = weights[pl.ds(pl.multiple_of(first + block * 16, 16), 16), :]
-        spread = [jnp.where(row == part % 4 * 4 + u, value, 0.0) for u in range(4)]
-        out = dot(jnp.concatenate(spread, axis=1).astype(BF), kernel, ((1,), (1,)))
+        apart = [jnp.where(row == part % 4 * 4 + u, value, 0.0) for u in range(4)]
+        out = dot(jnp.concatenate(apart, axis=1).astype(BF), kernel, ((1,), (1,)))
         sums[block] = out if part % 4 == 0 else sums[block] + out
         if part % 4 == 3:
             low = (sums[block] * (1.0 / math.sqrt(128))).astype(BF).astype(F32)
@@ -174,46 +183,46 @@
     span = 64
     lax.fori_loop(0, leaves // span, expand, 0)
 
+    @pl.when(step == 0)
+    def _():
+        first_ref[...] = source_ref[0:HW]
+
     @pl.when(step == pl.num_programs(0) - 1)
     def _():
+        last_ref[...] = source_ref[leaves - HW :]
+        group, place = lax.axis_index("oct"), lax.axis_index("leaf")
+        oct_size, leaf_size = sizes
         for partner in range(8):
+            if partner < 5:
+                other = jnp.clip(place + 2 - partner, 0, leaf_size - 1)
+                other = group * leaf_size + other
+            else:
+                by = (oct_size - 1, 1, oct_size // 2)[partner - 5]
+                other = lax.rem(group + by, oct_size) * leaf_size + place
 
             def pick(s, carry):
-                slot = jnp.maximum(slots_ref[partner, s], 0)
+                slot = jnp.maximum(slots_ref[s, other], 0)
                 spare[pl.ds(s, 1), :] = moments_low[pl.ds(slot, 1), :]
                 scratch[pl.ds(s, 1), :] = moments_high[pl.ds(slot, 1), :]
                 return carry
 
             lax.fori_loop(0, 32, pick, 0, unroll=8)
-            send_refs[partner][...] = jnp.concatenate(
+            send_refs[partner][-32:, :] = jnp.concatenate(
                 [spare[0:32, :], scratch[0:32, :]], axis=1
             ).astype(BF)
         low = jnp.concatenate([moments_low[...], moments_high[...]], axis=1).astype(BF)
-        parents = part_ref.shape[0]
-        acc = jnp.zeros(part_ref.shape, F32)
+        parents = part_refs[0].shape[0]
+        acc = jnp.zeros(part_refs[0].shape, F32)
         for c in range(8):
             row = lax.broadcasted_iota(jnp.int32, (parents, total), 0) + c * parents
             chosen = jnp.where(row == code_ref[...], 1.0, 0.0).astype(BF)
             high, rest = split(dot(chosen, low))
             acc += dot(high.astype(BF), m2m_ref[c]) + dot(rest.astype(BF), m2m_ref[c])
-        part_ref[...] = acc.astype(BF)
-
-
-def halo_kernel(raw_ref, source_ref, scratch):
-    def build(group, carry):
-        at = pl.ds(pl.multiple_of(group * 8, 8), 8)
-        _, source = panel_rows([raw_ref[d, at, :] for d in range(3)], raw_ref[3, at, :])
-
-        def put_source(u, value):
-            source_ref[group * 8 + u] = value
-
-        place_rows(source, scratch, put_source)
-        return carry
-
-    lax.fori_loop(0, raw_ref.shape[1] // 8, build, 0)
-
-
-def near_kernel(begin, index_ref, dir_ref, target_ref, *refs):
+        for part_ref in part_refs:
+            part_ref[0:parents, :] = acc.astype(BF)
+
+
+def near_kernel(begin, offset_ref, dir_ref, target_ref, *refs):
     *parts, scale_ref, add_ref, out_ref, window, sems = refs
     leaves = target_ref.shape[0]
     copies, at = [], 0
@@ -236,7 +245,7 @@
         whole = begin + leaf
         rows, weights = [], []
         for j in range(4):
-            base = window[index_ref[j, whole]]
+            base = window[leaf + HW + offset_ref[j, whole]]
             way = dir_ref[j, whole]
             rows.append(base * scale_ref[way] + add_ref[way])
             weights.append(base[16:32])
@@ -261,28 +270,39 @@
 
 
 def translate_kernel(
-    far_ref, coarse_from_ref, coarse_to_ref, recv_ref, parents_ref, m2l_ref, l2l_ref,
-    out_ref, z_low, z_high, groups_low, groups_high, parents_low, parents_high, acc,
-    rows_low, rows_high,
+    far_ref, coarse_from_ref, coarse_to_ref, *refs,
 ):
+    recv_refs, parent_refs, (m2l_ref, l2l_ref, out_ref) = refs[:8], refs[8:12], refs[12:15]
+    z_low, z_high, groups_low, groups_high, parents_low, parents_high = refs[15:21]
+    acc, rows_low, rows_high, recv_ref = refs[21:]
     step = pl.program_id(0)
     count = m2l_ref.shape[0]
     received = recv_ref.shape[0]
     cells = acc.shape[0]
-    entries, leaves = far_ref.shape
+    leaves = rows_low.shape[0]
+    entries = far_ref.shape[0] // leaves
     coarse, _ = coarse_from_ref.shape
 
     @pl.when(step == 0)
     def _():
         groups_low[...] = jnp.zeros(groups_low.shape, F32)
         groups_high[...] = jnp.zeros(groups_high.shape, F32)
-        parents_low[...] = parents_ref[:, :128].astype(F32)
-        parents_high[...] = parents_ref[:, 128:].astype(F32)
+        oct_size = parents_low.shape[0] // cells
+        before = 0
+        for part in parent_refs:
+            for k in range(part.shape[0] // cells):
+                owner = lax.rem(lax.axis_index("oct") + oct_size - before, oct_size)
+                at = pl.ds(pl.multiple_of(owner * cells, cells), cells)
+                piece = part[k * cells : (k + 1) * cells, :].astype(F32)
+                parents_low[at, :], parents_high[at, :] = piece[:, :128], piece[:, 128:]
+                before += 1
+        for k, part in enumerate(recv_refs):
+            recv_ref[k * 32 : (k + 1) * 32, :] = part[-32:, :]
         acc[...] = jnp.zeros(acc.shape, F32)
 
         def gather(q, carry):
             for j in range(coarse):
-                at = pl.ds(coarse_to_ref[j, q], 1)
+                at = pl.ds(coarse_to_ref[j, q] * cells + q, 1)
                 row = pl.ds(coarse_from_ref[j, q], 1)
                 groups_low[at, :] = groups_low[at, :] + parents_low[row, :]
                 groups_high[at, :] = groups_high[at, :] + parents_high[row, :]
@@ -315,7 +335,7 @@
             for u in range(8):
                 lows, highs = [None] * 4, [None] * 4
                 for j in range(entries):
-                    at = pl.ds(far_ref[j, group * 8 + u], 1)
+                    at = pl.ds(far_ref[j * leaves + group * 8 + u], 1)
                     low, high = z_low[at, :], z_high[at, :]
                     k = j % 4
                     lows[k] = low if lows[k] is None else lows[k] + low
@@ -330,7 +350,7 @@
         out_ref[:, 128:] = rows_high[...].astype(BF)
 
 
-def far_kernel(tile_ref, exp_ref, dens_ref, counts_ref, *refs):
+def far_kernel(counts_ref, tile_ref, exp_ref, dens_ref, *refs):
     near_refs, out_ref = refs[:-1], refs[-1]
     step = pl.program_id(0)
     leaves = out_ref.shape[0]
@@ -349,7 +369,8 @@
             other = near_refs[k][pl.ds(pl.multiple_of(step % per * leaves + group * unroll, 16), 16), :]
             near = jnp.where(step // per == k, other, near)
         value = 0.5 * dens_ref[at, :] + near + far * (1.0 / math.sqrt(256))
-        out_ref[at, :] = jnp.where(lane < counts_ref[at, :], value, 0.0)
+        counts = spread(counts_ref, step * leaves + group * unroll, unroll)
+        out_ref[at, :] = jnp.where(lane < counts, value, 0.0)
 
 
 def params(mib=56):
@@ -368,44 +389,20 @@
     group, place = lax.axis_index("oct"), lax.axis_index("leaf")
     cap = send_slots.shape[2]
     planes = positions.transpose(1, 0, 2)
-    counts_column = counts[:, None]
-    spread_counts = jnp.broadcast_to(counts_column, (leaves, panels))
     checks = check_rows(width)
     scale, add = shift_rows()
 
-    lanes = jnp.arange(panels, dtype=jnp.int32)[None, :]
-
-    def edge(begin):
-        rows = slice(begin, begin + HW)
-        masked = jnp.where(lanes < counts_column[rows], density[rows], 0.0)
-        return jnp.concatenate([planes[:, rows], masked[None]], axis=0)
-
-    up = [(i, i + 1) for i in range(leaf_size - 1)]
-    down = [(i + 1, i) for i in range(leaf_size - 1)]
-    before = lax.ppermute(edge(leaves - HW), "leaf", up)
-    after = lax.ppermute(edge(0), "leaf", down)
-
-    moves = [("leaf", k - 2) for k in range(5)]
-    moves += [("oct", 1), ("oct", -1), ("oct", oct_size // 2)]
-    targets = []
-    for axis, by in moves:
-        if axis == "leaf":
-            targets.append(group * leaf_size + jnp.clip(place - by, 0, leaf_size - 1))
-        else:
-            targets.append((group - by) % oct_size * leaf_size + place)
-    slots = jnp.stack([send_slots[0, target] for target in targets])
     code = (child_pos * cells + leaf_parent)[None, :]
 
     steps = 8
     block = leaves // steps
     chunk = leaves // 4
-    target, source, tile, partial, *send = pl.pallas_call(
-        moments_kernel,
+    target, source, tile, first, last, *send = pl.pallas_call(
+        functools.partial(moments_kernel, (oct_size, leaf_size)),
         grid=(steps,),
         in_specs=[
-            SMEM,
+            SMEM, SMEM,
             pl.BlockSpec((3, block, panels), lambda i: (0, i, 0)),
-            pl.BlockSpec((block, panels), lambda i: (i, 0)),
             pl.BlockSpec((block, panels), lambda i: (i, 0)),
             VMEM, VMEM, VMEM,
         ],
@@ -414,14 +411,16 @@
             pl.BlockSpec((block, ROWS, panels), lambda i: (i, 0, 0)),
             pl.BlockSpec((width, block * panels), lambda i: (0, i)),
         ]
-        + [VMEM] * 9,
+        + [VMEM] * 11,
         out_shape=[
             jax.ShapeDtypeStruct((leaves, ROWS, panels), BF),
             jax.ShapeDtypeStruct((leaves, ROWS, panels), BF),
             jax.ShapeDtypeStruct((width, leaves * panels), BF),
-            jax.ShapeDtypeStruct((cells, width), BF),
         ]
-        + [jax.ShapeDtypeStruct((cap, width), BF)] * 8,
+        + [jax.ShapeDtypeStruct((HW, ROWS, panels), BF)] * 2
+        + [jax.ShapeDtypeStruct((cells + cap, width), BF)] * 2
+        + [jax.ShapeDtypeStruct((cap, width), BF)] * 6
+        + [jax.ShapeDtypeStruct((cells, width), BF)],
         scratch_shapes=[
             pltpu.VMEM((block, 128), F32),
             pltpu.VMEM((leaves, 128), F32),
@@ -431,38 +430,16 @@
         ],
         compiler_params=params(),
         name="moments",
-    )(slots, planes, density, spread_counts, code, checks.T, m2m)
-
-    halo = pl.pallas_call(
-        halo_kernel,
-        in_specs=[VMEM],
-        out_specs=VMEM,
-        out_shape=jax.ShapeDtypeStruct((2 * HW, ROWS, panels), BF),
-        scratch_shapes=[pltpu.VMEM((8 * ROWS, panels), F32)],
-        compiler_params=params(),
-        name="halo",
-    )(jnp.concatenate([before, after], axis=1))
-
-    pieces = []
-    for k, (axis, by) in enumerate(moves):
-        if axis == "leaf" and by == 0:
-            pieces.append(send[k])
-        elif axis == "leaf":
-            pairs = [(i, i - by) for i in range(leaf_size) if 0 <= i - by < leaf_size]
-            pieces.append(lax.ppermute(send[k], "leaf", pairs))
-        else:
-            pairs = [(i, (i - by) % oct_size) for i in range(oct_size)]
-            pieces.append(lax.ppermute(send[k], "oct", pairs))
-    received = jnp.concatenate(pieces, axis=0)
-
-    index = (jnp.arange(leaves, dtype=jnp.int32)[:, None] % chunk + near_offset + HW).T
+    )(send_slots[0].T, counts, planes, density, code, checks.T, m2m)
+
+    offsets = near_offset.T
     ways = near_dir.T
 
     def near_part(begin):
         if begin == 0:
-            parts = [halo[:HW], source]
+            parts = [before, source]
         elif begin + chunk == leaves:
-            parts = [source, halo[HW:]]
+            parts = [source, after]
         else:
             parts = [source]
         return pl.pallas_call(
@@ -485,38 +462,55 @@
                 flops=10**10, bytes_accessed=10**6, transcendentals=chunk * 2 * 65536
             ),
             name="near",
-        )(index, ways, target, *parts, scale, add)
-
-    inner = 4
-
-    def exchange(value, number, other):
-        got = [value.astype(F32)]
-        for by in range(1, number):
-            pairs = [(i, other(i, by)) for i in range(leaf_size)]
-            got.append(lax.ppermute(value, "leaf", pairs).astype(F32))
-        return got
-
-    near = []
-    fours = exchange(partial, inner, lambda i, by: i // inner * inner + (i + by) % inner)
-    near.append(near_part(0))
-    near[0], *fours = lax.optimization_barrier((near[0], *fours))
-    total = sum(fours[1:], fours[0]).astype(BF)
-    over = leaf_size // inner
-    sixteen = exchange(total, over, lambda i, by: (i + by * inner) % leaf_size)
-    sixteen[0], source, target = lax.optimization_barrier((sixteen[0], source, target))
-    near.append(near_part(chunk))
-    near[1], *sixteen = lax.optimization_barrier((near[1], *sixteen))
-    total = sum(sixteen[1:], sixteen[0]).astype(BF)
-    others = []
-    for by in range(1, oct_size):
-        pairs = [(i, (i + by) % oct_size) for i in range(oct_size)]
-        others.append(lax.ppermute(total, "oct", pairs))
+        )(offsets, ways, target, *parts, scale, add)
+
+    def shifted(value, axis, by):
+        size = lax.axis_size(axis)
+        return lax.ppermute(value, axis, [(i, (i + by) % size) for i in range(size)])
+
+    def moved(value, by):
+        pairs = [(i, i + by) for i in range(leaf_size) if 0 <= i + by < leaf_size]
+        return lax.ppermute(value, "leaf", pairs)
+
+    def added(pieces):
+        total = pieces[0].astype(F32)
+        for piece in pieces[1:]:
+            total = total + piece.astype(F32)
+        return total.astype(BF)
+
+    partial = send[8]
+    by_two = shifted(send[0], "leaf", 2)
+    by_one = shifted(send[1], "leaf", 1)
+    by_three = shifted(partial, "leaf", 3)
+    back_one, back_two = moved(send[3], -1), moved(send[4], -2)
+    before, after = moved(last, 1), moved(first, -1)
+    near = [None] * 4
+    near[1] = near_part(chunk)
+    near[1], by_one, by_two, by_three, back_one, back_two, before, after = lax.optimization_barrier(
+        (near[1], by_one, by_two, by_three, back_one, back_two, before, after)
+    )
+    four = added([partial, by_one[:cells], by_two[:cells], by_three])
+    strides = [shifted(four, "leaf", by) for by in (4, 8, 12)]
+    across = [
+        shifted(send[5], "oct", -1), shifted(send[6], "oct", 1),
+        shifted(send[7], "oct", oct_size // 2),
+    ]
+    four, source, target = lax.optimization_barrier((four, source, target))
+    near[2] = near_part(2 * chunk)
+    near[2], four, *moving = lax.optimization_barrier((near[2], four, *strides, *across))
+    strides, across = moving[:3], moving[3:]
+    total = added([four, *strides])
+    lower = shifted(total, "oct", 1)
     total, source, target = lax.optimization_barrier((total, source, target))
-    for k in range(2, leaves // chunk):
-        near.append(near_part(k * chunk))
-    *near, received, total = lax.optimization_barrier((*near, received, total))
-    others = lax.optimization_barrier((near[-1], *others))[1:]
-    every_parent = jnp.concatenate([total, *others], axis=0)
+    near[0] = near_part(0)
+    near[0], total, lower = lax.optimization_barrier((near[0], total, lower))
+    pair = jnp.concatenate([total, lower], axis=0)
+    pairs = [shifted(pair, "oct", by) for by in (2, 4, 6)]
+    pair, source, target = lax.optimization_barrier((pair, source, target))
+    near[3] = near_part(3 * chunk)
+    near[3], pair, *pairs = lax.optimization_barrier((near[3], pair, *pairs))
+    every_parent = [pair, *pairs]
+    received = [by_two, by_one, send[2], back_one, back_two, *across]
 
     owner, slot = far_source // cap, far_source % cap
     owner_group, owner_place = owner // leaf_size, owner % leaf_size
@@ -531,15 +525,16 @@
     )
     far_rows = (far_type * 8 + partner) * cap + slot
     own_row = kinds * 8 * cap + child_pos * cells + leaf_parent
-    far_rows = jnp.concatenate([far_rows.T, own_row[None, :]], axis=0)
-    coarse_from = (group - coarse_source // cells) % oct_size * cells + coarse_source % cells
-    coarse_to = (coarse_type * cells + jnp.arange(cells, dtype=jnp.int32)[:, None]).T
+    far_rows = jnp.concatenate([far_rows.T.reshape(-1), own_row])
     span = 8
     expansions = pl.pallas_call(
         translate_kernel,
         grid=(kinds // span,),
         in_specs=[
-            SMEM, SMEM, SMEM, VMEM, VMEM,
+            SMEM, SMEM, SMEM,
+        ]
+        + [VMEM] * 12
+        + [
             pl.BlockSpec((span, width, width), lambda i: (i, 0, 0)),
             VMEM,
         ],
@@ -555,18 +550,19 @@
             pltpu.VMEM((cells, width), F32),
             pltpu.VMEM((leaves, 128), F32),
             pltpu.VMEM((leaves, 128), F32),
+            pltpu.VMEM((8 * cap, width), BF),
         ],
         compiler_params=params(),
         name="translate",
-    )(far_rows, coarse_from.T, coarse_to, received, every_parent, m2l, l2l)
+    )(far_rows, coarse_source.T, coarse_type.T, *received, *every_parent, m2l, l2l)
 
     return pl.pallas_call(
         far_kernel,
         grid=(steps,),
         in_specs=[
+            SMEM,
             pl.BlockSpec((width, block * panels), lambda i: (0, i)),
             pl.BlockSpec((block, width), lambda i: (i, 0)),
-            pl.BlockSpec((block, panels), lambda i: (i, 0)),
             pl.BlockSpec((block, panels), lambda i: (i, 0)),
         ]
         + [VMEM] * len(near),
@@ -574,7 +570,7 @@
         out_shape=jax.ShapeDtypeStruct((leaves, panels), F32),
         compiler_params=params(),
         name="far",
-    )(tile, expansions, density, spread_counts, *near)
+    )(counts, tile, expansions, density, *near)
 
 
 def solution(mesh):

time: 234 us -> 183 us (0.78)
  waiting for transfers between devices: 20.7 us -> 4.22 us
  starting transfers between devices: 50.6 us -> 34.4 us
  local copies, waits for them, and re-layouts: 8.44 us -> 0.71 us
  other arithmetic: 7.9 us -> 2.1 us
  Pallas kernels: 145 us -> 140 us
    ppermute x22 -> x17, waiting for transfers between devices: 20.7 us -> 4.22 us  [the longest x13 4.21 us: shifted(): lax.ppermute(value, axis, [(i, (i + by) % size) for i in range(size)])]
    ppermute x22 -> x17, starting transfers between devices: 50.6 us -> 34.4 us  [the longest x13 28.6 us: shifted(): lax.ppermute(value, axis, [(i, (i + by) % size) for i in range(size)])]
    slice x3 -> x0, local copies, waits for them, and re-layouts: 3.5 us -> none  [the longest x1 1.84 us: near_part(): parts = [source, halo[HW:]]]
    transpose x3 -> x1, other arithmetic: 3.64 us -> 0.15 us  [local(): far_rows = jnp.concatenate([far_rows.T.reshape(-1), own_row])]
    pallas_call x1, Pallas kernels: 36.8 us -> 33.5 us  [local(): pl.pallas_call(translate_kernel, grid=(kinds // span,), in_specs=[SMEM, S...]
    pallas_call x3 -> x2, Pallas kernels: 54.5 us -> 52.9 us  [the longest x1 38.6 us: local(): pl.pallas_call(functools.partial(moments_kernel, (oct_size, leaf_size)),...]
  transfers between devices with their start and end apart: 22 -> 17, of which waited for: 8 -> 1; matrix products, arithmetic and copies ran while one was open for 4% -> 0% of each run, Pallas kernels for 17% -> 30%
where the time goes in v3:
time: 183 us; the launch traced here: 182 us
  Pallas kernels  140 us (77%)
  starting transfers between devices  34.4 us (19%)
  waiting for transfers between devices  4.22 us (2%)
  other arithmetic  2.1 us (1%)
    pallas_call x4, Pallas kernels, near_part(): pl.pallas_call(functools.partial(near_kernel, begin), grid=(1,), in_specs...  53.9 us
    pallas_call x1, Pallas kernels, local(): pl.pallas_call(functools.partial(moments_kernel, (oct_size, leaf_size)),...  38.6 us
    pallas_call x1, Pallas kernels, local(): pl.pallas_call(translate_kernel, grid=(kinds // span,), in_specs=[SMEM, S...  33.5 us
    ppermute x13, starting transfers between devices, shifted(): lax.ppermute(value, axis, [(i, (i + by) % size) for i in range(size)])  28.6 us
    pallas_call x1, Pallas kernels, local(): pl.pallas_call(far_kernel, grid=(steps,), in_specs=[SMEM, pl.BlockSpec((w...  14.3 us
    ppermute x4, starting transfers between devices, moved(): return lax.ppermute(value, 'leaf', pairs)  5.86 us
    ppermute x13, waiting for transfers between devices, shifted(): lax.ppermute(value, axis, [(i, (i + by) % size) for i in range(size)])  4.21 us
  transfers between devices with their start and end apart: 17, of which 1 were waited for; matrix products, arithmetic and copies ran while one was open for 0% of the time, Pallas kernels for 30%

profile of v3, /device:TPU:1, one launch (start us, length us, event | category | flops | bytes accessed | tf_op | source)
XLA Modules:
  0.0 182.3 jit_solution(5666950903426801955)
XLA Ops:
  0.0 1.3 add_add_fusion
  1.3 38.6 %moments.1 = (bf16[512,32,128]{2,1,0:T(8,128)(2,1)}, bf16[512,32,128]{2,1,0:T(8,128)(2,1)}, bf16[256,65536]{1,0:T(8,128)(2,1)}, bf16[32,32,128]{2,1,0:T(8,128)(2...) custom-call(s32[32,128]{1,0:T(8,128)} %bitcast.12, ...), custom_call_target="tpu_custom_call" | custom-call | tf_op jit(solution)/shard_map/moments/pallas_call | solution.py:400
  39.9 3.6 %collective-permute-start.2 = (bf16[64,256]{1,0:T(8,128)(2,1)}, bf16[64,256]{1,0:T(8,128)(2,1)S(1)}, u32[]{:S(2)}, u32[]{:S(2)}) collective-permute-start(bf16[64,256]{1,0:T(8,128)(2,1)} %get-tuple-element.57), channel_id=1, source_target_pairs={{0,3},{1,4},{2,5},{3,6},{4,7},{5,8},{6,9},{7,10},{8,11},{9,12},{10... | collective-permute-start | bytes 98312 | tf_op jit(solution)/shard_map/ppermute | solution.py:469
  43.5 2.0 %collective-permute-start.5 = (bf16[32,32,128]{2,1,0:T(8,128)(2,1)}, bf16[32,32,128]{2,1,0:T(8,128)(2,1)S(1)}, u32[]{:S(2)}, u32[]{:S(2)}) collective-permute-start(bf16[32,32,128]{2,1,0:T(8,128)(2,1)} %get-tuple-element.60), channel_id=1, source_target_pairs={{0,1},{1,2},{2,3},{3,4},{4,5},{5,6},{6,7},{7,8},{8,9},{9,10},{10,1... | collective-permute-start | bytes 786440 | tf_op jit(solution)/shard_map/ppermute | solution.py:473
  45.5 1.3 collective-permute-start.6
  46.8 1.3 collective-permute-start.3
  48.1 1.3 collective-permute-start.4
  49.4 0.0 copy-start.6
  49.5 0.0 copy-start.7
  49.5 13.6 %near.4.refs_1_ = f32[128,128]{1,0:T(8,128)} custom-call(s32[4,512]{1,0:T(4,128)} %bitcast.16, s32[4,512]{1,0:T(4,128)} %bitcast.20, bf16[512,32,128]{2,1,0:T(8,128)(2,1)} %get-tuple-element.87.target_ref, bf16[512,32,128]{2,1,0:T(8,128)(2,1)} %get-tuple-element.88.refs_0_.refs_1_, bf16[27,32,128]{2,1,0:T(8,128)(2,1)} %constant.95.clone.refs_1_.refs_2_, ...), custom_call_target="tpu_custom_call" | custom-call | flops 10000000000 | bytes 1000000 | tf_op jit(solution)/shard_map/near/pallas_call | solution.py:445
  63.1 0.1 fusion.6
  63.3 0.0 collective-permute-done.3.refs_3_
  63.3 2.8 %collective-permute-start = (bf16[96,256]{1,0:T(8,128)(2,1)S(1)}, bf16[96,256]{1,0:T(8,128)(2,1)S(1)}, u32[]{:S(2)}, u32[]{:S(2)}) collective-permute-start(bf16[96,256]{1,0:T(8,128)(2,1)S(1)} %copy-done.17), channel_id=1, source_target_pairs={{0,1},{1,2},{2,3},{3,4},{4,5},{5,6},{6,7},{7,8},{8,9},{9,10},{10,1... | collective-permute-start | bytes 147464 | tf_op jit(solution)/shard_map/ppermute | solution.py:469
  66.1 0.0 collective-permute-done.4.refs_4_
  66.1 4.3 %collective-permute-start.1 = (bf16[96,256]{1,0:T(8,128)(2,1)S(1)}, bf16[96,256]{1,0:T(8,128)(2,1)S(1)}, u32[]{:S(2)}, u32[]{:S(2)}) collective-permute-start(bf16[96,256]{1,0:T(8,128)(2,1)S(1)} %copy-done.16), channel_id=1, source_target_pairs={{0,2},{1,3},{2,4},{3,5},{4,6},{5,7},{6,8},{7,9},{8,10},{9,11},{10,... | collective-permute-start | bytes 147464 | tf_op jit(solution)/shard_map/ppermute | solution.py:469
  70.5 0.6 pad_add_fusion.far_ref
  71.1 0.0 collective-permute-done.2
  71.1 2.3 %collective-permute-start.10 = (bf16[32,256]{1,0:T(8,128)(2,1)S(1)}, bf16[32,256]{1,0:T(8,128)(2,1)S(1)}, u32[]{:S(2)}, u32[]{:S(2)}) collective-permute-start(bf16[32,256]{1,0:T(8,128)(2,1)S(1)} %copy-done.20), channel_id=1, source_target_pairs={{0,112},{16,0},{32,16},{48,32},{64,48},{80,64},{96,80},{112,96},{1... | collective-permute-start | bytes 49160 | tf_op jit(solution)/shard_map/ppermute | solution.py:469
  73.3 4.2 %collective-permute-done.refs_1_ = bf16[96,256]{1,0:T(8,128)(2,1)S(1)} collective-permute-done((bf16[96,256]{1,0:T(8,128)(2,1)S(1)}, bf16[96,256]{1,0:T(8,128)(2,1)S(1)}, u32[]{:S(2)}, u32[]{:S(2)}) %collective-permute-start) | collective-permute-done | bytes 49184 | tf_op jit(solution)/shard_map/ppermute | solution.py:469
  77.5 4.0 %collective-permute-start.11 = (bf16[32,256]{1,0:T(8,128)(2,1)S(1)}, bf16[32,256]{1,0:T(8,128)(2,1)S(1)}, u32[]{:S(2)}, u32[]{:S(2)}) collective-permute-start(bf16[32,256]{1,0:T(8,128)(2,1)S(1)} %copy-done.19), channel_id=1, source_target_pairs={{0,16},{16,32},{32,48},{48,64},{64,80},{80,96},{96,112},{112,0},{1... | collective-permute-start | bytes 49160 | tf_op jit(solution)/shard_map/ppermute | solution.py:469
  81.6 0.0 collective-permute-done.1.refs_0_
  81.6 2.5 %collective-permute-start.12 = (bf16[32,256]{1,0:T(8,128)(2,1)S(1)}, bf16[32,256]{1,0:T(8,128)(2,1)S(1)}, u32[]{:S(2)}, u32[]{:S(2)}) collective-permute-start(bf16[32,256]{1,0:T(8,128)(2,1)S(1)} %copy-done.18), channel_id=1, source_target_pairs={{0,64},{16,80},{32,96},{48,112},{64,0},{80,16},{96,32},{112,48},{1... | collective-permute-start | bytes 49160 | tf_op jit(solution)/shard_map/ppermute | solution.py:469
  84.1 0.0 collective-permute-done.5.refs_0_
  84.1 0.0 collective-permute-done.6.refs_1_
  84.1 0.0 copy-start.14
  84.2 0.1 collective-permute-start.7
  84.3 1.6 collective-permute-start.8
  85.8 0.0 collective-permute-done.10.refs_5_
  85.8 1.3 collective-permute-start.9
  87.2 13.5 %near.5.refs_2_ = f32[128,128]{1,0:T(8,128)} custom-call(s32[4,512]{1,0:T(4,128)} %bitcast.17, s32[4,512]{1,0:T(4,128)} %bitcast.21, bf16[512,32,128]{2,1,0:T(8,128)(2,1)} %get-tuple-element.87.target_ref, bf16[512,32,128]{2,1,0:T(8,128)(2,1)} %get-tuple-element.88.refs_0_.refs_1_, bf16[27,32,128]{2,1,0:T(8,128)(2,1)} %constant.95.clone.refs_1_.refs_2_, ...), custom_call_target="tpu_custom_call" | custom-call | flops 10000000000 | bytes 1000000 | tf_op jit(solution)/shard_map/near/pallas_call | solution.py:445
  100.7 0.0 collective-permute-done.11.refs_6_
  100.8 0.0 collective-permute-done.12.refs_7_
  100.8 0.0 collective-permute-done.8
  100.8 0.0 collective-permute-done.9
  100.8 2.1 %collective-permute-start.13 = (bf16[64,256]{1,0:T(8,128)(2,1)S(1)}, bf16[64,256]{1,0:T(8,128)(2,1)S(1)}, u32[]{:S(2)}, u32[]{:S(2)}) collective-permute-start(bf16[64,256]{1,0:T(8,128)(2,1)S(1)} %add_convert_fusion), channel_id=1, source_target_pairs={{0,16},{16,32},{32,48},{48,64},{64,80},{80,96},{96,112},{112,0},{1... | collective-permute-start | bytes 98312 | tf_op jit(solution)/shard_map/ppermute | solution.py:469
  103.0 13.5 %near.6.refs_0_ = f32[128,128]{1,0:T(8,128)} custom-call(s32[4,512]{1,0:T(4,128)} %bitcast.18, s32[4,512]{1,0:T(4,128)} %bitcast.22, bf16[512,32,128]{2,1,0:T(8,128)(2,1)} %get-tuple-element.87.target_ref, bf16[32,32,128]{2,1,0:T(8,128)(2,1)} %copy-done.15, bf16[512,32,128]{2,1,0:T(8,128)(2,1)} %get-tuple-element.88.refs_0_.refs_1_, ...), custom_call_target="tpu_custom_call" | custom-call | flops 10000000000 | bytes 1000000 | tf_op jit(solution)/shard_map/near/pallas_call | solution.py:445
  116.5 0.1 collective-permute-start.14
  116.6 3.5 %collective-permute-start.15 = (bf16[128,256]{1,0:T(8,128)(2,1)S(1)}, bf16[128,256]{1,0:T(8,128)(2,1)S(1)}, u32[]{:S(2)}, u32[]{:S(2)}) collective-permute-start(bf16[128,256]{1,0:T(8,128)(2,1)S(1)} %constant_dynamic-update-slice_fusion.refs_8_), channel_id=1, source_target_pairs={{0,64},{16,80},{32,96},{48,112},{64,0},{80,16},{96,32},{112,48},{1... | collective-permute-start | bytes 196616 | tf_op jit(solution)/shard_map/ppermute | solution.py:469
  120.2 0.2 collective-permute-start.16
  120.4 13.4 %near.7.refs_3_ = f32[128,128]{1,0:T(8,128)} custom-call(s32[4,512]{1,0:T(4,128)} %bitcast.19, s32[4,512]{1,0:T(4,128)} %bitcast.23, bf16[512,32,128]{2,1,0:T(8,128)(2,1)} %get-tuple-element.87.target_ref, bf16[512,32,128]{2,1,0:T(8,128)(2,1)} %get-tuple-element.88.refs_0_.refs_1_, bf16[32,32,128]{2,1,0:T(8,128)(2,1)} %copy-done.14, ...), custom_call_target="tpu_custom_call" | custom-call | flops 10000000000 | bytes 1000000 | tf_op jit(solution)/shard_map/near/pallas_call | solution.py:445
  133.8 0.0 collective-permute-done.14.refs_9_
  133.9 0.0 copy-start.3
  133.9 0.0 collective-permute-done.16.refs_11_
  133.9 0.6 copy-done.3
  134.5 0.0 copy-done.4
  134.5 0.0 copy-done.5
  134.5 33.5 %translate.1.exp_ref = bf16[512,256]{1,0:T(8,128)(2,1)} custom-call(s32[14336]{0:T(1024)} %pad_add_fusion.far_ref, s32[16,64]{1,0:T(8,128)} %bitcast.14, s32[16,64]{1,0:T(8,128)} %bitcast.15, bf16[96,256]{1,0:T(8,128)(2,1)} %copy-done.2, bf16[96,256]{1,0:T(8,128)(2,1)} %copy-done.1, bf16[32,256]{1,0:T(8,128)(2,1)} %get-tuple-element.64.refs_2_, ...), custom_call_target="tpu_custom_call" | custom-call | tf_op jit(solution)/shard_map/translate/pallas_call | solution.py:530
  168.0 14.3 %far.1 = f32[512,128]{1,0:T(8,128)} custom-call(s32[512]{0:T(512)} %counts_ref.3, bf16[256,65536]{1,0:T(8,128)(2,1)} %get-tuple-element.52.tile_ref, bf16[512,256]{1,0:T(8,128)(2,1)} %translate.1.exp_ref, f32[512,128]{1,0:T(8,128)} %dens_ref.3, f32[128,128]{1,0:T(8,128)} %near.6.refs_0_, f32[128,128]{1,0:T(8,128)} %near.4.refs_1_, f32[128,128]{1,0:T(8,128)} %near.5.refs_2_, ...), custom_call_target="tpu_custom_call" | custom-call | tf_op jit(solution)/shard_map/far/pallas_call | solution.py:559
  (43 shorter events, 0.1 us)
Async XLA Ops:
  39.9 31.2 %collective-permute-start.2 = (bf16[64,256]{1,0:T(8,128)(2,1)}, bf16[64,256]{1,0:T(8,128)(2,1)S(1)}, u32[]{:S(2)}, u32[]{:S(2)}) collective-permute-start(bf16[64,256]{1,0:T(8,128)(2,1)} %get-tuple-element.57), channel_id=1, source_target_pairs={{0,3},{1,4},{2,5},{3,6},{4,7},{5,8},{6,9},{7,10},{8,11},{9,12},{10... | collective-permute-start | bytes 98312 | tf_op jit(solution)/shard_map/ppermute | solution.py:469
  43.5 40.6 %collective-permute-start.5 = (bf16[32,32,128]{2,1,0:T(8,128)(2,1)}, bf16[32,32,128]{2,1,0:T(8,128)(2,1)S(1)}, u32[]{:S(2)}, u32[]{:S(2)}) collective-permute-start(bf16[32,32,128]{2,1,0:T(8,128)(2,1)} %get-tuple-element.60), channel_id=1, source_target_pairs={{0,1},{1,2},{2,3},{3,4},{4,5},{5,6},{6,7},{7,8},{8,9},{9,10},{10,1... | collective-permute-start | bytes 786440 | tf_op jit(solution)/shard_map/ppermute | solution.py:473
  45.5 38.6 %collective-permute-start.6 = (bf16[32,32,128]{2,1,0:T(8,128)(2,1)}, bf16[32,32,128]{2,1,0:T(8,128)(2,1)S(1)}, u32[]{:S(2)}, u32[]{:S(2)}) collective-permute-start(bf16[32,32,128]{2,1,0:T(8,128)(2,1)} %get-tuple-element.61), channel_id=1, source_target_pairs={{1,0},{2,1},{3,2},{4,3},{5,4},{6,5},{7,6},{8,7},{9,8},{10,9},{11,1... | collective-permute-start | bytes 786440 | tf_op jit(solution)/shard_map/ppermute | solution.py:473
  46.8 16.5 %collective-permute-start.3 = (bf16[32,256]{1,0:T(8,128)(2,1)}, bf16[32,256]{1,0:T(8,128)(2,1)S(1)}, u32[]{:S(2)}, u32[]{:S(2)}) collective-permute-start(bf16[32,256]{1,0:T(8,128)(2,1)} %get-tuple-element.58), channel_id=1, source_target_pairs={{1,0},{2,1},{3,2},{4,3},{5,4},{6,5},{7,6},{8,7},{9,8},{10,9},{11,1... | collective-permute-start | bytes 49160 | tf_op jit(solution)/shard_map/ppermute | solution.py:473
  48.1 18.0 %collective-permute-start.4 = (bf16[32,256]{1,0:T(8,128)(2,1)}, bf16[32,256]{1,0:T(8,128)(2,1)S(1)}, u32[]{:S(2)}, u32[]{:S(2)}) collective-permute-start(bf16[32,256]{1,0:T(8,128)(2,1)} %get-tuple-element.59), channel_id=1, source_target_pairs={{2,0},{3,1},{4,2},{5,3},{6,4},{7,5},{8,6},{9,7},{10,8},{11,9},{12,... | collective-permute-start | bytes 49160 | tf_op jit(solution)/shard_map/ppermute | solution.py:473
  49.4 13.7 %copy-start.6 = (s32[512,27]{0,1:T(8,128)S(1)}, s32[512,27]{0,1:T(8,128)}, u32[]{:S(2)}) copy-start(s32[512,27]{0,1:T(8,128)} %param.25) | copy-start | bytes 165892
  49.5 13.7 %copy-start.7 = (s32[512,27]{0,1:T(8,128)S(1)}, s32[512,27]{0,1:T(8,128)}, u32[]{:S(2)}) copy-start(s32[512,27]{0,1:T(8,128)} %param.24) | copy-start | bytes 165892
  49.5 13.8 %copy-start.17 = (bf16[96,256]{1,0:T(8,128)(2,1)S(1)}, bf16[96,256]{1,0:T(8,128)(2,1)}, u32[]{:S(2)}) copy-start(bf16[96,256]{1,0:T(8,128)(2,1)} %get-tuple-element.55) | copy-start | bytes 147460
  49.5 16.6 %copy-start.16 = (bf16[96,256]{1,0:T(8,128)(2,1)S(1)}, bf16[96,256]{1,0:T(8,128)(2,1)}, u32[]{:S(2)}) copy-start(bf16[96,256]{1,0:T(8,128)(2,1)} %get-tuple-element.56) | copy-start | bytes 147460
  49.5 21.6 %copy-start.20 = (bf16[32,256]{1,0:T(8,128)(2,1)S(1)}, bf16[32,256]{1,0:T(8,128)(2,1)}, u32[]{:S(2)}) copy-start(bf16[32,256]{1,0:T(8,128)(2,1)} %get-tuple-element.71) | copy-start | bytes 49156
  49.5 28.0 %copy-start.19 = (bf16[32,256]{1,0:T(8,128)(2,1)S(1)}, bf16[32,256]{1,0:T(8,128)(2,1)}, u32[]{:S(2)}) copy-start(bf16[32,256]{1,0:T(8,128)(2,1)} %get-tuple-element.72) | copy-start | bytes 49156
  49.5 32.1 %copy-start.18 = (bf16[32,256]{1,0:T(8,128)(2,1)S(1)}, bf16[32,256]{1,0:T(8,128)(2,1)}, u32[]{:S(2)}) copy-start(bf16[32,256]{1,0:T(8,128)(2,1)} %get-tuple-element.73) | copy-start | bytes 49156
  49.5 34.6 %copy-start.8 = (bf16[64,256]{1,0:T(8,128)(2,1)S(1)}, bf16[64,256]{1,0:T(8,128)(2,1)}, u32[]{:S(2)}) copy-start(bf16[64,256]{1,0:T(8,128)(2,1)} %get-tuple-element.57) | copy-start | bytes 98308
  63.3 37.4 %copy-start.9 = (bf16[32,256]{1,0:T(8,128)(2,1)}, bf16[32,256]{1,0:T(8,128)(2,1)S(1)}, u32[]{:S(2)}) copy-start(bf16[32,256]{1,0:T(8,128)(2,1)S(1)} %collective-permute-done.3.refs_3_) | copy-start | bytes 49156
  63.3 14.2 %collective-permute-start = (bf16[96,256]{1,0:T(8,128)(2,1)S(1)}, bf16[96,256]{1,0:T(8,128)(2,1)S(1)}, u32[]{:S(2)}, u32[]{:S(2)}) collective-permute-start(bf16[96,256]{1,0:T(8,128)(2,1)S(1)} %copy-done.17), channel_id=1, source_target_pairs={{0,1},{1,2},{2,3},{3,4},{4,5},{5,6},{6,7},{7,8},{8,9},{9,10},{10,1... | collective-permute-start | bytes 147464 | tf_op jit(solution)/shard_map/ppermute | solution.py:469
  66.1 34.6 %copy-start.10 = (bf16[32,256]{1,0:T(8,128)(2,1)}, bf16[32,256]{1,0:T(8,128)(2,1)S(1)}, u32[]{:S(2)}) copy-start(bf16[32,256]{1,0:T(8,128)(2,1)S(1)} %collective-permute-done.4.refs_4_) | copy-start | bytes 49156
  66.1 15.5 %collective-permute-start.1 = (bf16[96,256]{1,0:T(8,128)(2,1)S(1)}, bf16[96,256]{1,0:T(8,128)(2,1)S(1)}, u32[]{:S(2)}, u32[]{:S(2)}) collective-permute-start(bf16[96,256]{1,0:T(8,128)(2,1)S(1)} %copy-done.16), channel_id=1, source_target_pairs={{0,2},{1,3},{2,4},{3,5},{4,6},{5,7},{6,8},{7,9},{8,10},{9,11},{10,... | collective-permute-start | bytes 147464 | tf_op jit(solution)/shard_map/ppermute | solution.py:469
  71.1 14.8 %collective-permute-start.10 = (bf16[32,256]{1,0:T(8,128)(2,1)S(1)}, bf16[32,256]{1,0:T(8,128)(2,1)S(1)}, u32[]{:S(2)}, u32[]{:S(2)}) collective-permute-start(bf16[32,256]{1,0:T(8,128)(2,1)S(1)} %copy-done.20), channel_id=1, source_target_pairs={{0,112},{16,0},{32,16},{48,32},{64,48},{80,64},{96,80},{112,96},{1... | collective-permute-start | bytes 49160 | tf_op jit(solution)/shard_map/ppermute | solution.py:469
  77.5 23.2 %copy-start.1 = (bf16[96,256]{1,0:T(8,128)(2,1)}, bf16[96,256]{1,0:T(8,128)(2,1)S(1)}, u32[]{:S(2)}) copy-start(bf16[96,256]{1,0:T(8,128)(2,1)S(1)} %collective-permute-done.refs_1_) | copy-start | bytes 147460
  77.5 23.2 %collective-permute-start.11 = (bf16[32,256]{1,0:T(8,128)(2,1)S(1)}, bf16[32,256]{1,0:T(8,128)(2,1)S(1)}, u32[]{:S(2)}, u32[]{:S(2)}) collective-permute-start(bf16[32,256]{1,0:T(8,128)(2,1)S(1)} %copy-done.19), channel_id=1, source_target_pairs={{0,16},{16,32},{32,48},{48,64},{64,80},{80,96},{96,112},{112,0},{1... | collective-permute-start | bytes 49160 | tf_op jit(solution)/shard_map/ppermute | solution.py:469
  81.6 19.1 %copy-start.2 = (bf16[96,256]{1,0:T(8,128)(2,1)}, bf16[96,256]{1,0:T(8,128)(2,1)S(1)}, u32[]{:S(2)}) copy-start(bf16[96,256]{1,0:T(8,128)(2,1)S(1)} %collective-permute-done.1.refs_0_) | copy-start | bytes 147460
  81.6 19.2 %collective-permute-start.12 = (bf16[32,256]{1,0:T(8,128)(2,1)S(1)}, bf16[32,256]{1,0:T(8,128)(2,1)S(1)}, u32[]{:S(2)}, u32[]{:S(2)}) collective-permute-start(bf16[32,256]{1,0:T(8,128)(2,1)S(1)} %copy-done.18), channel_id=1, source_target_pairs={{0,64},{16,80},{32,96},{48,112},{64,0},{80,16},{96,32},{112,48},{1... | collective-permute-start | bytes 49160 | tf_op jit(solution)/shard_map/ppermute | solution.py:469
  84.1 16.6 %copy-start.15 = (bf16[32,32,128]{2,1,0:T(8,128)(2,1)}, bf16[32,32,128]{2,1,0:T(8,128)(2,1)S(1)}, u32[]{:S(2)}) copy-start(bf16[32,32,128]{2,1,0:T(8,128)(2,1)S(1)} %collective-permute-done.5.refs_0_) | copy-start | bytes 786436
  84.1 16.6 %copy-start.14 = (bf16[32,32,128]{2,1,0:T(8,128)(2,1)}, bf16[32,32,128]{2,1,0:T(8,128)(2,1)S(1)}, u32[]{:S(2)}) copy-start(bf16[32,32,128]{2,1,0:T(8,128)(2,1)S(1)} %collective-permute-done.6.refs_1_) | copy-start | bytes 786436
  84.2 16.6 %collective-permute-start.7 = (bf16[64,256]{1,0:T(8,128)(2,1)S(1)}, bf16[64,256]{1,0:T(8,128)(2,1)S(1)}, u32[]{:S(2)}, u32[]{:S(2)}) collective-permute-start(bf16[64,256]{1,0:T(8,128)(2,1)S(1)} %add_convert_fusion.1), channel_id=1, source_target_pairs={{0,4},{1,5},{2,6},{3,7},{4,8},{5,9},{6,10},{7,11},{8,12},{9,13},{1... | collective-permute-start | bytes 98312 | tf_op jit(solution)/shard_map/ppermute | solution.py:469
  84.3 16.5 %collective-permute-start.8 = (bf16[64,256]{1,0:T(8,128)(2,1)S(1)}, bf16[64,256]{1,0:T(8,128)(2,1)S(1)}, u32[]{:S(2)}, u32[]{:S(2)}) collective-permute-start(bf16[64,256]{1,0:T(8,128)(2,1)S(1)} %add_convert_fusion.1), channel_id=1, source_target_pairs={{0,8},{1,9},{2,10},{3,11},{4,12},{5,13},{6,14},{7,15},{8,0},{9,1},... | collective-permute-start | bytes 98312 | tf_op jit(solution)/shard_map/ppermute | solution.py:469
  85.8 14.9 %copy-start.11 = (bf16[32,256]{1,0:T(8,128)(2,1)}, bf16[32,256]{1,0:T(8,128)(2,1)S(1)}, u32[]{:S(2)}) copy-start(bf16[32,256]{1,0:T(8,128)(2,1)S(1)} %collective-permute-done.10.refs_5_) | copy-start | bytes 49156
  85.8 15.0 %collective-permute-start.9 = (bf16[64,256]{1,0:T(8,128)(2,1)S(1)}, bf16[64,256]{1,0:T(8,128)(2,1)S(1)}, u32[]{:S(2)}, u32[]{:S(2)}) collective-permute-start(bf16[64,256]{1,0:T(8,128)(2,1)S(1)} %add_convert_fusion.1), channel_id=1, source_target_pairs={{0,12},{1,13},{2,14},{3,15},{4,0},{5,1},{6,2},{7,3},{8,4},{9,5},{1... | collective-permute-start | bytes 98312 | tf_op jit(solution)/shard_map/ppermute | solution.py:469
  100.8 15.7 %copy-start.12 = (bf16[32,256]{1,0:T(8,128)(2,1)}, bf16[32,256]{1,0:T(8,128)(2,1)S(1)}, u32[]{:S(2)}) copy-start(bf16[32,256]{1,0:T(8,128)(2,1)S(1)} %collective-permute-done.11.refs_6_) | copy-start | bytes 49156
  100.8 15.7 %copy-start.13 = (bf16[32,256]{1,0:T(8,128)(2,1)}, bf16[32,256]{1,0:T(8,128)(2,1)S(1)}, u32[]{:S(2)}) copy-start(bf16[32,256]{1,0:T(8,128)(2,1)S(1)} %collective-permute-done.12.refs_7_) | copy-start | bytes 49156
  100.8 15.6 %collective-permute-start.13 = (bf16[64,256]{1,0:T(8,128)(2,1)S(1)}, bf16[64,256]{1,0:T(8,128)(2,1)S(1)}, u32[]{:S(2)}, u32[]{:S(2)}) collective-permute-start(bf16[64,256]{1,0:T(8,128)(2,1)S(1)} %add_convert_fusion), channel_id=1, source_target_pairs={{0,16},{16,32},{32,48},{48,64},{64,80},{80,96},{96,112},{112,0},{1... | collective-permute-start | bytes 98312 | tf_op jit(solution)/shard_map/ppermute | solution.py:469
  116.5 17.3 %copy-start = (bf16[128,256]{1,0:T(8,128)(2,1)}, bf16[128,256]{1,0:T(8,128)(2,1)S(1)}, u32[]{:S(2)}) copy-start(bf16[128,256]{1,0:T(8,128)(2,1)S(1)} %constant_dynamic-update-slice_fusion.refs_8_) | copy-start | bytes 196612
  116.5 17.3 %collective-permute-start.14 = (bf16[128,256]{1,0:T(8,128)(2,1)S(1)}, bf16[128,256]{1,0:T(8,128)(2,1)S(1)}, u32[]{:S(2)}, u32[]{:S(2)}) collective-permute-start(bf16[128,256]{1,0:T(8,128)(2,1)S(1)} %constant_dynamic-update-slice_fusion.refs_8_), channel_id=1, source_target_pairs={{0,32},{16,48},{32,64},{48,80},{64,96},{80,112},{96,0},{112,16},{1... | collective-permute-start | bytes 196616 | tf_op jit(solution)/shard_map/ppermute | solution.py:469
  116.6 17.2 %collective-permute-start.15 = (bf16[128,256]{1,0:T(8,128)(2,1)S(1)}, bf16[128,256]{1,0:T(8,128)(2,1)S(1)}, u32[]{:S(2)}, u32[]{:S(2)}) collective-permute-start(bf16[128,256]{1,0:T(8,128)(2,1)S(1)} %constant_dynamic-update-slice_fusion.refs_8_), channel_id=1, source_target_pairs={{0,64},{16,80},{32,96},{48,112},{64,0},{80,16},{96,32},{112,48},{1... | collective-permute-start | bytes 196616 | tf_op jit(solution)/shard_map/ppermute | solution.py:469
  120.2 13.7 %collective-permute-start.16 = (bf16[128,256]{1,0:T(8,128)(2,1)S(1)}, bf16[128,256]{1,0:T(8,128)(2,1)S(1)}, u32[]{:S(2)}, u32[]{:S(2)}) collective-permute-start(bf16[128,256]{1,0:T(8,128)(2,1)S(1)} %constant_dynamic-update-slice_fusion.refs_8_), channel_id=1, source_target_pairs={{0,96},{16,112},{32,0},{48,16},{64,32},{80,48},{96,64},{112,80},{1... | collective-permute-start | bytes 196616 | tf_op jit(solution)/shard_map/ppermute | solution.py:469
  133.9 0.6 copy-start.3
  133.9 0.6 copy-start.4
  133.9 0.6 copy-start.5

commit v4 on v3

--- a/solution.py
+++ b/solution.py
@@ -16,6 +16,7 @@
 RADIUS = 2.0
 RATE = -KAPPA * math.log2(math.e)
 ROWS = 32
+PITCH = 36
 BF = jnp.bfloat16
 F32 = jnp.float32
 VMEM = pl.BlockSpec(memory_space=pltpu.VMEM)
@@ -107,9 +108,9 @@
 
 def place_rows(rows, scratch, write):
     for r, value in enumerate(rows):
-        scratch[pl.ds(r, 8, stride=ROWS), :] = value
+        scratch[pl.ds(r, 8, stride=PITCH), :] = value
     for u in range(8):
-        write(u, scratch[u * ROWS : (u + 1) * ROWS, :].astype(BF))
+        write(u, scratch[u * PITCH : u * PITCH + ROWS, :].astype(BF))
 
 
 def green(squared):
@@ -222,24 +223,25 @@
             part_ref[0:parents, :] = acc.astype(BF)
 
 
-def near_kernel(begin, offset_ref, dir_ref, target_ref, *refs):
-    *parts, scale_ref, add_ref, out_ref, window, sems = refs
-    leaves = target_ref.shape[0]
-    copies, at = [], 0
+def load_window(begin, target_ref, parts, target, window, sems):
+    leaves = target.shape[0]
+    copies = [pltpu.make_async_copy(target_ref.at[begin : begin + leaves], target, sems.at[2])]
+    at = 0
     for k, part in enumerate(parts):
         size = part.shape[0]
-        if size == HW:
-            source = part
-        else:
+        if size != HW:
             low = max(begin - HW, 0)
             size = min(begin + leaves + HW, size) - low
-            source = part.at[low : low + size]
-        copies.append(pltpu.make_async_copy(source, window.at[at : at + size], sems.at[k]))
+            part = part.at[low : low + size]
+        copies.append(pltpu.make_async_copy(part, window.at[at : at + size], sems.at[k]))
         at += size
     for copy in copies:
         copy.start()
-    for copy in copies:
-        copy.wait()
+    return copies
+
+
+def near_leaves(begin, first, number, refs, beside=None):
+    offset_ref, dir_ref, scale_ref, add_ref, target, window, out_ref = refs
 
     def squares(leaf):
         whole = begin + leaf
@@ -249,105 +251,135 @@
             way = dir_ref[j, whole]
             rows.append(base * scale_ref[way] + add_ref[way])
             weights.append(base[16:32])
-        value = dot(target_ref[leaf], jnp.concatenate(rows, 1), ((0,), (0,)))
+        value = dot(target[leaf], jnp.concatenate(rows, 1), ((0,), (0,)))
         return value, jnp.concatenate(weights, 1)
 
-    unroll, depth = 32, 2
+    depth = 2
+    ahead = []
+    for u in range(number + depth):
+        if u < number:
+            ahead.append(squares(first + u))
+            if beside is not None:
+                beside(u)
+        if u >= depth:
+            value, weights = ahead[u - depth]
+            ahead[u - depth] = None
+            out = dot(weights, green(value), ((1,), (1,)))[15:16]
+            out_ref[pl.ds(first + u - depth, 1), :] = out * (1.0 / math.sqrt(512))
+
+
+def near_kernel(begin, offset_ref, dir_ref, scale_ref, add_ref, target_ref, *refs):
+    *parts, out_ref, target, window, sems = refs
+    for copy in load_window(begin, target_ref, parts, target, window, sems):
+        copy.wait()
 
     def body(group, carry):
-        first = group * unroll
-        ahead = []
-        for u in range(unroll + depth):
-            if u < unroll:
-                ahead.append(squares(first + u))
-            if u >= depth:
-                value, weights = ahead[u - depth]
-                out = dot(weights, green(value), ((1,), (1,)))[15:16]
-                out_ref[pl.ds(first + u - depth, 1), :] = out * (1.0 / math.sqrt(512))
+        own = (offset_ref, dir_ref, scale_ref, add_ref, target, window, out_ref)
+        near_leaves(begin, group * 32, 32, own)
         return carry
 
-    lax.fori_loop(0, leaves // unroll, body, 0)
+    lax.fori_loop(0, target.shape[0] // 32, body, 0)
 
 
 def translate_kernel(
-    far_ref, coarse_from_ref, coarse_to_ref, *refs,
+    begin, offset_ref, dir_ref, far_ref, coarse_from_ref, coarse_to_ref,
+    scale_ref, add_ref, l2l_ref, target_ref, source_ref, after_ref, m2l_ref, *refs,
 ):
-    recv_refs, parent_refs, (m2l_ref, l2l_ref, out_ref) = refs[:8], refs[8:12], refs[12:15]
-    z_low, z_high, groups_low, groups_high, parents_low, parents_high = refs[15:21]
-    acc, rows_low, rows_high, recv_ref = refs[21:]
-    step = pl.program_id(0)
-    count = m2l_ref.shape[0]
+    recv_refs, parent_refs, (near_ref, out_ref) = refs[:8], refs[8:12], refs[12:14]
+    z_low, z_high, groups_low, groups_high, parents_low, parents_high = refs[14:20]
+    acc, rows_low, rows_high, recv_ref, target, window, table, sems, table_sems = refs[20:]
+    pieces = table_sems.shape[0]
+    kinds = table.shape[0]
+    span = kinds // pieces
     received = recv_ref.shape[0]
     cells = acc.shape[0]
     leaves = rows_low.shape[0]
     entries = far_ref.shape[0] // leaves
     coarse, _ = coarse_from_ref.shape
 
-    @pl.when(step == 0)
-    def _():
-        groups_low[...] = jnp.zeros(groups_low.shape, F32)
-        groups_high[...] = jnp.zeros(groups_high.shape, F32)
-        oct_size = parents_low.shape[0] // cells
-        before = 0
-        for part in parent_refs:
-            for k in range(part.shape[0] // cells):
-                owner = lax.rem(lax.axis_index("oct") + oct_size - before, oct_size)
-                at = pl.ds(pl.multiple_of(owner * cells, cells), cells)
-                piece = part[k * cells : (k + 1) * cells, :].astype(F32)
-                parents_low[at, :], parents_high[at, :] = piece[:, :128], piece[:, 128:]
-                before += 1
-        for k, part in enumerate(recv_refs):
-            recv_ref[k * 32 : (k + 1) * 32, :] = part[-32:, :]
-        acc[...] = jnp.zeros(acc.shape, F32)
-
-        def gather(q, carry):
-            for j in range(coarse):
-                at = pl.ds(coarse_to_ref[j, q] * cells + q, 1)
-                row = pl.ds(coarse_from_ref[j, q], 1)
-                groups_low[at, :] = groups_low[at, :] + parents_low[row, :]
-                groups_high[at, :] = groups_high[at, :] + parents_high[row, :]
+    loads = [
+        pltpu.make_async_copy(
+            m2l_ref.at[k * span : (k + 1) * span], table.at[k * span : (k + 1) * span],
+            table_sems.at[k],
+        )
+        for k in range(pieces)
+    ]
+    for load in loads:
+        load.start()
+    copies = load_window(begin, target_ref, [source_ref, after_ref], target, window, sems)
+    groups_low[...] = jnp.zeros(groups_low.shape, F32)
+    groups_high[...] = jnp.zeros(groups_high.shape, F32)
+    acc[...] = jnp.zeros(acc.shape, F32)
+    oct_size = parents_low.shape[0] // cells
+    before = 0
+    for part in parent_refs:
+        for k in range(part.shape[0] // cells):
+            owner = lax.rem(lax.axis_index("oct") + oct_size - before, oct_size)
+            at = pl.ds(pl.multiple_of(owner * cells, cells), cells)
+            piece = part[k * cells : (k + 1) * cells, :].astype(F32)
+            parents_low[at, :], parents_high[at, :] = piece[:, :128], piece[:, 128:]
+            before += 1
+    for k, part in enumerate(recv_refs):
+        recv_ref[k * 32 : (k + 1) * 32, :] = part[-32:, :]
+
+    def gather(q, carry):
+        for j in range(coarse):
+            at = pl.ds(coarse_to_ref[j, q] * cells + q, 1)
+            row = pl.ds(coarse_from_ref[j, q], 1)
+            groups_low[at, :] = groups_low[at, :] + parents_low[row, :]
+            groups_high[at, :] = groups_high[at, :] + parents_high[row, :]
+        return carry
+
+    lax.fori_loop(0, cells, gather, 0)
+    for k in range(pieces):
+        loads[k].wait()
+
+        def spread_out(t, carry):
+            kind = k * span + t
+            at = pl.ds(pl.multiple_of(kind * cells, cells), cells)
+            group = jnp.concatenate([groups_low[at, :], groups_high[at, :]], axis=1).astype(BF)
+            out = dot(recv_ref[...], table[kind])
+            at = pl.ds(pl.multiple_of(kind * received, received), received)
+            z_low[at, :] = out[:, :128]
+            z_high[at, :] = out[:, 128:]
+            acc[...] += dot(group, table[kind])
             return carry
 
-        lax.fori_loop(0, cells, gather, 0)
-
-    for t in range(count):
-        kind = step * count + t
-        at = pl.ds(pl.multiple_of(kind * cells, cells), cells)
-        group = jnp.concatenate([groups_low[at, :], groups_high[at, :]], axis=1).astype(BF)
-        table = m2l_ref[t]
-        out = dot(recv_ref[...], table)
-        at = pl.ds(pl.multiple_of(kind * received, received), received)
+        lax.fori_loop(0, span, spread_out, 0, unroll=True)
+    local = acc[...].astype(BF)
+    for c in range(8):
+        out = dot(local, l2l_ref[c])
+        at = pl.ds(received * kinds + c * cells, cells)
         z_low[at, :] = out[:, :128]
         z_high[at, :] = out[:, 128:]
-        acc[...] += dot(group, table)
-
-    @pl.when(step == pl.num_programs(0) - 1)
-    def _():
-        local = acc[...].astype(BF)
-        first = received * count * pl.num_programs(0)
-        for c in range(8):
-            out = dot(local, l2l_ref[c])
-            at = pl.ds(first + c * cells, cells)
-            z_low[at, :] = out[:, :128]
-            z_high[at, :] = out[:, 128:]
-
-        def block(group, carry):
-            for u in range(8):
+    for copy in copies:
+        copy.wait()
+    per = leaves // target.shape[0]
+
+    def body(group, carry):
+        first = group * 32
+
+        def add_rows(u):
+            for v in range(per):
+                leaf = first * per + u * per + v
                 lows, highs = [None] * 4, [None] * 4
                 for j in range(entries):
-                    at = pl.ds(far_ref[j * leaves + group * 8 + u], 1)
+                    at = pl.ds(far_ref[j * leaves + leaf], 1)
                     low, high = z_low[at, :], z_high[at, :]
                     k = j % 4
                     lows[k] = low if lows[k] is None else lows[k] + low
                     highs[k] = high if highs[k] is None else highs[k] + high
-                at = pl.ds(group * 8 + u, 1)
+                at = pl.ds(leaf, 1)
                 rows_low[at, :] = (lows[0] + lows[1]) + (lows[2] + lows[3])
                 rows_high[at, :] = (highs[0] + highs[1]) + (highs[2] + highs[3])
-            return carry
-
-        lax.fori_loop(0, leaves // 8, block, 0)
-        out_ref[:, :128] = rows_low[...].astype(BF)
-        out_ref[:, 128:] = rows_high[...].astype(BF)
+
+        own = (offset_ref, dir_ref, scale_ref, add_ref, target, window, near_ref)
+        near_leaves(begin, first, 32, own, add_rows)
+        return carry
+
+    lax.fori_loop(0, target.shape[0] // 32, body, 0)
+    out_ref[:, :128] = rows_low[...].astype(BF)
+    out_ref[:, 128:] = rows_high[...].astype(BF)
 
 
 def far_kernel(counts_ref, tile_ref, exp_ref, dens_ref, *refs):
@@ -357,17 +389,18 @@
     unroll = 16
     lane = lax.broadcasted_iota(jnp.int32, (unroll, 128), 1)
     row = lax.broadcasted_iota(jnp.int32, (unroll, 128), 0)
-    per = pl.num_programs(0) // len(near_refs)
     for group in range(leaves // unroll):
         at = pl.ds(group * unroll, unroll)
         out = dot(exp_ref[at, :], tile_ref[:, group * unroll * 128 : (group + 1) * unroll * 128])
         far = jnp.zeros((unroll, 128), F32)
         for u in range(unroll):
             far = jnp.where(row == u, out[:, u * 128 : (u + 1) * 128], far)
-        near = near_refs[0][pl.ds(pl.multiple_of(step % per * leaves + group * unroll, 16), 16), :]
-        for k in range(1, len(near_refs)):
-            other = near_refs[k][pl.ds(pl.multiple_of(step % per * leaves + group * unroll, 16), 16), :]
-            near = jnp.where(step // per == k, other, near)
+        near, begin = None, 0
+        for ref in near_refs:
+            at_near = jnp.clip(step * leaves + group * unroll - begin, 0, ref.shape[0] - unroll)
+            part = ref[pl.ds(pl.multiple_of(at_near, unroll), unroll), :]
+            near = part if near is None else jnp.where(step * leaves >= begin, part, near)
+            begin += ref.shape[0]
         value = 0.5 * dens_ref[at, :] + near + far * (1.0 / math.sqrt(256))
         counts = spread(counts_ref, step * leaves + group * unroll, unroll)
         out_ref[at, :] = jnp.where(lane < counts, value, 0.0)
@@ -396,7 +429,7 @@
 
     steps = 8
     block = leaves // steps
-    chunk = leaves // 4
+    chunk = leaves // 8
     target, source, tile, first, last, *send = pl.pallas_call(
         functools.partial(moments_kernel, (oct_size, leaf_size)),
         grid=(steps,),
@@ -425,8 +458,8 @@
             pltpu.VMEM((block, 128), F32),
             pltpu.VMEM((leaves, 128), F32),
             pltpu.VMEM((leaves, 128), F32),
-            pltpu.VMEM((8 * ROWS, panels), F32),
-            pltpu.VMEM((8 * ROWS, panels), F32),
+            pltpu.VMEM((8 * PITCH, panels), F32),
+            pltpu.VMEM((8 * PITCH, panels), F32),
         ],
         compiler_params=params(),
         name="moments",
@@ -435,34 +468,26 @@
     offsets = near_offset.T
     ways = near_dir.T
 
+    spaces = [SMEM, SMEM, VMEM, VMEM, pl.BlockSpec(memory_space=pl.ANY)]
+
     def near_part(begin):
-        if begin == 0:
-            parts = [before, source]
-        elif begin + chunk == leaves:
-            parts = [source, after]
-        else:
-            parts = [source]
+        parts = [before, source] if begin == 0 else [source]
         return pl.pallas_call(
             functools.partial(near_kernel, begin),
-            grid=(1,),
-            in_specs=[
-                SMEM, SMEM,
-                pl.BlockSpec((chunk, ROWS, panels), lambda i: (begin // chunk, 0, 0)),
-            ]
-            + [pl.BlockSpec(memory_space=pl.ANY)] * len(parts)
-            + [VMEM, VMEM],
+            in_specs=spaces + [pl.BlockSpec(memory_space=pl.ANY)] * len(parts),
             out_specs=VMEM,
             out_shape=jax.ShapeDtypeStruct((chunk, panels), F32),
             scratch_shapes=[
+                pltpu.VMEM((chunk, ROWS, panels), BF),
                 pltpu.VMEM((chunk + 2 * HW, ROWS, panels), BF),
-                pltpu.SemaphoreType.DMA((2,)),
+                pltpu.SemaphoreType.DMA((3,)),
             ],
             compiler_params=params(),
             cost_estimate=pl.CostEstimate(
                 flops=10**10, bytes_accessed=10**6, transcendentals=chunk * 2 * 65536
             ),
             name="near",
-        )(offsets, ways, target, *parts, scale, add)
+        )(offsets, ways, scale, add, target, *parts)
 
     def shifted(value, axis, by):
         size = lax.axis_size(axis)
@@ -482,28 +507,29 @@
     by_two = shifted(send[0], "leaf", 2)
     by_one = shifted(send[1], "leaf", 1)
     by_three = shifted(partial, "leaf", 3)
-    back_one, back_two = moved(send[3], -1), moved(send[4], -2)
     before, after = moved(last, 1), moved(first, -1)
     near = [None] * 4
     near[1] = near_part(chunk)
-    near[1], by_one, by_two, by_three, back_one, back_two, before, after = lax.optimization_barrier(
-        (near[1], by_one, by_two, by_three, back_one, back_two, before, after)
+    near[1], by_one, by_two, by_three, before, after = lax.optimization_barrier(
+        (near[1], by_one, by_two, by_three, before, after)
     )
     four = added([partial, by_one[:cells], by_two[:cells], by_three])
     strides = [shifted(four, "leaf", by) for by in (4, 8, 12)]
+    back_one, back_two = moved(send[3], -1), moved(send[4], -2)
+    four, source, target = lax.optimization_barrier((four, source, target))
+    near[0] = near_part(0)
+    near[0], four, back_one, back_two, *strides = lax.optimization_barrier(
+        (near[0], four, back_one, back_two, *strides)
+    )
+    total = added([four, *strides])
+    lower = shifted(total, "oct", 1)
     across = [
         shifted(send[5], "oct", -1), shifted(send[6], "oct", 1),
         shifted(send[7], "oct", oct_size // 2),
     ]
-    four, source, target = lax.optimization_barrier((four, source, target))
+    total, source, target = lax.optimization_barrier((total, source, target))
     near[2] = near_part(2 * chunk)
-    near[2], four, *moving = lax.optimization_barrier((near[2], four, *strides, *across))
-    strides, across = moving[:3], moving[3:]
-    total = added([four, *strides])
-    lower = shifted(total, "oct", 1)
-    total, source, target = lax.optimization_barrier((total, source, target))
-    near[0] = near_part(0)
-    near[0], total, lower = lax.optimization_barrier((near[0], total, lower))
+    near[2], total, lower, *across = lax.optimization_barrier((near[2], total, lower, *across))
     pair = jnp.concatenate([total, lower], axis=0)
     pairs = [shifted(pair, "oct", by) for by in (2, 4, 6)]
     pair, source, target = lax.optimization_barrier((pair, source, target))
@@ -526,20 +552,16 @@
     far_rows = (far_type * 8 + partner) * cap + slot
     own_row = kinds * 8 * cap + child_pos * cells + leaf_parent
     far_rows = jnp.concatenate([far_rows.T.reshape(-1), own_row])
-    span = 8
-    expansions = pl.pallas_call(
-        translate_kernel,
-        grid=(kinds // span,),
-        in_specs=[
-            SMEM, SMEM, SMEM,
-        ]
-        + [VMEM] * 12
-        + [
-            pl.BlockSpec((span, width, width), lambda i: (i, 0, 0)),
-            VMEM,
+    rest = leaves - 4 * chunk
+    any_space = pl.BlockSpec(memory_space=pl.ANY)
+    last_near, expansions = pl.pallas_call(
+        functools.partial(translate_kernel, 4 * chunk),
+        in_specs=[SMEM] * 5 + [VMEM] * 3 + [any_space] * 4 + [VMEM] * 12,
+        out_specs=[VMEM, VMEM],
+        out_shape=[
+            jax.ShapeDtypeStruct((rest, panels), F32),
+            jax.ShapeDtypeStruct((leaves, width), BF),
         ],
-        out_specs=VMEM,
-        out_shape=jax.ShapeDtypeStruct((leaves, width), BF),
         scratch_shapes=[
             pltpu.VMEM((kinds * 8 * cap + 8 * cells, 128), F32),
             pltpu.VMEM((kinds * 8 * cap + 8 * cells, 128), F32),
@@ -551,10 +573,19 @@
             pltpu.VMEM((leaves, 128), F32),
             pltpu.VMEM((leaves, 128), F32),
             pltpu.VMEM((8 * cap, width), BF),
+            pltpu.VMEM((rest, ROWS, panels), BF),
+            pltpu.VMEM((rest + 2 * HW, ROWS, panels), BF),
+            pltpu.VMEM(m2l.shape, BF),
+            pltpu.SemaphoreType.DMA((3,)),
+            pltpu.SemaphoreType.DMA((8,)),
         ],
         compiler_params=params(),
         name="translate",
-    )(far_rows, coarse_source.T, coarse_type.T, *received, *every_parent, m2l, l2l)
+    )(
+        offsets, ways, far_rows, coarse_source.T, coarse_type.T, scale, add, l2l,
+        target, source, after, m2l, *received, *every_parent,
+    )
+    near.append(last_near)
 
     return pl.pallas_call(
         far_kernel,

time: 183 us -> 163 us (0.89)
  Pallas kernels: 140 us -> 125 us
  waiting for transfers between devices: 4.22 us -> 0.04 us
    pallas_call x1, Pallas kernels: 38.6 us -> 29.9 us  [local(): pl.pallas_call(functools.partial(moments_kernel, (oct_size, leaf_size)),...]
    pallas_call x5, Pallas kernels: 87.4 us -> 80.6 us  [the longest x1 48.2 us: local(): pl.pallas_call(functools.partial(translate_kernel, 4 * chunk), in_specs=[...]
    ppermute x13, waiting for transfers between devices: 4.21 us -> 0.03 us  [shifted(): lax.ppermute(value, axis, [(i, (i + by) % size) for i in range(size)])]
    ppermute x13, starting transfers between devices: 28.6 us -> 26.1 us  [shifted(): lax.ppermute(value, axis, [(i, (i + by) % size) for i in range(size)])]
  transfers between devices with their start and end apart: 17 -> 17, of which waited for: 1 -> 0; matrix products, arithmetic and copies ran while one was open for 0% -> 1% of each run, Pallas kernels for 30% -> 20%
where the time goes in v4:
time: 163 us; the launch traced here: 162 us
  Pallas kernels  125 us (77%)
  starting transfers between devices  33.5 us (21%)
  other arithmetic  2.1 us (1%)
    pallas_call x1, Pallas kernels, local(): pl.pallas_call(functools.partial(translate_kernel, 4 * chunk), in_specs=[...  48.2 us
    pallas_call x4, Pallas kernels, near_part(): pl.pallas_call(functools.partial(near_kernel, begin), in_specs=spaces + [...  32.5 us
    pallas_call x1, Pallas kernels, local(): pl.pallas_call(functools.partial(moments_kernel, (oct_size, leaf_size)),...  29.9 us
    ppermute x13, starting transfers between devices, shifted(): lax.ppermute(value, axis, [(i, (i + by) % size) for i in range(size)])  26.1 us
    pallas_call x1, Pallas kernels, local(): pl.pallas_call(far_kernel, grid=(steps,), in_specs=[SMEM, pl.BlockSpec((w...  14.4 us
    ppermute x4, starting transfers between devices, moved(): return lax.ppermute(value, 'leaf', pairs)  7.38 us
  transfers between devices with their start and end apart: 17, of which 0 were waited for; matrix products, arithmetic and copies ran while one was open for 1% of the time, Pallas kernels for 20%

profile of v4, /device:TPU:1, one launch (start us, length us, event | category | flops | bytes accessed | tf_op | source)
XLA Modules:
  0.0 161.8 jit_solution(14649202598457849730)
XLA Ops:
  0.0 1.3 add_add_fusion
  1.3 29.9 %moments.1 = (bf16[512,32,128]{2,1,0:T(8,128)(2,1)}, bf16[512,32,128]{2,1,0:T(8,128)(2,1)}, bf16[256,65536]{1,0:T(8,128)(2,1)}, bf16[32,32,128]{2,1,0:T(8,128)(2...) custom-call(s32[32,128]{1,0:T(8,128)} %bitcast.12, ...), custom_call_target="tpu_custom_call" | custom-call | tf_op jit(solution)/shard_map/moments/pallas_call | solution.py:433
  31.2 3.7 %collective-permute-start.2 = (bf16[64,256]{1,0:T(8,128)(2,1)}, bf16[64,256]{1,0:T(8,128)(2,1)S(1)}, u32[]{:S(2)}, u32[]{:S(2)}) collective-permute-start(bf16[64,256]{1,0:T(8,128)(2,1)} %get-tuple-element.55), channel_id=1, source_target_pairs={{0,3},{1,4},{2,5},{3,6},{4,7},{5,8},{6,9},{7,10},{8,11},{9,12},{10... | collective-permute-start | bytes 98312 | tf_op jit(solution)/shard_map/ppermute | solution.py:494
  34.9 0.1 collective-permute-start
  35.0 2.9 %collective-permute-start.1 = (bf16[96,256]{1,0:T(8,128)(2,1)}, bf16[96,256]{1,0:T(8,128)(2,1)S(1)}, u32[]{:S(2)}, u32[]{:S(2)}) collective-permute-start(bf16[96,256]{1,0:T(8,128)(2,1)} %get-tuple-element.59), channel_id=1, source_target_pairs={{0,2},{1,3},{2,4},{3,5},{4,6},{5,7},{6,8},{7,9},{8,10},{9,11},{10,... | collective-permute-start | bytes 147464 | tf_op jit(solution)/shard_map/ppermute | solution.py:494
  37.8 3.5 %collective-permute-start.3 = (bf16[32,32,128]{2,1,0:T(8,128)(2,1)}, bf16[32,32,128]{2,1,0:T(8,128)(2,1)S(1)}, u32[]{:S(2)}, u32[]{:S(2)}) collective-permute-start(bf16[32,32,128]{2,1,0:T(8,128)(2,1)} %get-tuple-element.60), channel_id=1, source_target_pairs={{0,1},{1,2},{2,3},{3,4},{4,5},{5,6},{6,7},{7,8},{8,9},{9,10},{10,1... | collective-permute-start | bytes 786440 | tf_op jit(solution)/shard_map/ppermute | solution.py:498
  41.4 1.3 collective-permute-start.4
  42.7 0.0 copy-start.7
  42.7 0.0 copy-start.8
  42.7 8.2 %near.4.refs_1_ = f32[64,128]{1,0:T(8,128)} custom-call(s32[4,512]{1,0:T(4,128)} %bitcast.13, s32[4,512]{1,0:T(4,128)} %bitcast.18, bf16[27,32,128]{2,1,0:T(8,128)(2,1)} %constant.95.clone.scale_ref, bf16[27,32,128]{2,1,0:T(8,128)(2,1)} %constant.96.clone.add_ref, bf16[512,32,128]{2,1,0:T(8,128)(2,1)} %get-tuple-element.83.target_ref, ...), custom_call_target="tpu_custom_call" | custom-call | flops 10000000000 | bytes 1000000 | tf_op jit(solution)/shard_map/near/pallas_call | solution.py:475
  50.9 0.1 fusion.6
  51.1 0.6 pad_add_fusion.far_ref
  51.7 0.0 collective-permute-done.2
  51.7 1.3 collective-permute-start.5
  53.0 0.0 collective-permute-done.refs_1_
  53.0 1.3 collective-permute-start.6
  54.3 0.0 collective-permute-done.1.refs_0_
  54.4 0.0 collective-permute-done.3.refs_0_
  54.4 0.0 collective-permute-done.4.after_ref
  54.4 0.0 copy-start
  54.5 8.5 %collective-permute-start.9 = (bf16[64,256]{1,0:T(8,128)(2,1)S(1)}, bf16[64,256]{1,0:T(8,128)(2,1)S(1)}, u32[]{:S(2)}, u32[]{:S(2)}) collective-permute-start(bf16[64,256]{1,0:T(8,128)(2,1)S(1)} %add_convert_fusion.1), channel_id=1, source_target_pairs={{0,12},{1,13},{2,14},{3,15},{4,0},{5,1},{6,2},{7,3},{8,4},{9,5},{1... | collective-permute-start | bytes 98312 | tf_op jit(solution)/shard_map/ppermute | solution.py:494
  63.0 0.0 collective-permute-start.8
  63.0 0.7 collective-permute-start.7
  63.7 8.1 %near.5.refs_0_ = f32[64,128]{1,0:T(8,128)} custom-call(s32[4,512]{1,0:T(4,128)} %bitcast.14, s32[4,512]{1,0:T(4,128)} %bitcast.19, bf16[27,32,128]{2,1,0:T(8,128)(2,1)} %constant.95.clone.scale_ref, bf16[27,32,128]{2,1,0:T(8,128)(2,1)} %constant.96.clone.add_ref, bf16[512,32,128]{2,1,0:T(8,128)(2,1)} %get-tuple-element.83.target_ref, ...), custom_call_target="tpu_custom_call" | custom-call | flops 10000000000 | bytes 1000000 | tf_op jit(solution)/shard_map/near/pallas_call | solution.py:475
  71.8 0.0 collective-permute-done.5.refs_3_
  71.8 3.5 %collective-permute-start.11 = (bf16[32,256]{1,0:T(8,128)(2,1)S(1)}, bf16[32,256]{1,0:T(8,128)(2,1)S(1)}, u32[]{:S(2)}, u32[]{:S(2)}) collective-permute-start(bf16[32,256]{1,0:T(8,128)(2,1)S(1)} %copy-done.18), channel_id=1, source_target_pairs={{0,112},{16,0},{32,16},{48,32},{64,48},{80,64},{96,80},{112,96},{1... | collective-permute-start | bytes 49160 | tf_op jit(solution)/shard_map/ppermute | solution.py:494
  75.3 0.0 collective-permute-done.6.refs_4_
  75.4 1.1 collective-permute-start.12
  76.4 0.0 collective-permute-done.9
  76.4 2.5 %collective-permute-start.13 = (bf16[32,256]{1,0:T(8,128)(2,1)S(1)}, bf16[32,256]{1,0:T(8,128)(2,1)S(1)}, u32[]{:S(2)}, u32[]{:S(2)}) collective-permute-start(bf16[32,256]{1,0:T(8,128)(2,1)S(1)} %copy-done.16), channel_id=1, source_target_pairs={{0,64},{16,80},{32,96},{48,112},{64,0},{80,16},{96,32},{112,48},{1... | collective-permute-start | bytes 49160 | tf_op jit(solution)/shard_map/ppermute | solution.py:494
  79.0 0.0 collective-permute-done.8
  79.0 0.0 collective-permute-done.7
  79.0 0.2 collective-permute-start.10
  79.1 8.1 %near.6.refs_2_ = f32[64,128]{1,0:T(8,128)} custom-call(s32[4,512]{1,0:T(4,128)} %bitcast.15, s32[4,512]{1,0:T(4,128)} %bitcast.20, bf16[27,32,128]{2,1,0:T(8,128)(2,1)} %constant.95.clone.scale_ref, bf16[27,32,128]{2,1,0:T(8,128)(2,1)} %constant.96.clone.add_ref, bf16[512,32,128]{2,1,0:T(8,128)(2,1)} %get-tuple-element.83.target_ref, ...), custom_call_target="tpu_custom_call" | custom-call | flops 10000000000 | bytes 1000000 | tf_op jit(solution)/shard_map/near/pallas_call | solution.py:475
  87.3 0.0 collective-permute-done.11.refs_5_
  87.3 0.0 collective-permute-done.12.refs_6_
  87.3 0.0 collective-permute-done.13.refs_7_
  87.3 0.0 collective-permute-done.10
  87.4 2.4 %collective-permute-start.16 = (bf16[128,256]{1,0:T(8,128)(2,1)S(1)}, bf16[128,256]{1,0:T(8,128)(2,1)S(1)}, u32[]{:S(2)}, u32[]{:S(2)}) collective-permute-start(bf16[128,256]{1,0:T(8,128)(2,1)S(1)} %constant_dynamic-update-slice_fusion.refs_8_), channel_id=1, source_target_pairs={{0,96},{16,112},{32,0},{48,16},{64,32},{80,48},{96,64},{112,80},{1... | collective-permute-start | bytes 196616 | tf_op jit(solution)/shard_map/ppermute | solution.py:494
  89.8 0.7 collective-permute-start.14
  90.4 8.1 %near.7.refs_3_ = f32[64,128]{1,0:T(8,128)} custom-call(s32[4,512]{1,0:T(4,128)} %bitcast.16, s32[4,512]{1,0:T(4,128)} %bitcast.21, bf16[27,32,128]{2,1,0:T(8,128)(2,1)} %constant.95.clone.scale_ref, bf16[27,32,128]{2,1,0:T(8,128)(2,1)} %constant.96.clone.add_ref, bf16[512,32,128]{2,1,0:T(8,128)(2,1)} %get-tuple-element.83.target_ref, ...), custom_call_target="tpu_custom_call" | custom-call | flops 10000000000 | bytes 1000000 | tf_op jit(solution)/shard_map/near/pallas_call | solution.py:475
  98.6 0.0 collective-permute-done.16.refs_11_
  98.6 0.0 collective-permute-done.15.refs_10_
  98.7 0.6 copy-done.4
  99.2 0.0 copy-done.5
  99.3 0.0 copy-done.6
  99.3 48.2 %translate.1 = (f32[256,128]{1,0:T(8,128)}, bf16[512,256]{1,0:T(8,128)(2,1)}) custom-call(s32[4,512]{1,0:T(4,128)} %bitcast.17, s32[4,512]{1,0:T(4,128)} %bitcast.22, s32[14336]{0:T(1024)} %pad_add_fusion.far_ref, s32[16,64]{1,0:T(8,128)} %bitcast.23, s32[16,64]{1,0:T(8,128)} %bitcast.24, bf16[27,32,128]{2,1,0:T(8,128)(2,1)} %constant.95.clone.scale_ref, ...), custom_call_target="tpu_custom_call" | custom-call | tf_op jit(solution)/shard_map/translate/pallas_call | solution.py:557
  147.5 14.4 %far.1 = f32[512,128]{1,0:T(8,128)} custom-call(s32[512]{0:T(512)} %counts_ref.3, bf16[256,65536]{1,0:T(8,128)(2,1)} %get-tuple-element.54.tile_ref, bf16[512,256]{1,0:T(8,128)(2,1)} %get-tuple-element.97.exp_ref, f32[512,128]{1,0:T(8,128)} %dens_ref.3, f32[64,128]{1,0:T(8,128)} %near.5.refs_0_, f32[64,128]{1,0:T(8,128)} %near.4.refs_1_, ...), custom_call_target="tpu_custom_call" | custom-call | tf_op jit(solution)/shard_map/far/pallas_call | solution.py:590
  (43 shorter events, 0.1 us)
Async XLA Ops:
  31.2 20.5 %collective-permute-start.2 = (bf16[64,256]{1,0:T(8,128)(2,1)}, bf16[64,256]{1,0:T(8,128)(2,1)S(1)}, u32[]{:S(2)}, u32[]{:S(2)}) collective-permute-start(bf16[64,256]{1,0:T(8,128)(2,1)} %get-tuple-element.55), channel_id=1, source_target_pairs={{0,3},{1,4},{2,5},{3,6},{4,7},{5,8},{6,9},{7,10},{8,11},{9,12},{10... | collective-permute-start | bytes 98312 | tf_op jit(solution)/shard_map/ppermute | solution.py:494
  34.9 18.1 %collective-permute-start = (bf16[96,256]{1,0:T(8,128)(2,1)}, bf16[96,256]{1,0:T(8,128)(2,1)S(1)}, u32[]{:S(2)}, u32[]{:S(2)}) collective-permute-start(bf16[96,256]{1,0:T(8,128)(2,1)} %get-tuple-element.58), channel_id=1, source_target_pairs={{0,1},{1,2},{2,3},{3,4},{4,5},{5,6},{6,7},{7,8},{8,9},{9,10},{10,1... | collective-permute-start | bytes 147464 | tf_op jit(solution)/shard_map/ppermute | solution.py:494
  35.0 19.4 %collective-permute-start.1 = (bf16[96,256]{1,0:T(8,128)(2,1)}, bf16[96,256]{1,0:T(8,128)(2,1)S(1)}, u32[]{:S(2)}, u32[]{:S(2)}) collective-permute-start(bf16[96,256]{1,0:T(8,128)(2,1)} %get-tuple-element.59), channel_id=1, source_target_pairs={{0,2},{1,3},{2,4},{3,5},{4,6},{5,7},{6,8},{7,9},{8,10},{9,11},{10,... | collective-permute-start | bytes 147464 | tf_op jit(solution)/shard_map/ppermute | solution.py:494
  37.8 16.5 %collective-permute-start.3 = (bf16[32,32,128]{2,1,0:T(8,128)(2,1)}, bf16[32,32,128]{2,1,0:T(8,128)(2,1)S(1)}, u32[]{:S(2)}, u32[]{:S(2)}) collective-permute-start(bf16[32,32,128]{2,1,0:T(8,128)(2,1)} %get-tuple-element.60), channel_id=1, source_target_pairs={{0,1},{1,2},{2,3},{3,4},{4,5},{5,6},{6,7},{7,8},{8,9},{9,10},{10,1... | collective-permute-start | bytes 786440 | tf_op jit(solution)/shard_map/ppermute | solution.py:498
  41.4 13.0 %collective-permute-start.4 = (bf16[32,32,128]{2,1,0:T(8,128)(2,1)}, bf16[32,32,128]{2,1,0:T(8,128)(2,1)S(1)}, u32[]{:S(2)}, u32[]{:S(2)}) collective-permute-start(bf16[32,32,128]{2,1,0:T(8,128)(2,1)} %get-tuple-element.61), channel_id=1, source_target_pairs={{1,0},{2,1},{3,2},{4,3},{5,4},{6,5},{7,6},{8,7},{9,8},{10,9},{11,1... | collective-permute-start | bytes 786440 | tf_op jit(solution)/shard_map/ppermute | solution.py:498
  42.7 8.2 %copy-start.7 = (s32[512,27]{0,1:T(8,128)S(1)}, s32[512,27]{0,1:T(8,128)}, u32[]{:S(2)}) copy-start(s32[512,27]{0,1:T(8,128)} %param.25) | copy-start | bytes 165892
  42.7 8.2 %copy-start.8 = (s32[512,27]{0,1:T(8,128)S(1)}, s32[512,27]{0,1:T(8,128)}, u32[]{:S(2)}) copy-start(s32[512,27]{0,1:T(8,128)} %param.24) | copy-start | bytes 165892
  42.7 9.0 %copy-start.20 = (bf16[32,256]{1,0:T(8,128)(2,1)S(1)}, bf16[32,256]{1,0:T(8,128)(2,1)}, u32[]{:S(2)}) copy-start(bf16[32,256]{1,0:T(8,128)(2,1)} %get-tuple-element.69) | copy-start | bytes 49156
  42.7 10.3 %copy-start.19 = (bf16[32,256]{1,0:T(8,128)(2,1)S(1)}, bf16[32,256]{1,0:T(8,128)(2,1)}, u32[]{:S(2)}) copy-start(bf16[32,256]{1,0:T(8,128)(2,1)} %get-tuple-element.70) | copy-start | bytes 49156
  42.7 11.7 %copy-start.9 = (bf16[64,256]{1,0:T(8,128)(2,1)S(1)}, bf16[64,256]{1,0:T(8,128)(2,1)}, u32[]{:S(2)}) copy-start(bf16[64,256]{1,0:T(8,128)(2,1)} %get-tuple-element.55) | copy-start | bytes 98308
  51.7 20.1 %collective-permute-start.5 = (bf16[32,256]{1,0:T(8,128)(2,1)S(1)}, bf16[32,256]{1,0:T(8,128)(2,1)S(1)}, u32[]{:S(2)}, u32[]{:S(2)}) collective-permute-start(bf16[32,256]{1,0:T(8,128)(2,1)S(1)} %copy-done.20), channel_id=1, source_target_pairs={{1,0},{2,1},{3,2},{4,3},{5,4},{6,5},{7,6},{8,7},{9,8},{10,9},{11,1... | collective-permute-start | bytes 49160 | tf_op jit(solution)/shard_map/ppermute | solution.py:498
  53.0 18.7 %copy-start.2 = (bf16[96,256]{1,0:T(8,128)(2,1)}, bf16[96,256]{1,0:T(8,128)(2,1)S(1)}, u32[]{:S(2)}) copy-start(bf16[96,256]{1,0:T(8,128)(2,1)S(1)} %collective-permute-done.refs_1_) | copy-start | bytes 147460
  53.0 22.3 %collective-permute-start.6 = (bf16[32,256]{1,0:T(8,128)(2,1)S(1)}, bf16[32,256]{1,0:T(8,128)(2,1)S(1)}, u32[]{:S(2)}, u32[]{:S(2)}) collective-permute-start(bf16[32,256]{1,0:T(8,128)(2,1)S(1)} %copy-done.19), channel_id=1, source_target_pairs={{2,0},{3,1},{4,2},{5,3},{6,4},{7,5},{8,6},{9,7},{10,8},{11,9},{12,... | collective-permute-start | bytes 49160 | tf_op jit(solution)/shard_map/ppermute | solution.py:498
  54.4 17.4 %copy-start.3 = (bf16[96,256]{1,0:T(8,128)(2,1)}, bf16[96,256]{1,0:T(8,128)(2,1)S(1)}, u32[]{:S(2)}) copy-start(bf16[96,256]{1,0:T(8,128)(2,1)S(1)} %collective-permute-done.1.refs_0_) | copy-start | bytes 147460
  54.4 9.3 %copy-start.15 = (bf16[32,32,128]{2,1,0:T(8,128)(2,1)}, bf16[32,32,128]{2,1,0:T(8,128)(2,1)S(1)}, u32[]{:S(2)}) copy-start(bf16[32,32,128]{2,1,0:T(8,128)(2,1)S(1)} %collective-permute-done.3.refs_0_) | copy-start | bytes 786436
  54.4 17.4 %copy-start = (bf16[32,32,128]{2,1,0:T(8,128)(2,1)}, bf16[32,32,128]{2,1,0:T(8,128)(2,1)S(1)}, u32[]{:S(2)}) copy-start(bf16[32,32,128]{2,1,0:T(8,128)(2,1)S(1)} %collective-permute-done.4.after_ref) | copy-start | bytes 786436
  54.5 17.4 %copy-start.18 = (bf16[32,256]{1,0:T(8,128)(2,1)S(1)}, bf16[32,256]{1,0:T(8,128)(2,1)}, u32[]{:S(2)}) copy-start(bf16[32,256]{1,0:T(8,128)(2,1)} %get-tuple-element.78) | copy-start | bytes 49156
  54.5 20.9 %copy-start.17 = (bf16[32,256]{1,0:T(8,128)(2,1)S(1)}, bf16[32,256]{1,0:T(8,128)(2,1)}, u32[]{:S(2)}) copy-start(bf16[32,256]{1,0:T(8,128)(2,1)} %get-tuple-element.79) | copy-start | bytes 49156
  54.5 22.0 %copy-start.16 = (bf16[32,256]{1,0:T(8,128)(2,1)S(1)}, bf16[32,256]{1,0:T(8,128)(2,1)}, u32[]{:S(2)}) copy-start(bf16[32,256]{1,0:T(8,128)(2,1)} %get-tuple-element.80) | copy-start | bytes 49156
  54.5 22.0 %collective-permute-start.9 = (bf16[64,256]{1,0:T(8,128)(2,1)S(1)}, bf16[64,256]{1,0:T(8,128)(2,1)S(1)}, u32[]{:S(2)}, u32[]{:S(2)}) collective-permute-start(bf16[64,256]{1,0:T(8,128)(2,1)S(1)} %add_convert_fusion.1), channel_id=1, source_target_pairs={{0,12},{1,13},{2,14},{3,15},{4,0},{5,1},{6,2},{7,3},{8,4},{9,5},{1... | collective-permute-start | bytes 98312 | tf_op jit(solution)/shard_map/ppermute | solution.py:494
  63.0 16.0 %collective-permute-start.8 = (bf16[64,256]{1,0:T(8,128)(2,1)S(1)}, bf16[64,256]{1,0:T(8,128)(2,1)S(1)}, u32[]{:S(2)}, u32[]{:S(2)}) collective-permute-start(bf16[64,256]{1,0:T(8,128)(2,1)S(1)} %add_convert_fusion.1), channel_id=1, source_target_pairs={{0,8},{1,9},{2,10},{3,11},{4,12},{5,13},{6,14},{7,15},{8,0},{9,1},... | collective-permute-start | bytes 98312 | tf_op jit(solution)/shard_map/ppermute | solution.py:494
  63.0 16.0 %collective-permute-start.7 = (bf16[64,256]{1,0:T(8,128)(2,1)S(1)}, bf16[64,256]{1,0:T(8,128)(2,1)S(1)}, u32[]{:S(2)}, u32[]{:S(2)}) collective-permute-start(bf16[64,256]{1,0:T(8,128)(2,1)S(1)} %add_convert_fusion.1), channel_id=1, source_target_pairs={{0,4},{1,5},{2,6},{3,7},{4,8},{5,9},{6,10},{7,11},{8,12},{9,13},{1... | collective-permute-start | bytes 98312 | tf_op jit(solution)/shard_map/ppermute | solution.py:494
  71.8 15.5 %copy-start.10 = (bf16[32,256]{1,0:T(8,128)(2,1)}, bf16[32,256]{1,0:T(8,128)(2,1)S(1)}, u32[]{:S(2)}) copy-start(bf16[32,256]{1,0:T(8,128)(2,1)S(1)} %collective-permute-done.5.refs_3_) | copy-start | bytes 49156
  71.8 15.5 %collective-permute-start.11 = (bf16[32,256]{1,0:T(8,128)(2,1)S(1)}, bf16[32,256]{1,0:T(8,128)(2,1)S(1)}, u32[]{:S(2)}, u32[]{:S(2)}) collective-permute-start(bf16[32,256]{1,0:T(8,128)(2,1)S(1)} %copy-done.18), channel_id=1, source_target_pairs={{0,112},{16,0},{32,16},{48,32},{64,48},{80,64},{96,80},{112,96},{1... | collective-permute-start | bytes 49160 | tf_op jit(solution)/shard_map/ppermute | solution.py:494
  75.4 11.9 %copy-start.11 = (bf16[32,256]{1,0:T(8,128)(2,1)}, bf16[32,256]{1,0:T(8,128)(2,1)S(1)}, u32[]{:S(2)}) copy-start(bf16[32,256]{1,0:T(8,128)(2,1)S(1)} %collective-permute-done.6.refs_4_) | copy-start | bytes 49156
  75.4 11.9 %collective-permute-start.12 = (bf16[32,256]{1,0:T(8,128)(2,1)S(1)}, bf16[32,256]{1,0:T(8,128)(2,1)S(1)}, u32[]{:S(2)}, u32[]{:S(2)}) collective-permute-start(bf16[32,256]{1,0:T(8,128)(2,1)S(1)} %copy-done.17), channel_id=1, source_target_pairs={{0,16},{16,32},{32,48},{48,64},{64,80},{80,96},{96,112},{112,0},{1... | collective-permute-start | bytes 49160 | tf_op jit(solution)/shard_map/ppermute | solution.py:494
  76.4 10.9 %collective-permute-start.13 = (bf16[32,256]{1,0:T(8,128)(2,1)S(1)}, bf16[32,256]{1,0:T(8,128)(2,1)S(1)}, u32[]{:S(2)}, u32[]{:S(2)}) collective-permute-start(bf16[32,256]{1,0:T(8,128)(2,1)S(1)} %copy-done.16), channel_id=1, source_target_pairs={{0,64},{16,80},{32,96},{48,112},{64,0},{80,16},{96,32},{112,48},{1... | collective-permute-start | bytes 49160 | tf_op jit(solution)/shard_map/ppermute | solution.py:494
  79.0 8.4 %collective-permute-start.10 = (bf16[64,256]{1,0:T(8,128)(2,1)S(1)}, bf16[64,256]{1,0:T(8,128)(2,1)S(1)}, u32[]{:S(2)}, u32[]{:S(2)}) collective-permute-start(bf16[64,256]{1,0:T(8,128)(2,1)S(1)} %add_convert_fusion), channel_id=1, source_target_pairs={{0,16},{16,32},{32,48},{48,64},{64,80},{80,96},{96,112},{112,0},{1... | collective-permute-start | bytes 98312 | tf_op jit(solution)/shard_map/ppermute | solution.py:494
  87.3 11.3 %copy-start.12 = (bf16[32,256]{1,0:T(8,128)(2,1)}, bf16[32,256]{1,0:T(8,128)(2,1)S(1)}, u32[]{:S(2)}) copy-start(bf16[32,256]{1,0:T(8,128)(2,1)S(1)} %collective-permute-done.11.refs_5_) | copy-start | bytes 49156
  87.3 11.3 %copy-start.13 = (bf16[32,256]{1,0:T(8,128)(2,1)}, bf16[32,256]{1,0:T(8,128)(2,1)S(1)}, u32[]{:S(2)}) copy-start(bf16[32,256]{1,0:T(8,128)(2,1)S(1)} %collective-permute-done.12.refs_6_) | copy-start | bytes 49156
  87.3 11.2 %copy-start.14 = (bf16[32,256]{1,0:T(8,128)(2,1)}, bf16[32,256]{1,0:T(8,128)(2,1)S(1)}, u32[]{:S(2)}) copy-start(bf16[32,256]{1,0:T(8,128)(2,1)S(1)} %collective-permute-done.13.refs_7_) | copy-start | bytes 49156
  87.4 11.2 %copy-start.1 = (bf16[128,256]{1,0:T(8,128)(2,1)}, bf16[128,256]{1,0:T(8,128)(2,1)S(1)}, u32[]{:S(2)}) copy-start(bf16[128,256]{1,0:T(8,128)(2,1)S(1)} %constant_dynamic-update-slice_fusion.refs_8_) | copy-start | bytes 196612
  87.4 11.2 %collective-permute-start.16 = (bf16[128,256]{1,0:T(8,128)(2,1)S(1)}, bf16[128,256]{1,0:T(8,128)(2,1)S(1)}, u32[]{:S(2)}, u32[]{:S(2)}) collective-permute-start(bf16[128,256]{1,0:T(8,128)(2,1)S(1)} %constant_dynamic-update-slice_fusion.refs_8_), channel_id=1, source_target_pairs={{0,96},{16,112},{32,0},{48,16},{64,32},{80,48},{96,64},{112,80},{1... | collective-permute-start | bytes 196616 | tf_op jit(solution)/shard_map/ppermute | solution.py:494
  89.8 8.9 %collective-permute-start.15 = (bf16[128,256]{1,0:T(8,128)(2,1)S(1)}, bf16[128,256]{1,0:T(8,128)(2,1)S(1)}, u32[]{:S(2)}, u32[]{:S(2)}) collective-permute-start(bf16[128,256]{1,0:T(8,128)(2,1)S(1)} %constant_dynamic-update-slice_fusion.refs_8_), channel_id=1, source_target_pairs={{0,64},{16,80},{32,96},{48,112},{64,0},{80,16},{96,32},{112,48},{1... | collective-permute-start | bytes 196616 | tf_op jit(solution)/shard_map/ppermute | solution.py:494
  89.8 8.9 %collective-permute-start.14 = (bf16[128,256]{1,0:T(8,128)(2,1)S(1)}, bf16[128,256]{1,0:T(8,128)(2,1)S(1)}, u32[]{:S(2)}, u32[]{:S(2)}) collective-permute-start(bf16[128,256]{1,0:T(8,128)(2,1)S(1)} %constant_dynamic-update-slice_fusion.refs_8_), channel_id=1, source_target_pairs={{0,32},{16,48},{32,64},{48,80},{64,96},{80,112},{96,0},{112,16},{1... | collective-permute-start | bytes 196616 | tf_op jit(solution)/shard_map/ppermute | solution.py:494
  98.6 0.6 copy-start.4
  98.6 0.6 copy-start.5
  98.7 0.6 copy-start.6

commit v5 on v4

--- a/solution.py
+++ b/solution.py
@@ -125,9 +125,9 @@
 
 def moments_kernel(
     sizes, slots_ref, counts_ref, pos_ref, dens_ref, code_ref, checks_ref, m2m_ref,
-    target_ref, source_ref, tile_ref, first_ref, last_ref, *rest,
+    target_ref, source_ref, tile_ref, *rest,
 ):
-    send_refs, part_refs = rest[:8], (rest[8], rest[0], rest[1])
+    send_refs, part_refs = rest[:8], ((rest[8], 0), (rest[0], 0), (rest[1], HW))
     weights, moments_low, moments_high, scratch, spare = rest[9:]
     step = pl.program_id(0)
     leaves = pos_ref.shape[1]
@@ -158,7 +158,8 @@
         return dot(checks, jnp.concatenate([target_ref[leaf + u] for u in range(4)], axis=1))
 
     def finish(first, part, kernel, sums):
-        tile_ref[:, pl.ds(pl.multiple_of((first + part * 4) * 128, 512), 512)] = kernel
+        pair = first // 2 + part * 2
+        tile_ref[pair], tile_ref[pair + 1] = kernel[:, :256], kernel[:, 256:]
         block = part // 4
         value = weights[pl.ds(pl.multiple_of(first + block * 16, 16), 16), :]
         apart = [jnp.where(row == part % 4 * 4 + u, value, 0.0) for u in range(4)]
@@ -186,11 +187,11 @@
 
     @pl.when(step == 0)
     def _():
-        first_ref[...] = source_ref[0:HW]
+        send_refs[3][0:HW] = source_ref[0:HW]
 
     @pl.when(step == pl.num_programs(0) - 1)
     def _():
-        last_ref[...] = source_ref[leaves - HW :]
+        send_refs[1][0:HW] = source_ref[leaves - HW :]
         group, place = lax.axis_index("oct"), lax.axis_index("leaf")
         oct_size, leaf_size = sizes
         for partner in range(8):
@@ -208,19 +209,21 @@
                 return carry
 
             lax.fori_loop(0, 32, pick, 0, unroll=8)
-            send_refs[partner][-32:, :] = jnp.concatenate(
-                [spare[0:32, :], scratch[0:32, :]], axis=1
-            ).astype(BF)
+            last = send_refs[partner].shape[0]
+            send_refs[partner][last - 2] = spare[0:32, :].astype(BF)
+            send_refs[partner][last - 1] = scratch[0:32, :].astype(BF)
         low = jnp.concatenate([moments_low[...], moments_high[...]], axis=1).astype(BF)
-        parents = part_refs[0].shape[0]
-        acc = jnp.zeros(part_refs[0].shape, F32)
+        parents = 64
+        acc = jnp.zeros((parents, 2 * 128), F32)
         for c in range(8):
             row = lax.broadcasted_iota(jnp.int32, (parents, total), 0) + c * parents
             chosen = jnp.where(row == code_ref[...], 1.0, 0.0).astype(BF)
             high, rest = split(dot(chosen, low))
             acc += dot(high.astype(BF), m2m_ref[c]) + dot(rest.astype(BF), m2m_ref[c])
-        for part_ref in part_refs:
-            part_ref[0:parents, :] = acc.astype(BF)
+        for part_ref, at in part_refs:
+            for k in range(4):
+                piece = acc[k % 2 * 32 : k % 2 * 32 + 32, k // 2 * 128 : k // 2 * 128 + 128]
+                part_ref[at + k] = piece.astype(BF)
 
 
 def load_window(begin, target_ref, parts, target, window, sems):
@@ -229,7 +232,9 @@
     at = 0
     for k, part in enumerate(parts):
         size = part.shape[0]
-        if size != HW:
+        if size < 64:
+            size, part = HW, part.at[0:HW]
+        if part.shape[0] >= 64:
             low = max(begin - HW, 0)
             size = min(begin + leaves + HW, size) - low
             part = part.at[low : low + size]
@@ -285,11 +290,13 @@
     begin, offset_ref, dir_ref, far_ref, coarse_from_ref, coarse_to_ref,
     scale_ref, add_ref, l2l_ref, target_ref, source_ref, after_ref, m2l_ref, *refs,
 ):
-    recv_refs, parent_refs, (near_ref, out_ref) = refs[:8], refs[8:12], refs[12:14]
-    z_low, z_high, groups_low, groups_high, parents_low, parents_high = refs[14:20]
-    acc, rows_low, rows_high, recv_ref, target, window, table, sems, table_sems = refs[20:]
+    recv_refs, parent_refs = refs[:8], refs[8:12]
+    counts_ref, tile_ref, dens_ref, *near_refs, out_ref = refs[12:20]
+    z_low, z_high, groups_low, groups_high, parents_low, parents_high = refs[20:26]
+    acc, rows_low, rows_high, recv_ref, target, window, near_ref, table, *every_sem = refs[26:]
+    sems, table_sems, tile_sems = every_sem
     pieces = table_sems.shape[0]
-    kinds = table.shape[0]
+    kinds = m2l_ref.shape[0]
     span = kinds // pieces
     received = recv_ref.shape[0]
     cells = acc.shape[0]
@@ -313,14 +320,17 @@
     oct_size = parents_low.shape[0] // cells
     before = 0
     for part in parent_refs:
-        for k in range(part.shape[0] // cells):
+        for k in range(2):
             owner = lax.rem(lax.axis_index("oct") + oct_size - before, oct_size)
             at = pl.ds(pl.multiple_of(owner * cells, cells), cells)
-            piece = part[k * cells : (k + 1) * cells, :].astype(F32)
-            parents_low[at, :], parents_high[at, :] = piece[:, :128], piece[:, 128:]
+            piece = part[k * 4 : k * 4 + 4].astype(F32)
+            parents_low[at, :] = piece[0:2].reshape(cells, 128)
+            parents_high[at, :] = piece[2:4].reshape(cells, 128)
             before += 1
     for k, part in enumerate(recv_refs):
-        recv_ref[k * 32 : (k + 1) * 32, :] = part[-32:, :]
+        last = part.shape[0]
+        recv_ref[k * 32 : (k + 1) * 32, :128] = part[last - 2]
+        recv_ref[k * 32 : (k + 1) * 32, 128:] = part[last - 1]
 
     def gather(q, carry):
         for j in range(coarse):
@@ -331,6 +341,17 @@
         return carry
 
     lax.fori_loop(0, cells, gather, 0)
+    tile_blocks, width = tile_ref.shape[0] // 32, 32
+    slots = [kinds + width * k for k in range(tile_blocks - 3)] + [0, width, kinds]
+    tiles = [
+        pltpu.make_async_copy(
+            tile_ref.at[k * width : (k + 1) * width], table.at[slots[k] : slots[k] + width],
+            tile_sems.at[k],
+        )
+        for k in range(tile_blocks)
+    ]
+    for k in range(tile_blocks - 3):
+        tiles[k].start()
     for k in range(pieces):
         loads[k].wait()
 
@@ -346,6 +367,8 @@
             return carry
 
         lax.fori_loop(0, span, spread_out, 0, unroll=True)
+    for k in range(tile_blocks - 3, tile_blocks - 1):
+        tiles[k].start()
     local = acc[...].astype(BF)
     for c in range(8):
         out = dot(local, l2l_ref[c])
@@ -378,32 +401,30 @@
         return carry
 
     lax.fori_loop(0, target.shape[0] // 32, body, 0)
-    out_ref[:, :128] = rows_low[...].astype(BF)
-    out_ref[:, 128:] = rows_high[...].astype(BF)
-
-
-def far_kernel(counts_ref, tile_ref, exp_ref, dens_ref, *refs):
-    near_refs, out_ref = refs[:-1], refs[-1]
-    step = pl.program_id(0)
-    leaves = out_ref.shape[0]
-    unroll = 16
-    lane = lax.broadcasted_iota(jnp.int32, (unroll, 128), 1)
-    row = lax.broadcasted_iota(jnp.int32, (unroll, 128), 0)
-    for group in range(leaves // unroll):
-        at = pl.ds(group * unroll, unroll)
-        out = dot(exp_ref[at, :], tile_ref[:, group * unroll * 128 : (group + 1) * unroll * 128])
-        far = jnp.zeros((unroll, 128), F32)
-        for u in range(unroll):
-            far = jnp.where(row == u, out[:, u * 128 : (u + 1) * 128], far)
-        near, begin = None, 0
-        for ref in near_refs:
-            at_near = jnp.clip(step * leaves + group * unroll - begin, 0, ref.shape[0] - unroll)
-            part = ref[pl.ds(pl.multiple_of(at_near, unroll), unroll), :]
-            near = part if near is None else jnp.where(step * leaves >= begin, part, near)
-            begin += ref.shape[0]
-        value = 0.5 * dens_ref[at, :] + near + far * (1.0 / math.sqrt(256))
-        counts = spread(counts_ref, step * leaves + group * unroll, unroll)
-        out_ref[at, :] = jnp.where(lane < counts, value, 0.0)
+    row = lax.broadcasted_iota(jnp.int32, (16, 128), 0)
+    lane = lax.broadcasted_iota(jnp.int32, (16, 128), 1)
+    for k in range(tile_blocks):
+        tiles[k].wait()
+        near_part = near_refs[k] if k < len(near_refs) else near_ref
+        near_first = 0 if k < len(near_refs) else k * 2 * width - begin
+
+        def far(group, carry):
+            first = k * 2 * width + group * 16
+            at = pl.ds(pl.multiple_of(first, 16), 16)
+            local = jnp.concatenate([rows_low[at, :], rows_high[at, :]], axis=1).astype(BF)
+            value = jnp.zeros((16, 128), F32)
+            for u in range(8):
+                out = dot(local, table[slots[k] + group * 8 + u])
+                value = jnp.where(row == 2 * u, out[:, :128], value)
+                value = jnp.where(row == 2 * u + 1, out[:, 128:], value)
+            near = near_part[pl.ds(pl.multiple_of(near_first + group * 16, 16), 16), :]
+            total = 0.5 * dens_ref[at, :] + near + value * (1.0 / math.sqrt(256))
+            out_ref[at, :] = jnp.where(lane < spread(counts_ref, first, 16), total, 0.0)
+            return carry
+
+        lax.fori_loop(0, width // 8, far, 0)
+        if k == 0:
+            tiles[tile_blocks - 1].start()
 
 
 def params(mib=56):
@@ -430,7 +451,7 @@
     steps = 8
     block = leaves // steps
     chunk = leaves // 8
-    target, source, tile, first, last, *send = pl.pallas_call(
+    target, source, tile, *send = pl.pallas_call(
         functools.partial(moments_kernel, (oct_size, leaf_size)),
         grid=(steps,),
         in_specs=[
@@ -442,18 +463,15 @@
         out_specs=[
             pl.BlockSpec((block, ROWS, panels), lambda i: (i, 0, 0)),
             pl.BlockSpec((block, ROWS, panels), lambda i: (i, 0, 0)),
-            pl.BlockSpec((width, block * panels), lambda i: (0, i)),
+            pl.BlockSpec((block // 2, width, 2 * panels), lambda i: (i, 0, 0)),
         ]
-        + [VMEM] * 11,
+        + [VMEM] * 9,
         out_shape=[
             jax.ShapeDtypeStruct((leaves, ROWS, panels), BF),
             jax.ShapeDtypeStruct((leaves, ROWS, panels), BF),
-            jax.ShapeDtypeStruct((width, leaves * panels), BF),
+            jax.ShapeDtypeStruct((leaves // 2, width, 2 * panels), BF),
         ]
-        + [jax.ShapeDtypeStruct((HW, ROWS, panels), BF)] * 2
-        + [jax.ShapeDtypeStruct((cells + cap, width), BF)] * 2
-        + [jax.ShapeDtypeStruct((cap, width), BF)] * 6
-        + [jax.ShapeDtypeStruct((cells, width), BF)],
+        + [jax.ShapeDtypeStruct((n, 32, 128), BF) for n in (6, HW + 6, 2, HW + 2, 2, 2, 2, 2, 4)],
         scratch_shapes=[
             pltpu.VMEM((block, 128), F32),
             pltpu.VMEM((leaves, 128), F32),
@@ -493,10 +511,6 @@
         size = lax.axis_size(axis)
         return lax.ppermute(value, axis, [(i, (i + by) % size) for i in range(size)])
 
-    def moved(value, by):
-        pairs = [(i, i + by) for i in range(leaf_size) if 0 <= i + by < leaf_size]
-        return lax.ppermute(value, "leaf", pairs)
-
     def added(pieces):
         total = pieces[0].astype(F32)
         for piece in pieces[1:]:
@@ -504,39 +518,35 @@
         return total.astype(BF)
 
     partial = send[8]
+    by_one = shifted(send[1], "leaf", 1)
+    back_one = shifted(send[3], "leaf", -1)
     by_two = shifted(send[0], "leaf", 2)
-    by_one = shifted(send[1], "leaf", 1)
+    back_two = shifted(send[4], "leaf", -2)
     by_three = shifted(partial, "leaf", 3)
-    before, after = moved(last, 1), moved(first, -1)
     near = [None] * 4
     near[1] = near_part(chunk)
-    near[1], by_one, by_two, by_three, before, after = lax.optimization_barrier(
-        (near[1], by_one, by_two, by_three, before, after)
+    near[1], by_one, by_two, by_three, back_one, back_two = lax.optimization_barrier(
+        (near[1], by_one, by_two, by_three, back_one, back_two)
     )
-    four = added([partial, by_one[:cells], by_two[:cells], by_three])
+    before, after = by_one, back_one
+    four = added([partial, by_one[HW : HW + 4], by_two[:4], by_three])
     strides = [shifted(four, "leaf", by) for by in (4, 8, 12)]
-    back_one, back_two = moved(send[3], -1), moved(send[4], -2)
+    upper = shifted(send[5], "oct", -1)
     four, source, target = lax.optimization_barrier((four, source, target))
     near[0] = near_part(0)
-    near[0], four, back_one, back_two, *strides = lax.optimization_barrier(
-        (near[0], four, back_one, back_two, *strides)
-    )
+    near[0], four, upper, *strides = lax.optimization_barrier((near[0], four, upper, *strides))
     total = added([four, *strides])
-    lower = shifted(total, "oct", 1)
-    across = [
-        shifted(send[5], "oct", -1), shifted(send[6], "oct", 1),
-        shifted(send[7], "oct", oct_size // 2),
-    ]
+    lower = shifted(jnp.concatenate([total, send[6]], axis=0), "oct", 1)
     total, source, target = lax.optimization_barrier((total, source, target))
     near[2] = near_part(2 * chunk)
-    near[2], total, lower, *across = lax.optimization_barrier((near[2], total, lower, *across))
-    pair = jnp.concatenate([total, lower], axis=0)
+    near[2], total, lower = lax.optimization_barrier((near[2], total, lower))
+    pair = jnp.concatenate([total, lower[:4], send[7]], axis=0)
     pairs = [shifted(pair, "oct", by) for by in (2, 4, 6)]
     pair, source, target = lax.optimization_barrier((pair, source, target))
     near[3] = near_part(3 * chunk)
     near[3], pair, *pairs = lax.optimization_barrier((near[3], pair, *pairs))
     every_parent = [pair, *pairs]
-    received = [by_two, by_one, send[2], back_one, back_two, *across]
+    received = [by_two, by_one, send[2], back_one, back_two, upper, lower, pairs[1]]
 
     owner, slot = far_source // cap, far_source % cap
     owner_group, owner_place = owner // leaf_size, owner % leaf_size
@@ -554,14 +564,12 @@
     far_rows = jnp.concatenate([far_rows.T.reshape(-1), own_row])
     rest = leaves - 4 * chunk
     any_space = pl.BlockSpec(memory_space=pl.ANY)
-    last_near, expansions = pl.pallas_call(
+    return pl.pallas_call(
         functools.partial(translate_kernel, 4 * chunk),
-        in_specs=[SMEM] * 5 + [VMEM] * 3 + [any_space] * 4 + [VMEM] * 12,
-        out_specs=[VMEM, VMEM],
-        out_shape=[
-            jax.ShapeDtypeStruct((rest, panels), F32),
-            jax.ShapeDtypeStruct((leaves, width), BF),
-        ],
+        in_specs=[SMEM] * 5 + [VMEM] * 3 + [any_space] * 4 + [VMEM] * 12
+        + [SMEM, any_space] + [VMEM] * 5,
+        out_specs=VMEM,
+        out_shape=jax.ShapeDtypeStruct((leaves, panels), F32),
         scratch_shapes=[
             pltpu.VMEM((kinds * 8 * cap + 8 * cells, 128), F32),
             pltpu.VMEM((kinds * 8 * cap + 8 * cells, 128), F32),
@@ -575,33 +583,18 @@
             pltpu.VMEM((8 * cap, width), BF),
             pltpu.VMEM((rest, ROWS, panels), BF),
             pltpu.VMEM((rest + 2 * HW, ROWS, panels), BF),
-            pltpu.VMEM(m2l.shape, BF),
+            pltpu.VMEM((rest, panels), F32),
+            pltpu.VMEM((kinds + 5 * 32, width, width), BF),
             pltpu.SemaphoreType.DMA((3,)),
             pltpu.SemaphoreType.DMA((8,)),
+            pltpu.SemaphoreType.DMA((8,)),
         ],
-        compiler_params=params(),
+        compiler_params=params(62),
         name="translate",
     )(
         offsets, ways, far_rows, coarse_source.T, coarse_type.T, scale, add, l2l,
-        target, source, after, m2l, *received, *every_parent,
+        target, source, after, m2l, *received, *every_parent, counts, tile, density, *near,
     )
-    near.append(last_near)
-
-    return pl.pallas_call(
-        far_kernel,
-        grid=(steps,),
-        in_specs=[
-            SMEM,
-            pl.BlockSpec((width, block * panels), lambda i: (0, i)),
-            pl.BlockSpec((block, width), lambda i: (i, 0)),
-            pl.BlockSpec((block, panels), lambda i: (i, 0)),
-        ]
-        + [VMEM] * len(near),
-        out_specs=pl.BlockSpec((block, panels), lambda i: (i, 0)),
-        out_shape=jax.ShapeDtypeStruct((leaves, panels), F32),
-        compiler_params=params(),
-        name="far",
-    )(counts, tile, expansions, density, *near)
 
 
 def solution(mesh):

time: 163 us -> 146 us (0.90)
  starting transfers between devices: 33.5 us -> 22.9 us
  Pallas kernels: 125 us -> 119 us
    pallas_call x1 -> x0, Pallas kernels: 14.4 us -> none  [local(): pl.pallas_call(far_kernel, grid=(steps,), in_specs=[SMEM, pl.BlockSpec((w...]
    pallas_call x1, Pallas kernels: 48.2 us -> 56.6 us  [local(): pl.pallas_call(functools.partial(translate_kernel, 4 * chunk), in_specs=[...]
    ppermute x4 -> x0, starting transfers between devices: 7.38 us -> none  [moved(): return lax.ppermute(value, 'leaf', pairs)]
    ppermute x13, starting transfers between devices: 26.1 us -> 22.9 us  [shifted(): lax.ppermute(value, axis, [(i, (i + by) % size) for i in range(size)])]
  transfers between devices with their start and end apart: 17 -> 13, of which waited for: 0 -> 1; matrix products, arithmetic and copies ran while one was open for 1% -> 1% of each run, Pallas kernels for 20% -> 22%
where the time goes in v5:
time: 146 us
  Pallas kernels  119 us (82%)
  starting transfers between devices  22.9 us (16%)
  other arithmetic  2.09 us (1%)
    pallas_call x1, Pallas kernels, local(): pl.pallas_call(functools.partial(translate_kernel, 4 * chunk), in_specs=[...  56.6 us
    pallas_call x4, Pallas kernels, near_part(): pl.pallas_call(functools.partial(near_kernel, begin), in_specs=spaces + [...  32.5 us
    pallas_call x1, Pallas kernels, local(): pl.pallas_call(functools.partial(moments_kernel, (oct_size, leaf_size)),...  29.9 us
    ppermute x13, starting transfers between devices, shifted(): lax.ppermute(value, axis, [(i, (i + by) % size) for i in range(size)])  22.9 us
  transfers between devices with their start and end apart: 13, of which 1 were waited for; matrix products, arithmetic and copies ran while one was open for 1% of the time, Pallas kernels for 22%

profile of v5, /device:TPU:1, one launch (start us, length us, event | category | flops | bytes accessed | tf_op | source)
XLA Modules:
  0.0 145.6 jit_solution(11571203671316431878)
XLA Ops:
  0.0 1.2 multiply_add_fusion
  1.2 29.9 %moments.1 = (bf16[512,32,128]{2,1,0:T(8,128)(2,1)}, bf16[512,32,128]{2,1,0:T(8,128)(2,1)}, bf16[256,256,256]{2,1,0:T(8,128)(2,1)}, bf16[6,32,128]{2,1,0:T(8,128...) custom-call(s32[32,128]{1,0:T(8,128)} %bitcast.12, ...), custom_call_target="tpu_custom_call" | custom-call | tf_op jit(solution)/shard_map/moments/pallas_call | solution.py:454
  31.2 7.3 %collective-permute-start.4 = (bf16[2,32,128]{2,1,0:T(8,128)(2,1)}, bf16[2,32,128]{2,1,0:T(8,128)(2,1)S(1)}, u32[]{:S(2)}, u32[]{:S(2)}) collective-permute-start(bf16[2,32,128]{2,1,0:T(8,128)(2,1)} %get-tuple-element.52), channel_id=1, source_target_pairs={{0,14},{1,15},{2,0},{3,1},{4,2},{5,3},{6,4},{7,5},{8,6},{9,7},{10,... | collective-permute-start | bytes 49160 | tf_op jit(solution)/shard_map/ppermute | solution.py:512
  38.5 0.0 collective-permute-start.2
  38.5 0.0 collective-permute-start.1
  38.5 4.9 %collective-permute-start.3 = (bf16[34,32,128]{2,1,0:T(8,128)(2,1)}, bf16[34,32,128]{2,1,0:T(8,128)(2,1)S(1)}, u32[]{:S(2)}, u32[]{:S(2)}) collective-permute-start(bf16[34,32,128]{2,1,0:T(8,128)(2,1)} %get-tuple-element.51), channel_id=1, source_target_pairs={{0,15},{1,0},{2,1},{3,2},{4,3},{5,4},{6,5},{7,6},{8,7},{9,8},{10,9... | collective-permute-start | bytes 835592 | tf_op jit(solution)/shard_map/ppermute | solution.py:512
  43.4 0.0 collective-permute-start
  43.4 0.0 copy-start.10
  43.4 8.1 %near.4.refs_16_ = f32[64,128]{1,0:T(8,128)} custom-call(s32[4,512]{1,0:T(4,128)} %bitcast.13, s32[4,512]{1,0:T(4,128)} %bitcast.18, bf16[27,32,128]{2,1,0:T(8,128)(2,1)} %constant.95.clone.scale_ref, bf16[27,32,128]{2,1,0:T(8,128)(2,1)} %constant.96.clone.add_ref, bf16[512,32,128]{2,1,0:T(8,128)(2,1)} %get-tuple-element.71.target_ref, ...), custom_call_target="tpu_custom_call" | custom-call | flops 10000000000 | bytes 1000000 | tf_op jit(solution)/shard_map/near/pallas_call | solution.py:493
  51.6 0.0 copy-done.8
  51.6 0.0 copy-done.9
  51.6 0.1 fusion.6
  51.8 0.6 pad_add_fusion.far_ref
  52.4 0.0 collective-permute-done.4.refs_4_
  52.4 0.0 copy-done.15
  52.4 1.5 %collective-permute-start.5 = (bf16[2,32,128]{2,1,0:T(8,128)(2,1)S(1)}, bf16[2,32,128]{2,1,0:T(8,128)(2,1)S(1)}, u32[]{:S(2)}, u32[]{:S(2)}) collective-permute-start(bf16[2,32,128]{2,1,0:T(8,128)(2,1)S(1)} %copy-done.15), channel_id=1, source_target_pairs={{0,112},{16,0},{32,16},{48,32},{64,48},{80,64},{96,80},{112,96},{1... | collective-permute-start | bytes 49160 | tf_op jit(solution)/shard_map/ppermute | solution.py:512
  53.9 0.0 collective-permute-done.2
  53.9 0.0 collective-permute-done.1.refs_0_
  53.9 0.0 collective-permute-done.3.after_ref.refs_3_
  53.9 0.0 copy-start
  53.9 0.3 collective-permute-done.refs_0_.refs_1_
  54.3 0.0 copy-done.10
  54.3 0.0 copy-start.14
  54.3 2.3 %collective-permute-start.8 = (bf16[4,32,128]{2,1,0:T(8,128)(2,1)S(1)}, bf16[4,32,128]{2,1,0:T(8,128)(2,1)S(1)}, u32[]{:S(2)}, u32[]{:S(2)}) collective-permute-start(bf16[4,32,128]{2,1,0:T(8,128)(2,1)S(1)} %add_convert_fusion.1), channel_id=1, source_target_pairs={{0,12},{1,13},{2,14},{3,15},{4,0},{5,1},{6,2},{7,3},{8,4},{9,5},{1... | collective-permute-start | bytes 98312 | tf_op jit(solution)/shard_map/ppermute | solution.py:512
  56.6 0.0 collective-permute-start.7
  56.6 0.7 collective-permute-start.6
  57.3 0.0 copy-done.1
  57.3 8.1 %near.5.refs_15_ = f32[64,128]{1,0:T(8,128)} custom-call(s32[4,512]{1,0:T(4,128)} %bitcast.14, s32[4,512]{1,0:T(4,128)} %bitcast.19, bf16[27,32,128]{2,1,0:T(8,128)(2,1)} %constant.95.clone.scale_ref, bf16[27,32,128]{2,1,0:T(8,128)(2,1)} %constant.96.clone.add_ref, bf16[512,32,128]{2,1,0:T(8,128)(2,1)} %get-tuple-element.71.target_ref, ...), custom_call_target="tpu_custom_call" | custom-call | flops 10000000000 | bytes 1000000 | tf_op jit(solution)/shard_map/near/pallas_call | solution.py:493
  65.4 0.0 copy-done
  65.4 0.0 collective-permute-done.5.refs_5_
  65.4 0.0 collective-permute-done.8
  65.4 0.0 collective-permute-done.7
  65.4 0.0 collective-permute-done.6
  65.5 2.9 %collective-permute-start.9 = (bf16[6,32,128]{2,1,0:T(8,128)(2,1)S(1)}, bf16[6,32,128]{2,1,0:T(8,128)(2,1)S(1)}, u32[]{:S(2)}, u32[]{:S(2)}) collective-permute-start(bf16[6,32,128]{2,1,0:T(8,128)(2,1)S(1)} %pad_maximum_fusion.1), channel_id=1, source_target_pairs={{0,16},{16,32},{32,48},{48,64},{64,80},{80,96},{96,112},{112,0},{1... | collective-permute-start | bytes 147464 | tf_op jit(solution)/shard_map/ppermute | solution.py:512
  68.4 8.1 %near.6.refs_17_ = f32[64,128]{1,0:T(8,128)} custom-call(s32[4,512]{1,0:T(4,128)} %bitcast.15, s32[4,512]{1,0:T(4,128)} %bitcast.20, bf16[27,32,128]{2,1,0:T(8,128)(2,1)} %constant.95.clone.scale_ref, bf16[27,32,128]{2,1,0:T(8,128)(2,1)} %constant.96.clone.add_ref, bf16[512,32,128]{2,1,0:T(8,128)(2,1)} %get-tuple-element.71.target_ref, ...), custom_call_target="tpu_custom_call" | custom-call | flops 10000000000 | bytes 1000000 | tf_op jit(solution)/shard_map/near/pallas_call | solution.py:493
  76.6 0.0 collective-permute-done.9.refs_6_
  76.6 1.5 %collective-permute-start.12 = (bf16[10,32,128]{2,1,0:T(8,128)(2,1)S(1)}, bf16[10,32,128]{2,1,0:T(8,128)(2,1)S(1)}, u32[]{:S(2)}, u32[]{:S(2)}) collective-permute-start(bf16[10,32,128]{2,1,0:T(8,128)(2,1)S(1)} %pad_maximum_fusion.refs_8_), channel_id=1, source_target_pairs={{0,96},{16,112},{32,0},{48,16},{64,32},{80,48},{96,64},{112,80},{1... | collective-permute-start | bytes 245768 | tf_op jit(solution)/shard_map/ppermute | solution.py:512
  78.2 1.5 %collective-permute-start.11 = (bf16[10,32,128]{2,1,0:T(8,128)(2,1)S(1)}, bf16[10,32,128]{2,1,0:T(8,128)(2,1)S(1)}, u32[]{:S(2)}, u32[]{:S(2)}) collective-permute-start(bf16[10,32,128]{2,1,0:T(8,128)(2,1)S(1)} %pad_maximum_fusion.refs_8_), channel_id=1, source_target_pairs={{0,64},{16,80},{32,96},{48,112},{64,0},{80,16},{96,32},{112,48},{1... | collective-permute-start | bytes 245768 | tf_op jit(solution)/shard_map/ppermute | solution.py:512
  79.7 0.3 collective-permute-start.10
  80.0 8.1 %near.7.refs_18_ = f32[64,128]{1,0:T(8,128)} custom-call(s32[4,512]{1,0:T(4,128)} %bitcast.16, s32[4,512]{1,0:T(4,128)} %bitcast.21, bf16[27,32,128]{2,1,0:T(8,128)(2,1)} %constant.95.clone.scale_ref, bf16[27,32,128]{2,1,0:T(8,128)(2,1)} %constant.96.clone.add_ref, bf16[512,32,128]{2,1,0:T(8,128)(2,1)} %get-tuple-element.71.target_ref, ...), custom_call_target="tpu_custom_call" | custom-call | flops 10000000000 | bytes 1000000 | tf_op jit(solution)/shard_map/near/pallas_call | solution.py:493
  88.1 0.0 collective-permute-done.12.refs_11_
  88.1 0.0 copy-start.6
  88.1 0.0 collective-permute-done.11.refs_7_.refs_10_
  88.2 0.0 collective-permute-done.10.refs_9_
  88.2 0.6 copy-done.6
  88.8 0.0 copy-done.2
  88.8 0.0 copy-done.7
  88.8 56.6 %translate.1 = f32[512,128]{1,0:T(8,128)} custom-call(s32[4,512]{1,0:T(4,128)} %bitcast.17, s32[4,512]{1,0:T(4,128)} %bitcast.22, s32[14336]{0:T(1024)} %pad_add_fusion.far_ref, s32[16,64]{1,0:T(8,128)} %bitcast.23, s32[16,64]{1,0:T(8,128)} %bitcast.24, bf16[27,32,128]{2,1,0:T(8,128)(2,1)} %constant.95.clone.scale_ref, ...), custom_call_target="tpu_custom_call" | custom-call | tf_op jit(solution)/shard_map/translate/pallas_call | solution.py:567
  (25 shorter events, 0.1 us)
Async XLA Ops:
  31.2 21.2 %collective-permute-start.4 = (bf16[2,32,128]{2,1,0:T(8,128)(2,1)}, bf16[2,32,128]{2,1,0:T(8,128)(2,1)S(1)}, u32[]{:S(2)}, u32[]{:S(2)}) collective-permute-start(bf16[2,32,128]{2,1,0:T(8,128)(2,1)} %get-tuple-element.52), channel_id=1, source_target_pairs={{0,14},{1,15},{2,0},{3,1},{4,2},{5,3},{6,4},{7,5},{8,6},{9,7},{10,... | collective-permute-start | bytes 49160 | tf_op jit(solution)/shard_map/ppermute | solution.py:512
  38.5 15.4 %collective-permute-start.2 = (bf16[4,32,128]{2,1,0:T(8,128)(2,1)}, bf16[4,32,128]{2,1,0:T(8,128)(2,1)S(1)}, u32[]{:S(2)}, u32[]{:S(2)}) collective-permute-start(bf16[4,32,128]{2,1,0:T(8,128)(2,1)} %get-tuple-element.46), channel_id=1, source_target_pairs={{0,3},{1,4},{2,5},{3,6},{4,7},{5,8},{6,9},{7,10},{8,11},{9,12},{10... | collective-permute-start | bytes 98312 | tf_op jit(solution)/shard_map/ppermute | solution.py:512
  38.5 15.4 %collective-permute-start.1 = (bf16[6,32,128]{2,1,0:T(8,128)(2,1)}, bf16[6,32,128]{2,1,0:T(8,128)(2,1)S(1)}, u32[]{:S(2)}, u32[]{:S(2)}) collective-permute-start(bf16[6,32,128]{2,1,0:T(8,128)(2,1)} %get-tuple-element.50), channel_id=1, source_target_pairs={{0,2},{1,3},{2,4},{3,5},{4,6},{5,7},{6,8},{7,9},{8,10},{9,11},{10,... | collective-permute-start | bytes 147464 | tf_op jit(solution)/shard_map/ppermute | solution.py:512
  38.5 15.4 %collective-permute-start.3 = (bf16[34,32,128]{2,1,0:T(8,128)(2,1)}, bf16[34,32,128]{2,1,0:T(8,128)(2,1)S(1)}, u32[]{:S(2)}, u32[]{:S(2)}) collective-permute-start(bf16[34,32,128]{2,1,0:T(8,128)(2,1)} %get-tuple-element.51), channel_id=1, source_target_pairs={{0,15},{1,0},{2,1},{3,2},{4,3},{5,4},{6,5},{7,6},{8,7},{9,8},{10,9... | collective-permute-start | bytes 835592 | tf_op jit(solution)/shard_map/ppermute | solution.py:512
  43.4 10.9 %collective-permute-start = (bf16[38,32,128]{2,1,0:T(8,128)(2,1)}, bf16[38,32,128]{2,1,0:T(8,128)(2,1)S(1)}, u32[]{:S(2)}, u32[]{:S(2)}) collective-permute-start(bf16[38,32,128]{2,1,0:T(8,128)(2,1)} %get-tuple-element.49), channel_id=1, source_target_pairs={{0,1},{1,2},{2,3},{3,4},{4,5},{5,6},{6,7},{7,8},{8,9},{9,10},{10,1... | collective-permute-start | bytes 933896 | tf_op jit(solution)/shard_map/ppermute | solution.py:512
  43.4 8.2 %copy-start.8 = (s32[512,27]{0,1:T(8,128)S(1)}, s32[512,27]{0,1:T(8,128)}, u32[]{:S(2)}) copy-start(s32[512,27]{0,1:T(8,128)} %param.25) | copy-start | bytes 165892
  43.4 8.2 %copy-start.9 = (s32[512,27]{0,1:T(8,128)S(1)}, s32[512,27]{0,1:T(8,128)}, u32[]{:S(2)}) copy-start(s32[512,27]{0,1:T(8,128)} %param.24) | copy-start | bytes 165892
  43.4 9.0 %copy-start.15 = (bf16[2,32,128]{2,1,0:T(8,128)(2,1)S(1)}, bf16[2,32,128]{2,1,0:T(8,128)(2,1)}, u32[]{:S(2)}) copy-start(bf16[2,32,128]{2,1,0:T(8,128)(2,1)} %get-tuple-element.59) | copy-start | bytes 49156
  43.4 10.9 %copy-start.10 = (bf16[4,32,128]{2,1,0:T(8,128)(2,1)S(1)}, bf16[4,32,128]{2,1,0:T(8,128)(2,1)}, u32[]{:S(2)}) copy-start(bf16[4,32,128]{2,1,0:T(8,128)(2,1)} %get-tuple-element.46) | copy-start | bytes 98308
  52.4 24.2 %copy-start.11 = (bf16[2,32,128]{2,1,0:T(8,128)(2,1)}, bf16[2,32,128]{2,1,0:T(8,128)(2,1)S(1)}, u32[]{:S(2)}) copy-start(bf16[2,32,128]{2,1,0:T(8,128)(2,1)S(1)} %collective-permute-done.4.refs_4_) | copy-start | bytes 49156
  52.4 13.0 %collective-permute-start.5 = (bf16[2,32,128]{2,1,0:T(8,128)(2,1)S(1)}, bf16[2,32,128]{2,1,0:T(8,128)(2,1)S(1)}, u32[]{:S(2)}, u32[]{:S(2)}) collective-permute-start(bf16[2,32,128]{2,1,0:T(8,128)(2,1)S(1)} %copy-done.15), channel_id=1, source_target_pairs={{0,112},{16,0},{32,16},{48,32},{64,48},{80,64},{96,80},{112,96},{1... | collective-permute-start | bytes 49160 | tf_op jit(solution)/shard_map/ppermute | solution.py:512
  53.9 22.6 %copy-start.4 = (bf16[6,32,128]{2,1,0:T(8,128)(2,1)}, bf16[6,32,128]{2,1,0:T(8,128)(2,1)S(1)}, u32[]{:S(2)}) copy-start(bf16[6,32,128]{2,1,0:T(8,128)(2,1)S(1)} %collective-permute-done.1.refs_0_) | copy-start | bytes 147460
  53.9 11.4 %copy-start = (bf16[34,32,128]{2,1,0:T(8,128)(2,1)}, bf16[34,32,128]{2,1,0:T(8,128)(2,1)S(1)}, u32[]{:S(2)}) copy-start(bf16[34,32,128]{2,1,0:T(8,128)(2,1)S(1)} %collective-permute-done.3.after_ref.refs_3_) | copy-start | bytes 835588
  54.3 3.0 %copy-start.1 = (bf16[38,32,128]{2,1,0:T(8,128)(2,1)}, bf16[38,32,128]{2,1,0:T(8,128)(2,1)S(1)}, u32[]{:S(2)}) copy-start(bf16[38,32,128]{2,1,0:T(8,128)(2,1)S(1)} %collective-permute-done.refs_0_.refs_1_) | copy-start | bytes 933892
  54.3 11.2 %copy-start.14 = (bf16[2,32,128]{2,1,0:T(8,128)(2,1)S(1)}, bf16[2,32,128]{2,1,0:T(8,128)(2,1)}, u32[]{:S(2)}) copy-start(bf16[2,32,128]{2,1,0:T(8,128)(2,1)} %get-tuple-element.67) | copy-start | bytes 49156
  54.3 11.1 %collective-permute-start.8 = (bf16[4,32,128]{2,1,0:T(8,128)(2,1)S(1)}, bf16[4,32,128]{2,1,0:T(8,128)(2,1)S(1)}, u32[]{:S(2)}, u32[]{:S(2)}) collective-permute-start(bf16[4,32,128]{2,1,0:T(8,128)(2,1)S(1)} %add_convert_fusion.1), channel_id=1, source_target_pairs={{0,12},{1,13},{2,14},{3,15},{4,0},{5,1},{6,2},{7,3},{8,4},{9,5},{1... | collective-permute-start | bytes 98312 | tf_op jit(solution)/shard_map/ppermute | solution.py:512
  56.6 8.8 %collective-permute-start.7 = (bf16[4,32,128]{2,1,0:T(8,128)(2,1)S(1)}, bf16[4,32,128]{2,1,0:T(8,128)(2,1)S(1)}, u32[]{:S(2)}, u32[]{:S(2)}) collective-permute-start(bf16[4,32,128]{2,1,0:T(8,128)(2,1)S(1)} %add_convert_fusion.1), channel_id=1, source_target_pairs={{0,8},{1,9},{2,10},{3,11},{4,12},{5,13},{6,14},{7,15},{8,0},{9,1},... | collective-permute-start | bytes 98312 | tf_op jit(solution)/shard_map/ppermute | solution.py:512
  56.6 8.8 %collective-permute-start.6 = (bf16[4,32,128]{2,1,0:T(8,128)(2,1)S(1)}, bf16[4,32,128]{2,1,0:T(8,128)(2,1)S(1)}, u32[]{:S(2)}, u32[]{:S(2)}) collective-permute-start(bf16[4,32,128]{2,1,0:T(8,128)(2,1)S(1)} %add_convert_fusion.1), channel_id=1, source_target_pairs={{0,4},{1,5},{2,6},{3,7},{4,8},{5,9},{6,10},{7,11},{8,12},{9,13},{1... | collective-permute-start | bytes 98312 | tf_op jit(solution)/shard_map/ppermute | solution.py:512
  65.4 11.2 %copy-start.12 = (bf16[2,32,128]{2,1,0:T(8,128)(2,1)}, bf16[2,32,128]{2,1,0:T(8,128)(2,1)S(1)}, u32[]{:S(2)}) copy-start(bf16[2,32,128]{2,1,0:T(8,128)(2,1)S(1)} %collective-permute-done.5.refs_5_) | copy-start | bytes 49156
  65.5 11.1 %copy-start.13 = (bf16[2,32,128]{2,1,0:T(8,128)(2,1)S(1)}, bf16[2,32,128]{2,1,0:T(8,128)(2,1)}, u32[]{:S(2)}) copy-start(bf16[2,32,128]{2,1,0:T(8,128)(2,1)} %get-tuple-element.70) | copy-start | bytes 49156
  65.5 11.1 %collective-permute-start.9 = (bf16[6,32,128]{2,1,0:T(8,128)(2,1)S(1)}, bf16[6,32,128]{2,1,0:T(8,128)(2,1)S(1)}, u32[]{:S(2)}, u32[]{:S(2)}) collective-permute-start(bf16[6,32,128]{2,1,0:T(8,128)(2,1)S(1)} %pad_maximum_fusion.1), channel_id=1, source_target_pairs={{0,16},{16,32},{32,48},{48,64},{64,80},{80,96},{96,112},{112,0},{1... | collective-permute-start | bytes 147464 | tf_op jit(solution)/shard_map/ppermute | solution.py:512
  76.6 11.5 %copy-start.5 = (bf16[6,32,128]{2,1,0:T(8,128)(2,1)}, bf16[6,32,128]{2,1,0:T(8,128)(2,1)S(1)}, u32[]{:S(2)}) copy-start(bf16[6,32,128]{2,1,0:T(8,128)(2,1)S(1)} %collective-permute-done.9.refs_6_) | copy-start | bytes 147460
  76.6 11.5 %copy-start.3 = (bf16[10,32,128]{2,1,0:T(8,128)(2,1)}, bf16[10,32,128]{2,1,0:T(8,128)(2,1)S(1)}, u32[]{:S(2)}) copy-start(bf16[10,32,128]{2,1,0:T(8,128)(2,1)S(1)} %pad_maximum_fusion.refs_8_) | copy-start | bytes 245764
  76.6 11.5 %collective-permute-start.12 = (bf16[10,32,128]{2,1,0:T(8,128)(2,1)S(1)}, bf16[10,32,128]{2,1,0:T(8,128)(2,1)S(1)}, u32[]{:S(2)}, u32[]{:S(2)}) collective-permute-start(bf16[10,32,128]{2,1,0:T(8,128)(2,1)S(1)} %pad_maximum_fusion.refs_8_), channel_id=1, source_target_pairs={{0,96},{16,112},{32,0},{48,16},{64,32},{80,48},{96,64},{112,80},{1... | collective-permute-start | bytes 245768 | tf_op jit(solution)/shard_map/ppermute | solution.py:512
  78.2 10.0 %collective-permute-start.11 = (bf16[10,32,128]{2,1,0:T(8,128)(2,1)S(1)}, bf16[10,32,128]{2,1,0:T(8,128)(2,1)S(1)}, u32[]{:S(2)}, u32[]{:S(2)}) collective-permute-start(bf16[10,32,128]{2,1,0:T(8,128)(2,1)S(1)} %pad_maximum_fusion.refs_8_), channel_id=1, source_target_pairs={{0,64},{16,80},{32,96},{48,112},{64,0},{80,16},{96,32},{112,48},{1... | collective-permute-start | bytes 245768 | tf_op jit(solution)/shard_map/ppermute | solution.py:512
  79.7 8.5 %collective-permute-start.10 = (bf16[10,32,128]{2,1,0:T(8,128)(2,1)S(1)}, bf16[10,32,128]{2,1,0:T(8,128)(2,1)S(1)}, u32[]{:S(2)}, u32[]{:S(2)}) collective-permute-start(bf16[10,32,128]{2,1,0:T(8,128)(2,1)S(1)} %pad_maximum_fusion.refs_8_), channel_id=1, source_target_pairs={{0,32},{16,48},{32,64},{48,80},{64,96},{80,112},{96,0},{112,16},{1... | collective-permute-start | bytes 245768 | tf_op jit(solution)/shard_map/ppermute | solution.py:512
  88.1 0.6 copy-start.6
  88.1 0.6 copy-start.2
  88.2 0.6 copy-start.7
